TPU v7x, 32 devices: a whole 2x2x4 slice. The times are simulated.
32 devices in a mesh: depth: 4 (over y, x), trans: 8 (over z, core).
Axes of the slice: x: 2, y: 2, z: 4, core: 2. Of those that a mesh axis runs over, the one named last changes fastest.
Arguments:
- flight_fields: bfloat16 [4, 2, 2, 1024, 1024], P('depth', None, None, 'trans'), may hold values from -6 to 6
- top_fields: bfloat16 [2, 2, 1024, 1024], P(None, None, 'trans'), may hold values from -6 to 6
- slowness: float32 [4, 1024, 1024], P('depth', 'trans'), may hold values from 0.5 to 1.5
- ref_slowness: float32 [4], P('depth'), may hold values from 0.6 to 1
- flight_blocks: int32 [4], replicated, may hold values from 128 to 191
- top_block: int32 [1], replicated, may hold values from 0 to 255
Outputs:
- image: float32 [4, 1024, 1024], P('depth', 'trans')
- next_fields: bfloat16 [4, 2, 2, 1024, 1024], P('depth', None, None, 'trans')
All inputs are finite; a program needn't handle non-finite values.
Results may differ from a plain program's by a relative error of at most 0.02.
Values may be sent and summed in bfloat16 or wider, within the bound.
No kernel may reach another device: no remote copies, remote signals or barrier semaphores. Data moves between devices by JAX's collectives and lax.ppermute only.
A program may use at most 64 MiB of HBM per device.

v0:
```python
import functools
import math

import jax
import jax.numpy as jnp
import numpy as np
from jax import lax
from jax.experimental import pallas as pl
from jax.experimental.pallas import tpu as pltpu
from jax.sharding import Mesh, PartitionSpec as P

NFREQ = 256

omega_top = 4.0
step_length = 0.5

VMEM = pl.BlockSpec(memory_space=pltpu.VMEM)
SMEM = pl.BlockSpec(memory_space=pltpu.SMEM)
F32 = jnp.float32
BF16 = jnp.bfloat16


def partners(count):
    return sorted(range(count), key=lambda k: (-k.bit_length(), k))


def cas_tables(length):
    positions = np.arange(length // 2, dtype=np.int64)

    def table(modes):
        angles = (modes[:, None] * positions[None, :] % length) * (2.0 * math.pi / length)
        return ((np.cos(angles) + np.sin(angles)) / math.sqrt(length)).astype(jnp.bfloat16)

    even, odd = table(2 * positions), table(2 * positions + 1)
    return jnp.asarray(even), jnp.asarray(odd), jnp.asarray(odd.T.copy())


def dot(left, right):
    return jnp.dot(left, right, preferred_element_type=F32)


def signed_wave(index, length):
    signed = jnp.where(index < length // 2, index, index - length)
    return signed.astype(F32) * (2.0 * math.pi / length)


def cos_sin(angle):
    square = angle * angle
    cosine = jnp.full_like(square, 1.0 / math.factorial(16))
    for order in range(14, -1, -2):
        cosine = cosine * -square + 1.0 / math.factorial(order)
    sine = jnp.full_like(square, 1.0 / math.factorial(15))
    for order in range(13, 0, -2):
        sine = sine * -square + 1.0 / math.factorial(order)
    return cosine, sine * angle


def factors_kernel(odd, length_y, place_ref, scalar_ref, cos_ref, sin_ref):
    length_x, modes = cos_ref.shape
    half = length_x // 2
    angular, reference_s, sign = scalar_ref[0], scalar_ref[1], scalar_ref[2]
    step = 64
    lane = lax.broadcasted_iota(jnp.int32, (step, modes), 1)
    line = lax.broadcasted_iota(jnp.int32, (step, modes), 0)
    wave_y = signed_wave(2 * (place_ref[0] * modes + lane) + odd, length_y)
    constant = (angular * reference_s) ** 2 - wave_y * wave_y

    @pl.loop(0, length_x // step)
    def _(chunk):
        rows = pl.ds(pl.multiple_of(chunk * step, step), step)
        place = chunk * step + line
        kx = jnp.where(place < half, 2 * place, 2 * place - length_x + 1)
        wave_x = signed_wave(kx, length_x)
        quad = constant - wave_x * wave_x
        root = jnp.sqrt(jnp.abs(quad)) * step_length
        travels = quad > 0.0
        cosine, sine = cos_sin(jnp.where(travels, root, 0.0))
        damping = jnp.exp(jnp.where(travels, 0.0, -root))
        cos_ref[rows, :] = damping * cosine
        sin_ref[rows, :] = (sign * damping) * sine


def phase_kernel(place_ref, scalar_ref, mine_ref, other_ref, cos_ref, sin_ref):
    angular, reference_s, sign = scalar_ref[0], scalar_ref[1], scalar_ref[2]
    rows = mine_ref.shape[0]
    step = 8
    for index, slowness in enumerate((mine_ref, other_ref)):
        start = (place_ref[1] ^ index) * rows

        @pl.loop(0, rows // step)
        def _(chunk):
            there = pl.ds(pl.multiple_of(start + chunk * step, step), step)
            here = pl.ds(pl.multiple_of(chunk * step, step), step)
            cosine, sine = cos_sin(angular * (slowness[here, :] - reference_s) * step_length)
            cos_ref[there, :] = cosine
            sin_ref[there, :] = sign * sine


def rows_of(start, size):
    return pl.ds(pl.multiple_of(start, size), size)


def split_modes(here, whole, outs):
    rows, width = outs[0].shape
    block = width // 2
    for k, out in zip(partners(len(outs)), outs):
        columns = rows_of((here ^ k) * block, block)
        for part in range(2):
            out[:, part * block : (part + 1) * block] = whole[
                part * rows : (part + 1) * rows, columns
            ]


def join_modes(here, pieces, whole, lines=None):
    rows, width = pieces[0].shape
    block = width // 2
    size = rows if lines is None else lines.size
    for k, piece in zip(partners(len(pieces)), pieces):
        columns = rows_of((here ^ k) * block, block)
        for part in range(2):
            whole[part * size : (part + 1) * size, columns] = piece[
                slice(None) if lines is None else lines, part * block : (part + 1) * block
            ]


def to_modes_kernel(odd, place_ref, fields_ref, other_ref, table_ref, *refs):
    outs, (folded, modes) = refs[:-2], refs[-2:]
    rows = other_ref.shape[0] // 2
    half = table_ref.shape[0]
    core = place_ref[1]
    for part in range(2):
        mine = rows_of((2 * core + part) * rows, rows)
        for lines, source, index in ((mine, fields_ref, 0), (slice(part * rows, (part + 1) * rows), other_ref, 1)):
            low, high = source[lines, :half], source[lines, half:]
            there = rows_of(2 * part * rows + (core ^ index) * rows, rows)
            folded[there, :] = low - high if odd else low + high
    modes[...] = dot(folded[...], table_ref[...]).astype(BF16)
    split_modes(place_ref[0], modes, outs)


def along_x_kernel(count, place_ref, cos_ref, sin_ref, even_ref, odd_ref, turned_ref, *refs):
    pieces, outs = refs[:count], refs[count : 2 * count]
    held, shifted = refs[2 * count :]
    here = place_ref[0]
    rows, width = outs[0].shape
    block = width // 2
    for k, piece in zip(partners(count), pieces):
        held[rows_of((here ^ k) * rows, rows), :] = piece[...]
    half = even_ref.shape[0]
    low, high = held[:half, :], held[half:, :]
    for part, table, values in ((0, even_ref, low + high), (1, odd_ref, low - high)):
        lines = slice(part * half, (part + 1) * half)
        spectrum = dot(table[...], values)
        real, imag = spectrum[:, :block], spectrum[:, block:]
        cosine, sine = cos_ref[lines, :], sin_ref[lines, :]
        shifted[lines, :block] = (real * cosine - imag * sine).astype(BF16)
        shifted[lines, block:] = (real * sine + imag * cosine).astype(BF16)
    first = dot(even_ref[...], shifted[:half, :])
    second = dot(turned_ref[...], shifted[half:, :])
    held[:half, :] = (first + second).astype(BF16)
    held[half:, :] = (first - second).astype(BF16)
    for k, out in zip(partners(count), outs):
        out[...] = held[rows_of((here ^ k) * rows, rows), :]


def even_part_kernel(place_ref, table_ref, *refs):
    pieces, (out_ref, modes) = refs[:-2], refs[-2:]
    join_modes(place_ref[0], pieces, modes)
    out_ref[...] = dot(modes[...], table_ref[...])


def turned(real, imag, cosine, sine):
    return (real * cosine - imag * sine).astype(BF16), (real * sine + imag * cosine).astype(BF16)


def turn_around_kernel(
    count, place_ref, cos_ref, sin_ref, top_ref, top_other_ref, even_ref, odd_ref, part_ref, *refs
):
    pieces, outs = refs[:count], refs[count : 2 * count]
    folded_ref, keep_ref, give_ref, modes, space, sums = refs[2 * count :]
    here, core = place_ref[0], place_ref[1]
    rows = pieces[0].shape[0]
    own = rows // 2
    half = odd_ref.shape[0]
    join_modes(here, pieces, modes)
    step = 256
    for start in range(0, half, step):
        columns = slice(start, start + step)
        second = dot(modes[...], odd_ref[:, columns])
        first = part_ref[:, columns]
        for values, at in ((first + second, start), (first - second, start + half)):
            lanes = slice(at, at + step)
            real, imag = turned(values[:rows], values[rows:], cos_ref[:, lanes], sin_ref[:, lanes])
            space[:rows, lanes] = real
            space[rows:, lanes] = imag
    for index, out in enumerate((keep_ref, give_ref)):
        for part in range(2):
            out[part * own : (part + 1) * own, :] = space[
                rows_of(part * rows + (core ^ index) * own, own), :
            ]

    @pl.when(place_ref[2] == 1)
    def _():
        for part in range(2):
            space[rows_of(part * rows + core * own, own), :] = top_ref[
                rows_of((2 * core + part) * own, own), :
            ]
            space[rows_of(part * rows + (core ^ 1) * own, own), :] = top_other_ref[
                part * own : (part + 1) * own, :
            ]

    sums[...] = space[:, :half] + space[:, half:]
    folded_ref[...] = space[:, :half] - space[:, half:]
    modes[...] = dot(sums[...], even_ref[...]).astype(BF16)
    split_modes(here, modes, outs)


def odd_modes_kernel(place_ref, folded_ref, table_ref, *refs):
    outs, modes = refs[:-1], refs[-1]
    modes[...] = dot(folded_ref[...], table_ref[...]).astype(BF16)
    split_modes(place_ref[0], modes, outs)


def half_space_kernel(index, place_ref, cos_ref, sin_ref, odd_ref, part_ref, *refs):
    pieces, (out_ref, modes) = refs[:-2], refs[-2:]
    rows = pieces[0].shape[0]
    own = rows // 2
    half = odd_ref.shape[0]
    offset = (place_ref[1] ^ index) * own
    lines = rows_of(offset, own)
    join_modes(place_ref[0], pieces, modes, lines)
    step = 256
    for start in range(0, half, step):
        columns = slice(start, start + step)
        second = dot(modes[...], odd_ref[:, columns])
        for sign, at in ((1.0, start), (-1.0, start + half)):
            lanes = slice(at, at + step)
            real, imag = [
                part_ref[rows_of(part * rows + offset, own), columns]
                + sign * second[part * own : (part + 1) * own]
                for part in range(2)
            ]
            out_ref[:own, lanes], out_ref[own:, lanes] = turned(
                real, imag, cos_ref[lines, lanes], sin_ref[lines, lanes]
            )


def finish_kernel(place_ref, first_ref, first_other_ref, keep_ref, got_ref, fields_ref, image_ref):
    rows = keep_ref.shape[0]
    own = rows // 2
    core = place_ref[1]
    fields_ref[rows_of(core * rows, rows), :] = keep_ref[...]
    fields_ref[rows_of((core ^ 1) * rows, rows), :] = got_ref[...]
    step = 16
    for start in range(0, own, step):
        total = None
        for one, two in ((first_ref, first_other_ref), (keep_ref, got_ref)):
            for part in range(2):
                lines = slice(part * own + start, part * own + start + step)
                term = one[lines, :].astype(F32) * two[lines, :].astype(F32)
                total = term if total is None else total + term
        image_ref[start : start + step, :] = total


def call(kernel, operands, outs, scratch=(), flops=0, name=None, scalars=1):
    moved = sum(math.prod(a.shape) * a.dtype.itemsize for a in operands)
    moved += sum(math.prod(a.shape) * a.dtype.itemsize for a in outs)
    return pl.pallas_call(
        kernel,
        out_shape=tuple(outs),
        in_specs=[SMEM] * scalars + [VMEM] * (len(operands) - scalars),
        out_specs=tuple(VMEM for _ in outs),
        scratch_shapes=list(scratch),
        compiler_params=pltpu.CompilerParams(vmem_limit_bytes=24 * 1024 * 1024),
        cost_estimate=pl.CostEstimate(flops=flops, bytes_accessed=moved, transcendentals=0),
        name=name,
    )(*operands)


def per_device(flight_fields, top_fields, slowness, ref_slowness, flight_blocks, top_block):
    slabs, chips = lax.axis_size("depth"), lax.axis_size("z")
    own, length_y = flight_fields.shape[3:]
    rows = 2 * own
    length_x = rows * chips
    half = length_y // 2
    block = half // chips
    even_x, odd_x, turned_x = cas_tables(length_x)
    even_y, odd_y, turned_y = cas_tables(length_y)
    depth, chip, core = (lax.axis_index(name) for name in ("depth", "z", "core"))
    place = jnp.stack([chip, core, (depth == slabs - 1).astype(jnp.int32)]).astype(jnp.int32)
    sign = 1.0 - 2.0 * core.astype(F32)

    def of(shape, dtype=BF16):
        return jax.ShapeDtypeStruct(shape, dtype)

    def other_core(value):
        return lax.ppermute(value, "core", [(0, 1), (1, 0)])

    def scalars(block_id, reference_s):
        angular = omega_top * (block_id.astype(F32) + 1.0) / NFREQ
        return jnp.stack([angular, reference_s, sign])

    def above(slab):
        return jnp.where(slab == 0, top_block[0], flight_blocks[jnp.maximum(slab - 1, 0)])

    def other_field(fields):
        taken = lax.dynamic_index_in_dim(fields, 1 - core, 0, keepdims=False)
        return other_core(taken.reshape(rows, length_y))

    fields = flight_fields.reshape(2 * rows, length_y)
    fields_other = other_field(flight_fields[0])

    below = lax.ppermute(
        ref_slowness, "depth", [((d + 1) % slabs, d) for d in range(slabs)]
    )
    target = (depth + 1 - core) % slabs
    first_scalars = scalars(flight_blocks[depth], ref_slowness[0])
    target_scalars = scalars(above(target), jnp.where(core == 1, ref_slowness[0], below[0]))
    second_scalars = scalars(above(depth), ref_slowness[0])

    cells = own * length_y

    def factors(scalar, odd):
        return call(
            functools.partial(factors_kernel, odd, length_y), (place, scalar),
            [of((length_x, block), F32)] * 2, flops=400 * cells, name="factors", scalars=2,
        )

    def phases(scalar):
        return call(
            phase_kernel, (place, scalar, slowness[0], slowness_other),
            [of((rows, length_y), F32)] * 2, flops=800 * cells, name="phases", scalars=2,
        )

    pieces_of = [of((rows, 2 * block))] * chips
    lines = (2 * rows, half)
    part = pltpu.VMEM(lines, BF16)
    flops = 2 * 2 * rows * half * half
    x_part = pltpu.VMEM((length_x, 2 * block), BF16)

    def exchange(pieces, moving=None):
        got = []
        for k, piece in zip(partners(chips), pieces):
            if k == 0 and moving is None:
                got.append(piece)
                continue
            pairs = []
            for d in range(slabs):
                for z in range(chips):
                    for c in range(2):
                        there = (d + 1) % slabs if c == moving else d
                        pairs.append(
                            ((d * chips + z) * 2 + c, (there * chips + (z ^ k)) * 2 + c)
                        )
            got.append(lax.ppermute(piece, ("depth", "z", "core"), pairs))
        return got

    def to_modes(odd):
        return call(
            functools.partial(to_modes_kernel, odd),
            (place, fields, fields_other, turned_y if odd else even_y),
            pieces_of, [part, part], flops, "to_modes",
        )

    def along_x(pieces, factor):
        return call(
            functools.partial(along_x_kernel, chips),
            (place, *factor, even_x, odd_x, turned_x, *pieces),
            pieces_of, [x_part, x_part], 2 * flops, "along_x",
        )

    def even_part(pieces):
        return call(
            even_part_kernel, (place, even_y, *pieces), [of(lines, F32)], [part], flops, "even_part"
        )[0]

    evens = exchange(to_modes(0))
    odds = exchange(to_modes(1))
    slowness_other = other_core(slowness[0])
    top_other = other_field(top_fields)
    evens = exchange(along_x(evens, factors(first_scalars, 0)))
    odds = exchange(along_x(odds, factors(first_scalars, 1)))
    *evens, folded, first_keep, first_give = call(
        functools.partial(turn_around_kernel, chips),
        (
            place, *phases(first_scalars), top_fields.reshape(2 * rows, length_y), top_other,
            even_y, odd_y, even_part(evens), *odds,
        ),
        pieces_of + [of(lines)] + [of((rows, length_y))] * 2,
        [part, pltpu.VMEM((2 * rows, length_y), BF16), part], 2 * flops, "turn_around",
    )
    evens = exchange(evens, 1)
    odds = exchange(
        call(odd_modes_kernel, (place, folded, turned_y), pieces_of, [part], flops, "odd_modes"), 1
    )
    first_got = other_core(first_give)
    evens = exchange(along_x(evens, factors(target_scalars, 0)), 0)
    odds = exchange(along_x(odds, factors(target_scalars, 1)), 0)
    second_phases = phases(second_scalars)
    first_part = even_part(evens)
    give, keep = [
        call(
            functools.partial(half_space_kernel, index),
            (place, *second_phases, odd_y, first_part, *odds),
            [of((rows, length_y))], [pltpu.VMEM((rows, half), BF16)], flops // 2, "half_space",
        )[0]
        for index in (1, 0)
    ]
    got = other_core(give)
    fields, image = call(
        finish_kernel, (place, first_keep, first_got, keep, got),
        [of((2 * rows, length_y)), of((own, length_y), F32)], flops=8 * cells, name="finish",
    )
    return image[None], fields.reshape(flight_fields.shape)


def passed_along(value, axis, steps):
    count = lax.axis_size(axis)
    leading, last = (max(0, -steps), min(count, count - steps))
    return lax.ppermute(value, axis, [(source, source + steps) for source in range(leading, last)])


def make_table(length):
    positions = jnp.arange(length, dtype=jnp.int32)
    product = positions[:, None] * positions[None, :] % length
    angles = product.astype(jnp.float32) * (2.0 * math.pi / length)
    scaling = 1.0 / math.sqrt(length)
    return (jnp.concatenate([jnp.cos(angles), jnp.sin(angles)], axis=1) * scaling).astype(
        jnp.bfloat16
    )


def wavenumber(positions, length):
    signed = jnp.where(positions < length // 2, positions, positions - length)
    return signed.astype(jnp.float32) * (2.0 * math.pi / length)


def mix(product, along, half_size, orient):
    cosine_part = lax.slice_in_dim(product, 0, half_size, axis=along)
    sine_part = lax.slice_in_dim(product, half_size, 2 * half_size, axis=along)
    real_part = cosine_part[:, 0] + orient * sine_part[:, 1]
    imag_part = cosine_part[:, 1] - orient * sine_part[:, 0]
    return jnp.stack([real_part, imag_part], axis=1)


def rotate(values, cosines, sine_vals):
    real_part = values[:, 0] * cosines - values[:, 1] * sine_vals
    imag_part = values[:, 0] * sine_vals + values[:, 1] * cosines
    return jnp.stack([real_part, imag_part], axis=1)


def spectral(angular, reference_s, wave_x, wave_y):
    quad = (angular * reference_s) ** 2 - wave_x * wave_x - wave_y * wave_y
    travel = jnp.sqrt(jnp.maximum(quad, 0.0)) * step_length
    damping = jnp.exp(-jnp.sqrt(jnp.maximum(-quad, 0.0)) * step_length)
    cosines = damping * jnp.cos(travel)
    sine_vals = damping * jnp.sin(travel)
    return (jnp.stack([cosines, cosines]), jnp.stack([sine_vals, -sine_vals]))


def propagate(fields, spec_cos, spec_sin, space_cos, space_sin, to_cols, to_rows, table_x, table_y):
    length_y = table_y.shape[0]
    length_x = table_x.shape[0]
    product = jnp.einsum("fcry,yk->fckr", fields, table_y, preferred_element_type=jnp.float32)
    first = mix(product, 2, length_y, 1.0).astype(jnp.bfloat16)
    columns = to_cols(first)
    product = jnp.dot(columns, table_x, preferred_element_type=jnp.float32)
    spectrum = mix(product, 3, length_x, 1.0)
    shifted = rotate(spectrum, spec_cos, spec_sin).astype(jnp.bfloat16)
    product = jnp.dot(shifted, table_x, preferred_element_type=jnp.float32)
    back_x = mix(product, 3, length_x, -1.0).astype(jnp.bfloat16)
    rows_back = to_rows(back_x)
    product = jnp.einsum("fckr,ky->fcry", rows_back, table_y, preferred_element_type=jnp.float32)
    space = mix(product, 3, length_y, -1.0)
    return rotate(space, space_cos, space_sin).astype(jnp.bfloat16)


def together_cols(values):
    return lax.all_to_all(values, "trans", split_axis=2, concat_axis=3, tiled=True)


def together_rows(values):
    return lax.all_to_all(values, "trans", split_axis=3, concat_axis=2, tiled=True)


def advance(fields, block_id, slowness, ref_slowness, table_x, table_y):
    length_x = table_x.shape[0]
    length_y = table_y.shape[0]
    trans_count = lax.axis_size("trans")
    local_ky = length_y // trans_count
    ky_rows = lax.axis_index("trans") * local_ky + jnp.arange(local_ky, dtype=jnp.int32)
    wave_y = wavenumber(ky_rows, length_y)[:, None]
    wave_x = wavenumber(jnp.arange(length_x, dtype=jnp.int32), length_x)[None, :]
    angular = omega_top * (block_id.astype(jnp.float32) + 1.0) / NFREQ
    reference_s = ref_slowness[0]
    spec_cos, spec_sin = spectral(angular, reference_s, wave_x, wave_y)
    rotation = angular * (slowness[0] - reference_s) * step_length
    cos_r = jnp.cos(rotation)
    sin_r = jnp.sin(rotation)
    space_cos = jnp.stack([cos_r, cos_r])
    space_sin = jnp.stack([sin_r, -sin_r])
    fields = propagate(
        fields,
        spec_cos,
        spec_sin,
        space_cos,
        space_sin,
        together_cols,
        together_rows,
        table_x,
        table_y,
    )
    values = fields.astype(jnp.float32)
    terms = [values[0, 0] * values[1, 0] + values[0, 1] * values[1, 1]]
    return (fields, jnp.stack(terms))


def general_per_device(flight_fields, top_fields, slowness, ref_slowness, flight_blocks, top_block):
    table_x = make_table(flight_fields.shape[3] * lax.axis_size("trans"))
    table_y = make_table(flight_fields.shape[4])
    depth_idx = lax.axis_index("depth")
    first_block = flight_blocks[depth_idx]
    above_block = flight_blocks[jnp.maximum(depth_idx - 1, 0)]
    second_block = jnp.where(depth_idx == 0, top_block[0], above_block)
    after_first, first_terms = advance(
        flight_fields[0], first_block, slowness, ref_slowness, table_x, table_y
    )
    handed = passed_along(after_first, "depth", 1)
    incoming = jnp.where(depth_idx == 0, top_fields, handed)
    after_second, second_terms = advance(
        incoming, second_block, slowness, ref_slowness, table_x, table_y
    )
    return (first_terms + second_terms, after_second[None])


def solution(mesh):
    slabs, count = mesh.shape["depth"], mesh.shape["trans"]
    chips = count // 2

    def mapped(body, over, trans):
        placed = (
            P("depth", None, None, trans, None),
            P(None, None, trans, None),
            P("depth", trans, None),
            P("depth"),
            P(),
            P(),
        )
        return jax.shard_map(
            body,
            mesh=over,
            in_specs=placed,
            out_specs=(P("depth", trans, None), P("depth", None, None, trans, None)),
            check_vma=False,
        )

    def run(*arrays):
        length_x, length_y = arrays[0].shape[3:]
        fits = count % 2 == 0 and chips & (chips - 1) == 0
        fits = fits and length_y % (256 * chips) == 0 and length_y % 512 == 0
        if not fits or length_x % (32 * chips) or length_x % 128:
            return mapped(general_per_device, mesh, "trans")(*arrays)
        cores = Mesh(mesh.devices.reshape(slabs, chips, 2), ("depth", "z", "core"))
        return mapped(per_device, cores, ("z", "core"))(*arrays)

    return run
```

profile of v0, /device:TPU:9, one launch (start us, length us, event | category | flops | bytes accessed | tf_op | source)
XLA Modules:
  0.0 116.5 jit_solution(12341663787185116044)
XLA Ops:
  5.3 1.8 %to_modes.2 = (bf16[256,256]{1,0:T(8,128)(2,1)}, bf16[256,256]{1,0:T(8,128)(2,1)}, bf16[256,256]{1,0:T(8,128)(2,1)}, bf16[256,256]{1,0:T(8,128)(2,1)S(1)}) custom-call(s32[3]{0:T(128)S(1)} %pad_add_fusion.place_ref, bf16[512,1024]{1,0:T(8,128)(2,1)S(1)} %bitcast.22, bf16[256,1024]{1,0:T(8,128)(2,1)S(1)} %collective-permute-done.2.other_ref, ...), custom_call_target="tpu_custom_call" | custom-call | flops 268435456 | bytes 2621452 | tf_op jit(solution)/shard_map/to_modes/pallas_call | solution.py:268
  7.1 2.3 %collective-permute-start.3 = (bf16[256,256]{1,0:T(8,128)(2,1)}, bf16[256,256]{1,0:T(8,128)(2,1)S(1)}, u32[]{:S(2)}, u32[]{:S(2)}) collective-permute-start(bf16[256,256]{1,0:T(8,128)(2,1)} %get-tuple-element.55), channel_id=1, source_target_pairs={{0,4},{1,5},{2,6},{3,7},{4,0},{5,1},{6,2},{7,3},{8,12},{9,13},{10,... | collective-permute-start | bytes 393224 | tf_op jit(solution)/shard_map/ppermute | solution.py:355
  14.6 1.6 %collective-permute-start.5 = (bf16[256,256]{1,0:T(8,128)(2,1)}, bf16[256,256]{1,0:T(8,128)(2,1)S(1)}, u32[]{:S(2)}, u32[]{:S(2)}) collective-permute-start(bf16[256,256]{1,0:T(8,128)(2,1)} %get-tuple-element.57), channel_id=1, source_target_pairs={{0,2},{1,3},{2,0},{3,1},{4,6},{5,7},{6,4},{7,5},{8,10},{9,11},{10,... | collective-permute-start | bytes 393224 | tf_op jit(solution)/shard_map/ppermute | solution.py:355
  18.7 2.6 %collective-permute-done.4.refs_1_ = bf16[256,256]{1,0:T(8,128)(2,1)S(1)} collective-permute-done((bf16[256,256]{1,0:T(8,128)(2,1)}, bf16[256,256]{1,0:T(8,128)(2,1)S(1)}, u32[]{:S(2)}, u32[]{:S(2)}) %collective-permute-start.4) | collective-permute-done | bytes 131104 | tf_op jit(solution)/shard_map/ppermute | solution.py:355
  22.7 1.9 %collective-permute-start.9 = (bf16[256,256]{1,0:T(8,128)(2,1)S(1)}, bf16[256,256]{1,0:T(8,128)(2,1)S(1)}, u32[]{:S(2)}, u32[]{:S(2)}) collective-permute-start(bf16[256,256]{1,0:T(8,128)(2,1)S(1)} %get-tuple-element.65), channel_id=1, source_target_pairs={{0,4},{1,5},{2,6},{3,7},{4,0},{5,1},{6,2},{7,3},{8,12},{9,13},{10,... | collective-permute-start | bytes 393224 | tf_op jit(solution)/shard_map/ppermute | solution.py:355
  24.6 1.8 %factors.4 = (f32[1024,128]{1,0:T(8,128)S(1)}, f32[1024,128]{1,0:T(8,128)S(1)}) custom-call(s32[3]{0:T(128)S(1)} %pad_add_fusion.place_ref, f32[3]{0:T(128)S(1)} %get-tuple-element.103.scalar_ref), custom_call_target="tpu_custom_call" | custom-call | flops 52428800 | bytes 1048600 | tf_op jit(solution)/shard_map/factors/pallas_call | solution.py:268
  26.5 1.5 %along_x.4 = (bf16[256,256]{1,0:T(8,128)(2,1)S(1)}, bf16[256,256]{1,0:T(8,128)(2,1)S(1)}, bf16[256,256]{1,0:T(8,128)(2,1)S(1)}, bf16[256,256]{1,0:T(8,128)(2,1)S(1)}) custom-call(s32[3]{0:T(128)S(1)} %pad_add_fusion.place_ref, f32[1024,128]{1,0:T(8,128)S(1)} %get-tuple-element.53.cos_ref, f32[1024,128]{1,0:T(8,128)S(1)} %get-tuple-element.54.sin_ref, ...), custom_call_target="tpu_custom_call" | custom-call | flops 536870912 | bytes 3670028 | tf_op jit(solution)/shard_map/along_x/pallas_call | solution.py:268
  29.1 1.4 %collective-permute-start.7 = (bf16[256,256]{1,0:T(8,128)(2,1)S(1)}, bf16[256,256]{1,0:T(8,128)(2,1)S(1)}, u32[]{:S(2)}, u32[]{:S(2)}) collective-permute-start(bf16[256,256]{1,0:T(8,128)(2,1)S(1)} %get-tuple-element.60), channel_id=1, source_target_pairs={{0,6},{1,7},{2,4},{3,5},{4,2},{5,3},{6,0},{7,1},{8,14},{9,15},{10,... | collective-permute-start | bytes 393224 | tf_op jit(solution)/shard_map/ppermute | solution.py:355
  30.5 1.8 %factors.5 = (f32[1024,128]{1,0:T(8,128)S(1)}, f32[1024,128]{1,0:T(8,128)S(1)}) custom-call(s32[3]{0:T(128)S(1)} %pad_add_fusion.place_ref, f32[3]{0:T(128)S(1)} %get-tuple-element.103.scalar_ref), custom_call_target="tpu_custom_call" | custom-call | flops 52428800 | bytes 1048600 | tf_op jit(solution)/shard_map/factors/pallas_call | solution.py:268
  32.3 5.7 %collective-permute-done.9.refs_0_ = bf16[256,256]{1,0:T(8,128)(2,1)S(1)} collective-permute-done((bf16[256,256]{1,0:T(8,128)(2,1)S(1)}, bf16[256,256]{1,0:T(8,128)(2,1)S(1)}, u32[]{:S(2)}, u32[]{:S(2)}) %collective-permute-start.9) | collective-permute-done | bytes 131104 | tf_op jit(solution)/shard_map/ppermute | solution.py:355
  38.0 1.5 %along_x.5 = (bf16[256,256]{1,0:T(8,128)(2,1)S(1)}, bf16[256,256]{1,0:T(8,128)(2,1)S(1)}, bf16[256,256]{1,0:T(8,128)(2,1)S(1)}, bf16[256,256]{1,0:T(8,128)(2,1)S(1)}) custom-call(s32[3]{0:T(128)S(1)} %pad_add_fusion.place_ref, f32[1024,128]{1,0:T(8,128)S(1)} %get-tuple-element.63.cos_ref, f32[1024,128]{1,0:T(8,128)S(1)} %get-tuple-element.64.sin_ref, ...), custom_call_target="tpu_custom_call" | custom-call | flops 536870912 | bytes 3670028 | tf_op jit(solution)/shard_map/along_x/pallas_call | solution.py:268
  39.5 3.2 %collective-permute-start.12 = (bf16[256,256]{1,0:T(8,128)(2,1)S(1)}, bf16[256,256]{1,0:T(8,128)(2,1)S(1)}, u32[]{:S(2)}, u32[]{:S(2)}) collective-permute-start(bf16[256,256]{1,0:T(8,128)(2,1)S(1)} %get-tuple-element.69), channel_id=1, source_target_pairs={{0,4},{1,5},{2,6},{3,7},{4,0},{5,1},{6,2},{7,3},{8,12},{9,13},{10,... | collective-permute-start | bytes 393224 | tf_op jit(solution)/shard_map/ppermute | solution.py:355
  43.6 1.5 %collective-permute-start.14 = (bf16[256,256]{1,0:T(8,128)(2,1)S(1)}, bf16[256,256]{1,0:T(8,128)(2,1)S(1)}, u32[]{:S(2)}, u32[]{:S(2)}) collective-permute-start(bf16[256,256]{1,0:T(8,128)(2,1)S(1)} %get-tuple-element.71), channel_id=1, source_target_pairs={{0,2},{1,3},{2,0},{3,1},{4,6},{5,7},{6,4},{7,5},{8,10},{9,11},{10,... | collective-permute-start | bytes 393224 | tf_op jit(solution)/shard_map/ppermute | solution.py:355
  45.1 2.7 %phases.2 = (f32[256,1024]{1,0:T(8,128)S(1)}, f32[256,1024]{1,0:T(8,128)S(1)}) custom-call(s32[3]{0:T(128)S(1)} %pad_add_fusion.place_ref, f32[3]{0:T(128)S(1)} %get-tuple-element.103.scalar_ref, f32[128,1024]{1,0:T(8,128)} %bitcast.4.mine_ref, f32[128,1024]{1,0:T(8,128)} %collective-permute-done.other_ref), custom_call_target="tpu_custom_call" | custom-call | flops 104857600 | bytes 3145752 | tf_op jit(solution)/shard_map/phases/pallas_call | solution.py:268
  49.0 2.6 %collective-permute-done.12.refs_0_ = bf16[256,256]{1,0:T(8,128)(2,1)S(1)} collective-permute-done((bf16[256,256]{1,0:T(8,128)(2,1)S(1)}, bf16[256,256]{1,0:T(8,128)(2,1)S(1)}, u32[]{:S(2)}, u32[]{:S(2)}) %collective-permute-start.12) | collective-permute-done | bytes 131104 | tf_op jit(solution)/shard_map/ppermute | solution.py:355
  51.5 3.3 %collective-permute-done.13.refs_1_ = bf16[256,256]{1,0:T(8,128)(2,1)S(1)} collective-permute-done((bf16[256,256]{1,0:T(8,128)(2,1)S(1)}, bf16[256,256]{1,0:T(8,128)(2,1)S(1)}, u32[]{:S(2)}, u32[]{:S(2)}) %collective-permute-start.13) | collective-permute-done | bytes 131104 | tf_op jit(solution)/shard_map/ppermute | solution.py:355
  54.8 3.2 %turn_around.1 = (bf16[256,256]{1,0:T(8,128)(2,1)}, bf16[256,256]{1,0:T(8,128)(2,1)S(1)}, bf16[256,256]{1,0:T(8,128)(2,1)S(1)}, bf16[256,256]{1,0:T(8,128)(2,1)S...) custom-call(s32[3]{0:T(128)S(1)} %pad_add_fusion.place_ref, ...), custom_call_target="tpu_custom_call" | custom-call | flops 536870912 | bytes 8388620 | tf_op jit(solution)/shard_map/turn_around/pallas_call | solution.py:268
  58.7 1.4 %collective-permute-start.17 = (bf16[256,256]{1,0:T(8,128)(2,1)}, bf16[256,256]{1,0:T(8,128)(2,1)S(1)}, u32[]{:S(2)}, u32[]{:S(2)}) collective-permute-start(bf16[256,256]{1,0:T(8,128)(2,1)} %get-tuple-element.79), channel_id=1, source_target_pairs={{0,4},{1,13},{2,6},{3,15},{4,0},{5,9},{6,2},{7,11},{8,12},{9,21},{... | collective-permute-start | bytes 393224 | tf_op jit(solution)/shard_map/ppermute | solution.py:355
  63.4 2.4 %collective-permute-start.18 = (bf16[256,256]{1,0:T(8,128)(2,1)}, bf16[256,256]{1,0:T(8,128)(2,1)S(1)}, u32[]{:S(2)}, u32[]{:S(2)}) collective-permute-start(bf16[256,256]{1,0:T(8,128)(2,1)} %copy-done.7), channel_id=1, source_target_pairs={{0,6},{1,15},{2,4},{3,13},{4,2},{5,11},{6,0},{7,9},{8,14},{9,23},{... | collective-permute-start | bytes 393224 | tf_op jit(solution)/shard_map/ppermute | solution.py:355
  65.7 2.8 %collective-permute-start.19 = (bf16[256,256]{1,0:T(8,128)(2,1)S(1)}, bf16[256,256]{1,0:T(8,128)(2,1)S(1)}, u32[]{:S(2)}, u32[]{:S(2)}) collective-permute-start(bf16[256,256]{1,0:T(8,128)(2,1)S(1)} %get-tuple-element.81), channel_id=1, source_target_pairs={{0,2},{1,11},{2,0},{3,9},{4,6},{5,15},{6,4},{7,13},{8,10},{9,19},{... | collective-permute-start | bytes 393224 | tf_op jit(solution)/shard_map/ppermute | solution.py:355
  68.5 2.9 %collective-permute-start.20 = (bf16[256,256]{1,0:T(8,128)(2,1)S(1)}, bf16[256,256]{1,0:T(8,128)(2,1)S(1)}, u32[]{:S(2)}, u32[]{:S(2)}) collective-permute-start(bf16[256,256]{1,0:T(8,128)(2,1)S(1)} %get-tuple-element.82), channel_id=1, source_target_pairs={{0,0},{1,9},{2,2},{3,11},{4,4},{5,13},{6,6},{7,15},{8,8},{9,17},{1... | collective-permute-start | bytes 393224 | tf_op jit(solution)/shard_map/ppermute | solution.py:355
  72.5 1.8 %collective-permute-start.25 = (bf16[256,256]{1,0:T(8,128)(2,1)S(1)}, bf16[256,256]{1,0:T(8,128)(2,1)S(1)}, u32[]{:S(2)}, u32[]{:S(2)}) collective-permute-start(bf16[256,256]{1,0:T(8,128)(2,1)S(1)} %get-tuple-element.90), channel_id=1, source_target_pairs={{0,4},{1,13},{2,6},{3,15},{4,0},{5,9},{6,2},{7,11},{8,12},{9,21},{... | collective-permute-start | bytes 393224 | tf_op jit(solution)/shard_map/ppermute | solution.py:355
  74.7 1.8 %factors.6 = (f32[1024,128]{1,0:T(8,128)S(1)}, f32[1024,128]{1,0:T(8,128)S(1)}) custom-call(s32[3]{0:T(128)S(1)} %pad_add_fusion.place_ref, f32[3]{0:T(128)S(1)} %maximum_maximum_fusion.2.scalar_ref), custom_call_target="tpu_custom_call" | custom-call | flops 52428800 | bytes 1048600 | tf_op jit(solution)/shard_map/factors/pallas_call | solution.py:268
  76.5 3.5 %collective-permute-start.27 = (bf16[256,256]{1,0:T(8,128)(2,1)S(1)}, bf16[256,256]{1,0:T(8,128)(2,1)S(1)}, u32[]{:S(2)}, u32[]{:S(2)}) collective-permute-start(bf16[256,256]{1,0:T(8,128)(2,1)S(1)} %get-tuple-element.92), channel_id=1, source_target_pairs={{0,2},{1,11},{2,0},{3,9},{4,6},{5,15},{6,4},{7,13},{8,10},{9,19},{... | collective-permute-start | bytes 393224 | tf_op jit(solution)/shard_map/ppermute | solution.py:355
  80.0 2.9 %collective-permute-start.28 = (bf16[256,256]{1,0:T(8,128)(2,1)S(1)}, bf16[256,256]{1,0:T(8,128)(2,1)S(1)}, u32[]{:S(2)}, u32[]{:S(2)}) collective-permute-start(bf16[256,256]{1,0:T(8,128)(2,1)S(1)} %get-tuple-element.93), channel_id=1, source_target_pairs={{0,0},{1,9},{2,2},{3,11},{4,4},{5,13},{6,6},{7,15},{8,8},{9,17},{1... | collective-permute-start | bytes 393224 | tf_op jit(solution)/shard_map/ppermute | solution.py:355
  82.9 1.5 %along_x.6 = (bf16[256,256]{1,0:T(8,128)(2,1)S(1)}, bf16[256,256]{1,0:T(8,128)(2,1)S(1)}, bf16[256,256]{1,0:T(8,128)(2,1)S(1)}, bf16[256,256]{1,0:T(8,128)(2,1)S(1)}) custom-call(s32[3]{0:T(128)S(1)} %pad_add_fusion.place_ref, f32[1024,128]{1,0:T(8,128)S(1)} %get-tuple-element.77.cos_ref, f32[1024,128]{1,0:T(8,128)S(1)} %get-tuple-element.78.sin_ref, ...), custom_call_target="tpu_custom_call" | custom-call | flops 536870912 | bytes 3670028 | tf_op jit(solution)/shard_map/along_x/pallas_call | solution.py:268
  86.5 6.5 %collective-permute-done.26.refs_1_ = bf16[256,256]{1,0:T(8,128)(2,1)S(1)} collective-permute-done((bf16[256,256]{1,0:T(8,128)(2,1)S(1)}, bf16[256,256]{1,0:T(8,128)(2,1)S(1)}, u32[]{:S(2)}, u32[]{:S(2)}) %collective-permute-start.26) | collective-permute-done | bytes 131104 | tf_op jit(solution)/shard_map/ppermute | solution.py:355
  93.0 1.8 %factors.7 = (f32[1024,128]{1,0:T(8,128)S(1)}, f32[1024,128]{1,0:T(8,128)S(1)}) custom-call(s32[3]{0:T(128)S(1)} %pad_add_fusion.place_ref, f32[3]{0:T(128)S(1)} %maximum_maximum_fusion.2.scalar_ref), custom_call_target="tpu_custom_call" | custom-call | flops 52428800 | bytes 1048600 | tf_op jit(solution)/shard_map/factors/pallas_call | solution.py:268
  95.5 1.5 %along_x.7 = (bf16[256,256]{1,0:T(8,128)(2,1)S(1)}, bf16[256,256]{1,0:T(8,128)(2,1)S(1)}, bf16[256,256]{1,0:T(8,128)(2,1)S(1)}, bf16[256,256]{1,0:T(8,128)(2,1)S(1)}) custom-call(s32[3]{0:T(128)S(1)} %pad_add_fusion.place_ref, f32[1024,128]{1,0:T(8,128)S(1)} %get-tuple-element.87.cos_ref, f32[1024,128]{1,0:T(8,128)S(1)} %get-tuple-element.88.sin_ref, ...), custom_call_target="tpu_custom_call" | custom-call | flops 536870912 | bytes 3670028 | tf_op jit(solution)/shard_map/along_x/pallas_call | solution.py:268
  101.3 2.7 %phases.3 = (f32[256,1024]{1,0:T(8,128)S(1)}, f32[256,1024]{1,0:T(8,128)S(1)}) custom-call(s32[3]{0:T(128)S(1)} %pad_add_fusion.place_ref, f32[3]{0:T(128)S(1)} %get-tuple-element.104.scalar_ref, f32[128,1024]{1,0:T(8,128)} %bitcast.4.mine_ref, f32[128,1024]{1,0:T(8,128)} %collective-permute-done.other_ref), custom_call_target="tpu_custom_call" | custom-call | flops 104857600 | bytes 3145752 | tf_op jit(solution)/shard_map/phases/pallas_call | solution.py:268
  104.0 5.6 %collective-permute-start.15 = (bf16[256,1024]{1,0:T(8,128)(2,1)S(1)}, bf16[256,1024]{1,0:T(8,128)(2,1)S(1)}, u32[]{:S(2)}, u32[]{:S(2)}) collective-permute-start(bf16[256,1024]{1,0:T(8,128)(2,1)S(1)} %get-tuple-element.74), channel_id=1, source_target_pairs={{0,1},{1,0},{2,3},{3,2},{4,5},{5,4},{6,7},{7,6},{8,9},{9,8},{10,11... | collective-permute-start | bytes 1572872 | tf_op jit(solution)/shard_map/ppermute | solution.py:297
  114.7 1.8 %finish.1 = (bf16[512,1024]{1,0:T(8,128)(2,1)}, f32[128,1024]{1,0:T(8,128)}) custom-call(s32[3]{0:T(128)S(1)} %pad_add_fusion.place_ref, bf16[256,1024]{1,0:T(8,128)(2,1)S(1)} %get-tuple-element.73.first_ref, bf16[256,1024]{1,0:T(8,128)(2,1)S(1)} %collective-permute-done.15.first_other_ref, bf16[256,1024]{1,0:T(8,128)(2,1)S(1)} %half_space.2.keep_ref, ...), custom_call_target="tpu_custom_call" | custom-call | flops 1048576 | bytes 3670028 | tf_op jit(solution)/shard_map/finish/pallas_call | solution.py:268
  (79 shorter events, 30.8 us)
Async XLA Ops:
  2.5 37.0 %collective-permute-start = (f32[128,1024]{1,0:T(8,128)}, f32[128,1024]{1,0:T(8,128)}, u32[]{:S(2)}, u32[]{:S(2)}) collective-permute-start(f32[128,1024]{1,0:T(8,128)} %bitcast.4.mine_ref), channel_id=1, source_target_pairs={{0,1},{1,0},{2,3},{3,2},{4,5},{5,4},{6,7},{7,6},{8,9},{9,8},{10,11... | collective-permute-start | bytes 1572872 | tf_op jit(solution)/shard_map/ppermute | solution.py:297
  7.1 11.4 %collective-permute-start.3 = (bf16[256,256]{1,0:T(8,128)(2,1)}, bf16[256,256]{1,0:T(8,128)(2,1)S(1)}, u32[]{:S(2)}, u32[]{:S(2)}) collective-permute-start(bf16[256,256]{1,0:T(8,128)(2,1)} %get-tuple-element.55), channel_id=1, source_target_pairs={{0,4},{1,5},{2,6},{3,7},{4,0},{5,1},{6,2},{7,3},{8,12},{9,13},{10,... | collective-permute-start | bytes 393224 | tf_op jit(solution)/shard_map/ppermute | solution.py:355
  9.4 11.9 %collective-permute-start.4 = (bf16[256,256]{1,0:T(8,128)(2,1)}, bf16[256,256]{1,0:T(8,128)(2,1)S(1)}, u32[]{:S(2)}, u32[]{:S(2)}) collective-permute-start(bf16[256,256]{1,0:T(8,128)(2,1)} %get-tuple-element.56), channel_id=1, source_target_pairs={{0,6},{1,7},{2,4},{3,5},{4,2},{5,3},{6,0},{7,1},{8,14},{9,15},{10,... | collective-permute-start | bytes 393224 | tf_op jit(solution)/shard_map/ppermute | solution.py:355
  10.3 38.7 %collective-permute-start.1 = (bf16[256,1024]{1,0:T(8,128)(2,1)}, bf16[256,1024]{1,0:T(8,128)(2,1)}, u32[]{:S(2)}, u32[]{:S(2)}) collective-permute-start(bf16[256,1024]{1,0:T(8,128)(2,1)} %bitcast.6), channel_id=1, source_target_pairs={{0,1},{1,0},{2,3},{3,2},{4,5},{5,4},{6,7},{7,6},{8,9},{9,8},{10,11... | collective-permute-start | bytes 1572872 | tf_op jit(solution)/shard_map/ppermute | solution.py:297
  14.6 8.1 %collective-permute-start.5 = (bf16[256,256]{1,0:T(8,128)(2,1)}, bf16[256,256]{1,0:T(8,128)(2,1)S(1)}, u32[]{:S(2)}, u32[]{:S(2)}) collective-permute-start(bf16[256,256]{1,0:T(8,128)(2,1)} %get-tuple-element.57), channel_id=1, source_target_pairs={{0,2},{1,3},{2,0},{3,1},{4,6},{5,7},{6,4},{7,5},{8,10},{9,11},{10,... | collective-permute-start | bytes 393224 | tf_op jit(solution)/shard_map/ppermute | solution.py:355
  18.5 9.5 %collective-permute-start.10 = (bf16[256,256]{1,0:T(8,128)(2,1)S(1)}, bf16[256,256]{1,0:T(8,128)(2,1)S(1)}, u32[]{:S(2)}, u32[]{:S(2)}) collective-permute-start(bf16[256,256]{1,0:T(8,128)(2,1)S(1)} %get-tuple-element.66), channel_id=1, source_target_pairs={{0,6},{1,7},{2,4},{3,5},{4,2},{5,3},{6,0},{7,1},{8,14},{9,15},{10,... | collective-permute-start | bytes 393224 | tf_op jit(solution)/shard_map/ppermute | solution.py:355
  21.3 7.8 %collective-permute-start.11 = (bf16[256,256]{1,0:T(8,128)(2,1)S(1)}, bf16[256,256]{1,0:T(8,128)(2,1)S(1)}, u32[]{:S(2)}, u32[]{:S(2)}) collective-permute-start(bf16[256,256]{1,0:T(8,128)(2,1)S(1)} %get-tuple-element.67), channel_id=1, source_target_pairs={{0,2},{1,3},{2,0},{3,1},{4,6},{5,7},{6,4},{7,5},{8,10},{9,11},{10,... | collective-permute-start | bytes 393224 | tf_op jit(solution)/shard_map/ppermute | solution.py:355
  22.7 15.3 %collective-permute-start.9 = (bf16[256,256]{1,0:T(8,128)(2,1)S(1)}, bf16[256,256]{1,0:T(8,128)(2,1)S(1)}, u32[]{:S(2)}, u32[]{:S(2)}) collective-permute-start(bf16[256,256]{1,0:T(8,128)(2,1)S(1)} %get-tuple-element.65), channel_id=1, source_target_pairs={{0,4},{1,5},{2,6},{3,7},{4,0},{5,1},{6,2},{7,3},{8,12},{9,13},{10,... | collective-permute-start | bytes 393224 | tf_op jit(solution)/shard_map/ppermute | solution.py:355
  27.9 14.7 %collective-permute-start.6 = (bf16[256,256]{1,0:T(8,128)(2,1)S(1)}, bf16[256,256]{1,0:T(8,128)(2,1)S(1)}, u32[]{:S(2)}, u32[]{:S(2)}) collective-permute-start(bf16[256,256]{1,0:T(8,128)(2,1)S(1)} %get-tuple-element.59), channel_id=1, source_target_pairs={{0,4},{1,5},{2,6},{3,7},{4,0},{5,1},{6,2},{7,3},{8,12},{9,13},{10,... | collective-permute-start | bytes 393224 | tf_op jit(solution)/shard_map/ppermute | solution.py:355
  29.1 14.6 %collective-permute-start.7 = (bf16[256,256]{1,0:T(8,128)(2,1)S(1)}, bf16[256,256]{1,0:T(8,128)(2,1)S(1)}, u32[]{:S(2)}, u32[]{:S(2)}) collective-permute-start(bf16[256,256]{1,0:T(8,128)(2,1)S(1)} %get-tuple-element.60), channel_id=1, source_target_pairs={{0,6},{1,7},{2,4},{3,5},{4,2},{5,3},{6,0},{7,1},{8,14},{9,15},{10,... | collective-permute-start | bytes 393224 | tf_op jit(solution)/shard_map/ppermute | solution.py:355
  38.0 9.8 %collective-permute-start.8 = (bf16[256,256]{1,0:T(8,128)(2,1)S(1)}, bf16[256,256]{1,0:T(8,128)(2,1)S(1)}, u32[]{:S(2)}, u32[]{:S(2)}) collective-permute-start(bf16[256,256]{1,0:T(8,128)(2,1)S(1)} %get-tuple-element.61), channel_id=1, source_target_pairs={{0,2},{1,3},{2,0},{3,1},{4,6},{5,7},{6,4},{7,5},{8,10},{9,11},{10,... | collective-permute-start | bytes 393224 | tf_op jit(solution)/shard_map/ppermute | solution.py:355
  39.5 12.0 %collective-permute-start.12 = (bf16[256,256]{1,0:T(8,128)(2,1)S(1)}, bf16[256,256]{1,0:T(8,128)(2,1)S(1)}, u32[]{:S(2)}, u32[]{:S(2)}) collective-permute-start(bf16[256,256]{1,0:T(8,128)(2,1)S(1)} %get-tuple-element.69), channel_id=1, source_target_pairs={{0,4},{1,5},{2,6},{3,7},{4,0},{5,1},{6,2},{7,3},{8,12},{9,13},{10,... | collective-permute-start | bytes 393224 | tf_op jit(solution)/shard_map/ppermute | solution.py:355
  42.7 12.1 %collective-permute-start.13 = (bf16[256,256]{1,0:T(8,128)(2,1)S(1)}, bf16[256,256]{1,0:T(8,128)(2,1)S(1)}, u32[]{:S(2)}, u32[]{:S(2)}) collective-permute-start(bf16[256,256]{1,0:T(8,128)(2,1)S(1)} %get-tuple-element.70), channel_id=1, source_target_pairs={{0,6},{1,7},{2,4},{3,5},{4,2},{5,3},{6,0},{7,1},{8,14},{9,15},{10,... | collective-permute-start | bytes 393224 | tf_op jit(solution)/shard_map/ppermute | solution.py:355
  43.6 11.2 %collective-permute-start.14 = (bf16[256,256]{1,0:T(8,128)(2,1)S(1)}, bf16[256,256]{1,0:T(8,128)(2,1)S(1)}, u32[]{:S(2)}, u32[]{:S(2)}) collective-permute-start(bf16[256,256]{1,0:T(8,128)(2,1)S(1)} %get-tuple-element.71), channel_id=1, source_target_pairs={{0,2},{1,3},{2,0},{3,1},{4,6},{5,7},{6,4},{7,5},{8,10},{9,11},{10,... | collective-permute-start | bytes 393224 | tf_op jit(solution)/shard_map/ppermute | solution.py:355
  58.7 15.6 %collective-permute-start.17 = (bf16[256,256]{1,0:T(8,128)(2,1)}, bf16[256,256]{1,0:T(8,128)(2,1)S(1)}, u32[]{:S(2)}, u32[]{:S(2)}) collective-permute-start(bf16[256,256]{1,0:T(8,128)(2,1)} %get-tuple-element.79), channel_id=1, source_target_pairs={{0,4},{1,13},{2,6},{3,15},{4,0},{5,9},{6,2},{7,11},{8,12},{9,21},{... | collective-permute-start | bytes 393224 | tf_op jit(solution)/shard_map/ppermute | solution.py:355
  60.1 2.6 %collective-permute-start.16 = (f32[1]{0:T(128)}, f32[1]{0:T(128)}, u32[]{:S(2)}, u32[]{:S(2)}) collective-permute-start(f32[1]{0:T(128)} %param.15), channel_id=1, source_target_pairs={{8,0},{16,8},{24,16},{0,24},{9,1},{17,9},{25,17},{1,25},{10,2},{18... | collective-permute-start | bytes 20 | tf_op jit(solution)/shard_map/ppermute | solution.py:313
  63.4 13.2 %collective-permute-start.18 = (bf16[256,256]{1,0:T(8,128)(2,1)}, bf16[256,256]{1,0:T(8,128)(2,1)S(1)}, u32[]{:S(2)}, u32[]{:S(2)}) collective-permute-start(bf16[256,256]{1,0:T(8,128)(2,1)} %copy-done.7), channel_id=1, source_target_pairs={{0,6},{1,15},{2,4},{3,13},{4,2},{5,11},{6,0},{7,9},{8,14},{9,23},{... | collective-permute-start | bytes 393224 | tf_op jit(solution)/shard_map/ppermute | solution.py:355
  65.7 14.3 %collective-permute-start.19 = (bf16[256,256]{1,0:T(8,128)(2,1)S(1)}, bf16[256,256]{1,0:T(8,128)(2,1)S(1)}, u32[]{:S(2)}, u32[]{:S(2)}) collective-permute-start(bf16[256,256]{1,0:T(8,128)(2,1)S(1)} %get-tuple-element.81), channel_id=1, source_target_pairs={{0,2},{1,11},{2,0},{3,9},{4,6},{5,15},{6,4},{7,13},{8,10},{9,19},{... | collective-permute-start | bytes 393224 | tf_op jit(solution)/shard_map/ppermute | solution.py:355
  68.5 14.4 %collective-permute-start.20 = (bf16[256,256]{1,0:T(8,128)(2,1)S(1)}, bf16[256,256]{1,0:T(8,128)(2,1)S(1)}, u32[]{:S(2)}, u32[]{:S(2)}) collective-permute-start(bf16[256,256]{1,0:T(8,128)(2,1)S(1)} %get-tuple-element.82), channel_id=1, source_target_pairs={{0,0},{1,9},{2,2},{3,11},{4,4},{5,13},{6,6},{7,15},{8,8},{9,17},{1... | collective-permute-start | bytes 393224 | tf_op jit(solution)/shard_map/ppermute | solution.py:355
  72.5 13.0 %collective-permute-start.25 = (bf16[256,256]{1,0:T(8,128)(2,1)S(1)}, bf16[256,256]{1,0:T(8,128)(2,1)S(1)}, u32[]{:S(2)}, u32[]{:S(2)}) collective-permute-start(bf16[256,256]{1,0:T(8,128)(2,1)S(1)} %get-tuple-element.90), channel_id=1, source_target_pairs={{0,4},{1,13},{2,6},{3,15},{4,0},{5,9},{6,2},{7,11},{8,12},{9,21},{... | collective-permute-start | bytes 393224 | tf_op jit(solution)/shard_map/ppermute | solution.py:355
  74.3 18.8 %collective-permute-start.26 = (bf16[256,256]{1,0:T(8,128)(2,1)S(1)}, bf16[256,256]{1,0:T(8,128)(2,1)S(1)}, u32[]{:S(2)}, u32[]{:S(2)}) collective-permute-start(bf16[256,256]{1,0:T(8,128)(2,1)S(1)} %get-tuple-element.91), channel_id=1, source_target_pairs={{0,6},{1,15},{2,4},{3,13},{4,2},{5,11},{6,0},{7,9},{8,14},{9,23},{... | collective-permute-start | bytes 393224 | tf_op jit(solution)/shard_map/ppermute | solution.py:355
  76.5 18.3 %collective-permute-start.27 = (bf16[256,256]{1,0:T(8,128)(2,1)S(1)}, bf16[256,256]{1,0:T(8,128)(2,1)S(1)}, u32[]{:S(2)}, u32[]{:S(2)}) collective-permute-start(bf16[256,256]{1,0:T(8,128)(2,1)S(1)} %get-tuple-element.92), channel_id=1, source_target_pairs={{0,2},{1,11},{2,0},{3,9},{4,6},{5,15},{6,4},{7,13},{8,10},{9,19},{... | collective-permute-start | bytes 393224 | tf_op jit(solution)/shard_map/ppermute | solution.py:355
  80.0 15.5 %collective-permute-start.28 = (bf16[256,256]{1,0:T(8,128)(2,1)S(1)}, bf16[256,256]{1,0:T(8,128)(2,1)S(1)}, u32[]{:S(2)}, u32[]{:S(2)}) collective-permute-start(bf16[256,256]{1,0:T(8,128)(2,1)S(1)} %get-tuple-element.93), channel_id=1, source_target_pairs={{0,0},{1,9},{2,2},{3,11},{4,4},{5,13},{6,6},{7,15},{8,8},{9,17},{1... | collective-permute-start | bytes 393224 | tf_op jit(solution)/shard_map/ppermute | solution.py:355
  84.4 14.0 %collective-permute-start.21 = (bf16[256,256]{1,0:T(8,128)(2,1)S(1)}, bf16[256,256]{1,0:T(8,128)(2,1)S(1)}, u32[]{:S(2)}, u32[]{:S(2)}) collective-permute-start(bf16[256,256]{1,0:T(8,128)(2,1)S(1)} %get-tuple-element.83), channel_id=1, source_target_pairs={{0,12},{1,5},{2,14},{3,7},{4,8},{5,1},{6,10},{7,3},{8,20},{9,13},{... | collective-permute-start | bytes 393224 | tf_op jit(solution)/shard_map/ppermute | solution.py:355
  85.5 14.2 %collective-permute-start.22 = (bf16[256,256]{1,0:T(8,128)(2,1)S(1)}, bf16[256,256]{1,0:T(8,128)(2,1)S(1)}, u32[]{:S(2)}, u32[]{:S(2)}) collective-permute-start(bf16[256,256]{1,0:T(8,128)(2,1)S(1)} %get-tuple-element.84), channel_id=1, source_target_pairs={{0,14},{1,7},{2,12},{3,5},{4,10},{5,3},{6,8},{7,1},{8,22},{9,15},{... | collective-permute-start | bytes 393224 | tf_op jit(solution)/shard_map/ppermute | solution.py:355
  93.0 7.6 %collective-permute-start.23 = (bf16[256,256]{1,0:T(8,128)(2,1)S(1)}, bf16[256,256]{1,0:T(8,128)(2,1)S(1)}, u32[]{:S(2)}, u32[]{:S(2)}) collective-permute-start(bf16[256,256]{1,0:T(8,128)(2,1)S(1)} %get-tuple-element.85), channel_id=1, source_target_pairs={{0,10},{1,3},{2,8},{3,1},{4,14},{5,7},{6,12},{7,5},{8,18},{9,11},{... | collective-permute-start | bytes 393224 | tf_op jit(solution)/shard_map/ppermute | solution.py:355
  94.8 9.2 %collective-permute-start.24 = (bf16[256,256]{1,0:T(8,128)(2,1)S(1)}, bf16[256,256]{1,0:T(8,128)(2,1)S(1)}, u32[]{:S(2)}, u32[]{:S(2)}) collective-permute-start(bf16[256,256]{1,0:T(8,128)(2,1)S(1)} %get-tuple-element.86), channel_id=1, source_target_pairs={{0,8},{1,1},{2,10},{3,3},{4,12},{5,5},{6,14},{7,7},{8,16},{9,9},{1... | collective-permute-start | bytes 393224 | tf_op jit(solution)/shard_map/ppermute | solution.py:355
  97.0 13.7 %collective-permute-start.29 = (bf16[256,256]{1,0:T(8,128)(2,1)S(1)}, bf16[256,256]{1,0:T(8,128)(2,1)S(1)}, u32[]{:S(2)}, u32[]{:S(2)}) collective-permute-start(bf16[256,256]{1,0:T(8,128)(2,1)S(1)} %get-tuple-element.94), channel_id=1, source_target_pairs={{0,12},{1,5},{2,14},{3,7},{4,8},{5,1},{6,10},{7,3},{8,20},{9,13},{... | collective-permute-start | bytes 393224 | tf_op jit(solution)/shard_map/ppermute | solution.py:355
  98.4 13.3 %collective-permute-start.30 = (bf16[256,256]{1,0:T(8,128)(2,1)S(1)}, bf16[256,256]{1,0:T(8,128)(2,1)S(1)}, u32[]{:S(2)}, u32[]{:S(2)}) collective-permute-start(bf16[256,256]{1,0:T(8,128)(2,1)S(1)} %get-tuple-element.95), channel_id=1, source_target_pairs={{0,14},{1,7},{2,12},{3,5},{4,10},{5,3},{6,8},{7,1},{8,22},{9,15},{... | collective-permute-start | bytes 393224 | tf_op jit(solution)/shard_map/ppermute | solution.py:355
  99.7 11.9 %collective-permute-start.31 = (bf16[256,256]{1,0:T(8,128)(2,1)S(1)}, bf16[256,256]{1,0:T(8,128)(2,1)S(1)}, u32[]{:S(2)}, u32[]{:S(2)}) collective-permute-start(bf16[256,256]{1,0:T(8,128)(2,1)S(1)} %get-tuple-element.96), channel_id=1, source_target_pairs={{0,10},{1,3},{2,8},{3,1},{4,14},{5,7},{6,12},{7,5},{8,18},{9,11},{... | collective-permute-start | bytes 393224 | tf_op jit(solution)/shard_map/ppermute | solution.py:355
  100.6 11.0 %collective-permute-start.32 = (bf16[256,256]{1,0:T(8,128)(2,1)S(1)}, bf16[256,256]{1,0:T(8,128)(2,1)S(1)}, u32[]{:S(2)}, u32[]{:S(2)}) collective-permute-start(bf16[256,256]{1,0:T(8,128)(2,1)S(1)} %get-tuple-element.97), channel_id=1, source_target_pairs={{0,8},{1,1},{2,10},{3,3},{4,12},{5,5},{6,14},{7,7},{8,16},{9,9},{1... | collective-permute-start | bytes 393224 | tf_op jit(solution)/shard_map/ppermute | solution.py:355
  104.0 9.8 %collective-permute-start.15 = (bf16[256,1024]{1,0:T(8,128)(2,1)S(1)}, bf16[256,1024]{1,0:T(8,128)(2,1)S(1)}, u32[]{:S(2)}, u32[]{:S(2)}) collective-permute-start(bf16[256,1024]{1,0:T(8,128)(2,1)S(1)} %get-tuple-element.74), channel_id=1, source_target_pairs={{0,1},{1,0},{2,3},{3,2},{4,5},{5,4},{6,7},{7,6},{8,9},{9,8},{10,11... | collective-permute-start | bytes 1572872 | tf_op jit(solution)/shard_map/ppermute | solution.py:297
  (11 other events, 49.2 us)
where the time goes:
time: 119 us; the launch traced here: 116 us
  starting transfers between devices  47.6 us (40%)
  Pallas kernels  31.7 us (27%)
  waiting for transfers between devices  27.2 us (23%)
  local copies, waits for them, and re-layouts  5.15 us (4%)
  between operations  4.59 us (4%)
    ppermute x28, starting transfers between devices, exchange(): got.append(lax.ppermute(piece, ('depth', 'z', 'core'), pairs))  39.3 us
    pallas_call x19, Pallas kernels, call(): pl.pallas_call(kernel, out_shape=tuple(outs), in_specs=[SMEM] * scalars +...  31.7 us
    ppermute x28, waiting for transfers between devices, exchange(): got.append(lax.ppermute(piece, ('depth', 'z', 'core'), pairs))  24.1 us
    ppermute x5, starting transfers between devices, other_core(): return lax.ppermute(value, 'core', [(0, 1), (1, 0)])  7.17 us
    unnamed x18, local copies, waits for them, and re-layouts  2.56 us
  transfers between devices with their start and end apart: 34, of which 12 were waited for; matrix products, arithmetic and copies ran while one was open for 1% of the time, Pallas kernels for 23%

commit v1 on v0

--- a/solution.py
+++ b/solution.py
@@ -16,6 +16,7 @@
 
 VMEM = pl.BlockSpec(memory_space=pltpu.VMEM)
 SMEM = pl.BlockSpec(memory_space=pltpu.SMEM)
+ANY = pl.BlockSpec(memory_space=pl.ANY)
 F32 = jnp.float32
 BF16 = jnp.bfloat16
 
@@ -26,66 +27,91 @@
 
 def cas_tables(length):
     positions = np.arange(length // 2, dtype=np.int64)
-
-    def table(modes):
+    quarter = length // 4
+
+    def table(low):
+        modes = np.concatenate([low, np.where(low == 0, length // 2, -low)])
         angles = (modes[:, None] * positions[None, :] % length) * (2.0 * math.pi / length)
         return ((np.cos(angles) + np.sin(angles)) / math.sqrt(length)).astype(jnp.bfloat16)
 
-    even, odd = table(2 * positions), table(2 * positions + 1)
-    return jnp.asarray(even), jnp.asarray(odd), jnp.asarray(odd.T.copy())
+    both = [table(2 * positions[:quarter] + odd) for odd in (0, 1)]
+    return [jnp.asarray(t) for one in both for t in (one, one.T.copy())]
+
+
+def wave(index, length, odd):
+    quarter = length // 4
+    low = jnp.where(index < quarter, index, index - quarter)
+    mode = 2 * low + odd
+    if not odd:
+        mode = jnp.where(index == quarter, length // 2, mode)
+    return mode.astype(F32) * (2.0 * math.pi / length)
 
 
 def dot(left, right):
     return jnp.dot(left, right, preferred_element_type=F32)
 
 
-def signed_wave(index, length):
-    signed = jnp.where(index < length // 2, index, index - length)
-    return signed.astype(F32) * (2.0 * math.pi / length)
+def fitted(function, degree):
+    nodes = 2.1 * (1.0 + np.cos(math.pi * (np.arange(64) + 0.5) / 64))
+    fit = np.polynomial.Chebyshev.fit(nodes, function(np.sqrt(nodes)), degree, domain=[0, 4.2])
+    return [float(c) for c in fit.convert(kind=np.polynomial.Polynomial).coef]
+
+
+COSINE = fitted(np.cos, 5)
+SINE = fitted(lambda angle: np.sin(angle) / angle, 5)
+
+
+def field_sign():
+    return jnp.where(lax.axis_index("core") == 1, -1.0, 1.0)
 
 
 def cos_sin(angle):
     square = angle * angle
-    cosine = jnp.full_like(square, 1.0 / math.factorial(16))
-    for order in range(14, -1, -2):
-        cosine = cosine * -square + 1.0 / math.factorial(order)
-    sine = jnp.full_like(square, 1.0 / math.factorial(15))
-    for order in range(13, 0, -2):
-        sine = sine * -square + 1.0 / math.factorial(order)
+    cosine = jnp.full_like(square, COSINE[-1])
+    for coefficient in COSINE[-2::-1]:
+        cosine = cosine * square + coefficient
+    sine = jnp.full_like(square, SINE[-1])
+    for coefficient in SINE[-2::-1]:
+        sine = sine * square + coefficient
     return cosine, sine * angle
 
 
-def factors_kernel(odd, length_y, place_ref, scalar_ref, cos_ref, sin_ref):
+def factors_kernel(odd, length_y, stage, settings_ref, cos_ref, sin_ref):
     length_x, modes = cos_ref.shape
-    half = length_x // 2
-    angular, reference_s, sign = scalar_ref[0], scalar_ref[1], scalar_ref[2]
-    step = 64
+    quarter = length_x // 4
+    angular, reference_s = settings_ref[2 * stage], settings_ref[2 * stage + 1]
+    sign = field_sign()
+    step = min(64, quarter)
     lane = lax.broadcasted_iota(jnp.int32, (step, modes), 1)
     line = lax.broadcasted_iota(jnp.int32, (step, modes), 0)
-    wave_y = signed_wave(2 * (place_ref[0] * modes + lane) + odd, length_y)
+    wave_y = wave(lax.axis_index("z") * modes + lane, length_y, odd)
     constant = (angular * reference_s) ** 2 - wave_y * wave_y
 
-    @pl.loop(0, length_x // step)
-    def _(chunk):
-        rows = pl.ds(pl.multiple_of(chunk * step, step), step)
-        place = chunk * step + line
-        kx = jnp.where(place < half, 2 * place, 2 * place - length_x + 1)
-        wave_x = signed_wave(kx, length_x)
+    def work_out(wave_x, constant):
         quad = constant - wave_x * wave_x
         root = jnp.sqrt(jnp.abs(quad)) * step_length
         travels = quad > 0.0
         cosine, sine = cos_sin(jnp.where(travels, root, 0.0))
         damping = jnp.exp(jnp.where(travels, 0.0, -root))
-        cos_ref[rows, :] = damping * cosine
-        sin_ref[rows, :] = (sign * damping) * sine
-
-
-def phase_kernel(place_ref, scalar_ref, mine_ref, other_ref, cos_ref, sin_ref):
-    angular, reference_s, sign = scalar_ref[0], scalar_ref[1], scalar_ref[2]
+        return damping * cosine, (sign * damping) * sine
+
+    for x_odd in range(2):
+        for start in range(0, quarter, step):
+            values = work_out(wave(start + line, length_x, x_odd), constant)
+            for half in range(2):
+                at = (2 * x_odd + half) * quarter + start
+                cos_ref[at : at + step, :], sin_ref[at : at + step, :] = values
+    values = work_out(wave(quarter + line[:8], length_x, 0), constant[:8])
+    cos_ref[quarter : quarter + 8, :], sin_ref[quarter : quarter + 8, :] = values
+
+
+def phase_kernel(stage, settings_ref, mine_ref, other_ref, cos_ref, sin_ref):
+    angular, reference_s = settings_ref[2 * stage], settings_ref[2 * stage + 1]
+    sign = field_sign()
     rows = mine_ref.shape[0]
     step = 8
     for index, slowness in enumerate((mine_ref, other_ref)):
-        start = (place_ref[1] ^ index) * rows
+        start = (lax.axis_index("core") ^ index) * rows
 
         @pl.loop(0, rows // step)
         def _(chunk):
@@ -123,25 +149,27 @@
             ]
 
 
-def to_modes_kernel(odd, place_ref, fields_ref, other_ref, table_ref, *refs):
+def to_modes_kernel(odd, fields_ref, other_ref, table_ref, *refs):
     outs, (folded, modes) = refs[:-2], refs[-2:]
-    rows = other_ref.shape[0] // 2
+    rows = other_ref.shape[0] // 4
     half = table_ref.shape[0]
-    core = place_ref[1]
+    core = lax.axis_index("core")
     for part in range(2):
         mine = rows_of((2 * core + part) * rows, rows)
-        for lines, source, index in ((mine, fields_ref, 0), (slice(part * rows, (part + 1) * rows), other_ref, 1)):
-            low, high = source[lines, :half], source[lines, half:]
+        for index, source in enumerate((fields_ref, other_ref)):
+            low, high = source[mine, :half], source[mine, half:]
             there = rows_of(2 * part * rows + (core ^ index) * rows, rows)
             folded[there, :] = low - high if odd else low + high
     modes[...] = dot(folded[...], table_ref[...]).astype(BF16)
-    split_modes(place_ref[0], modes, outs)
-
-
-def along_x_kernel(count, place_ref, cos_ref, sin_ref, even_ref, odd_ref, turned_ref, *refs):
+    split_modes(lax.axis_index("z"), modes, outs)
+
+
+def along_x_kernel(
+    count, cos_ref, sin_ref, even_ref, even_t_ref, odd_ref, odd_t_ref, *refs
+):
     pieces, outs = refs[:count], refs[count : 2 * count]
     held, shifted = refs[2 * count :]
-    here = place_ref[0]
+    here = lax.axis_index("z")
     rows, width = outs[0].shape
     block = width // 2
     for k, piece in zip(partners(count), pieces):
@@ -155,17 +183,17 @@
         cosine, sine = cos_ref[lines, :], sin_ref[lines, :]
         shifted[lines, :block] = (real * cosine - imag * sine).astype(BF16)
         shifted[lines, block:] = (real * sine + imag * cosine).astype(BF16)
-    first = dot(even_ref[...], shifted[:half, :])
-    second = dot(turned_ref[...], shifted[half:, :])
+    first = dot(even_t_ref[...], shifted[:half, :])
+    second = dot(odd_t_ref[...], shifted[half:, :])
     held[:half, :] = (first + second).astype(BF16)
     held[half:, :] = (first - second).astype(BF16)
     for k, out in zip(partners(count), outs):
         out[...] = held[rows_of((here ^ k) * rows, rows), :]
 
 
-def even_part_kernel(place_ref, table_ref, *refs):
+def even_part_kernel(table_ref, *refs):
     pieces, (out_ref, modes) = refs[:-2], refs[-2:]
-    join_modes(place_ref[0], pieces, modes)
+    join_modes(lax.axis_index("z"), pieces, modes)
     out_ref[...] = dot(modes[...], table_ref[...])
 
 
@@ -174,11 +202,11 @@
 
 
 def turn_around_kernel(
-    count, place_ref, cos_ref, sin_ref, top_ref, top_other_ref, even_ref, odd_ref, part_ref, *refs
+    count, cos_ref, sin_ref, top_ref, top_other_ref, even_t_ref, odd_ref, part_ref, *refs
 ):
     pieces, outs = refs[:count], refs[count : 2 * count]
     folded_ref, keep_ref, give_ref, modes, space, sums = refs[2 * count :]
-    here, core = place_ref[0], place_ref[1]
+    here, core = lax.axis_index("z"), lax.axis_index("core")
     rows = pieces[0].shape[0]
     own = rows // 2
     half = odd_ref.shape[0]
@@ -199,36 +227,36 @@
                 rows_of(part * rows + (core ^ index) * own, own), :
             ]
 
-    @pl.when(place_ref[2] == 1)
+    @pl.when(lax.axis_index("depth") == lax.axis_size("depth") - 1)
     def _():
         for part in range(2):
             space[rows_of(part * rows + core * own, own), :] = top_ref[
                 rows_of((2 * core + part) * own, own), :
             ]
             space[rows_of(part * rows + (core ^ 1) * own, own), :] = top_other_ref[
-                part * own : (part + 1) * own, :
+                rows_of((2 * core + part) * own, own), :
             ]
 
     sums[...] = space[:, :half] + space[:, half:]
     folded_ref[...] = space[:, :half] - space[:, half:]
-    modes[...] = dot(sums[...], even_ref[...]).astype(BF16)
+    modes[...] = dot(sums[...], even_t_ref[...]).astype(BF16)
     split_modes(here, modes, outs)
 
 
-def odd_modes_kernel(place_ref, folded_ref, table_ref, *refs):
+def odd_modes_kernel(folded_ref, table_ref, *refs):
     outs, modes = refs[:-1], refs[-1]
     modes[...] = dot(folded_ref[...], table_ref[...]).astype(BF16)
-    split_modes(place_ref[0], modes, outs)
-
-
-def half_space_kernel(index, place_ref, cos_ref, sin_ref, odd_ref, part_ref, *refs):
+    split_modes(lax.axis_index("z"), modes, outs)
+
+
+def half_space_kernel(index, cos_ref, sin_ref, odd_ref, part_ref, *refs):
     pieces, (out_ref, modes) = refs[:-2], refs[-2:]
     rows = pieces[0].shape[0]
     own = rows // 2
     half = odd_ref.shape[0]
-    offset = (place_ref[1] ^ index) * own
+    offset = (lax.axis_index("core") ^ index) * own
     lines = rows_of(offset, own)
-    join_modes(place_ref[0], pieces, modes, lines)
+    join_modes(lax.axis_index("z"), pieces, modes, lines)
     step = 256
     for start in range(0, half, step):
         columns = slice(start, start + step)
@@ -245,10 +273,10 @@
             )
 
 
-def finish_kernel(place_ref, first_ref, first_other_ref, keep_ref, got_ref, fields_ref, image_ref):
+def finish_kernel(first_ref, first_other_ref, keep_ref, got_ref, fields_ref, image_ref):
     rows = keep_ref.shape[0]
     own = rows // 2
-    core = place_ref[1]
+    core = lax.axis_index("core")
     fields_ref[rows_of(core * rows, rows), :] = keep_ref[...]
     fields_ref[rows_of((core ^ 1) * rows, rows), :] = got_ref[...]
     step = 16
@@ -262,19 +290,23 @@
         image_ref[start : start + step, :] = total
 
 
-def call(kernel, operands, outs, scratch=(), flops=0, name=None, scalars=1):
+def after(count, kernel, *refs):
+    return kernel(*refs[count:])
+
+
+def call(kernel, operands, outs, scratch=(), flops=0, name=None, scalars=0, behind=()):
     moved = sum(math.prod(a.shape) * a.dtype.itemsize for a in operands)
     moved += sum(math.prod(a.shape) * a.dtype.itemsize for a in outs)
     return pl.pallas_call(
-        kernel,
+        functools.partial(after, len(behind), kernel),
         out_shape=tuple(outs),
-        in_specs=[SMEM] * scalars + [VMEM] * (len(operands) - scalars),
+        in_specs=[ANY] * len(behind) + [SMEM] * scalars + [VMEM] * (len(operands) - scalars),
         out_specs=tuple(VMEM for _ in outs),
         scratch_shapes=list(scratch),
         compiler_params=pltpu.CompilerParams(vmem_limit_bytes=24 * 1024 * 1024),
         cost_estimate=pl.CostEstimate(flops=flops, bytes_accessed=moved, transcendentals=0),
         name=name,
-    )(*operands)
+    )(*behind, *operands)
 
 
 def per_device(flight_fields, top_fields, slowness, ref_slowness, flight_blocks, top_block):
@@ -284,11 +316,9 @@
     length_x = rows * chips
     half = length_y // 2
     block = half // chips
-    even_x, odd_x, turned_x = cas_tables(length_x)
-    even_y, odd_y, turned_y = cas_tables(length_y)
-    depth, chip, core = (lax.axis_index(name) for name in ("depth", "z", "core"))
-    place = jnp.stack([chip, core, (depth == slabs - 1).astype(jnp.int32)]).astype(jnp.int32)
-    sign = 1.0 - 2.0 * core.astype(F32)
+    cells = own * length_y
+    tables_x = cas_tables(length_x)
+    even_y, even_y_t, odd_y, odd_y_t = tables_x if length_x == length_y else cas_tables(length_y)
 
     def of(shape, dtype=BF16):
         return jax.ShapeDtypeStruct(shape, dtype)
@@ -296,40 +326,37 @@
     def other_core(value):
         return lax.ppermute(value, "core", [(0, 1), (1, 0)])
 
-    def scalars(block_id, reference_s):
-        angular = omega_top * (block_id.astype(F32) + 1.0) / NFREQ
-        return jnp.stack([angular, reference_s, sign])
-
-    def above(slab):
-        return jnp.where(slab == 0, top_block[0], flight_blocks[jnp.maximum(slab - 1, 0)])
-
-    def other_field(fields):
-        taken = lax.dynamic_index_in_dim(fields, 1 - core, 0, keepdims=False)
-        return other_core(taken.reshape(rows, length_y))
-
     fields = flight_fields.reshape(2 * rows, length_y)
-    fields_other = other_field(flight_fields[0])
-
-    below = lax.ppermute(
-        ref_slowness, "depth", [((d + 1) % slabs, d) for d in range(slabs)]
-    )
-    target = (depth + 1 - core) % slabs
-    first_scalars = scalars(flight_blocks[depth], ref_slowness[0])
-    target_scalars = scalars(above(target), jnp.where(core == 1, ref_slowness[0], below[0]))
-    second_scalars = scalars(above(depth), ref_slowness[0])
-
-    cells = own * length_y
-
-    def factors(scalar, odd):
+    top = top_fields.reshape(2 * rows, length_y)
+    mine = slowness[0]
+    fields_other, top_other, other = other_core(fields), other_core(top), other_core(mine)
+    below = lax.ppermute(ref_slowness, "depth", [((d + 1) % slabs, d) for d in range(slabs)])
+
+    depth = lax.axis_index("depth")
+
+    def angular(block_id):
+        return omega_top * (block_id.astype(F32) + 1.0) / NFREQ
+
+    second = jnp.where(depth == 0, top_block[0], flight_blocks[jnp.maximum(depth - 1, 0)])
+    odd_second = jnp.where(depth == slabs - 1, top_block[0], flight_blocks[depth])
+    settings = jnp.stack([
+        angular(flight_blocks[depth]), ref_slowness[0],
+        angular(second), ref_slowness[0],
+        angular(odd_second), below[0],
+    ])
+
+    def factors(stage, odd, behind):
         return call(
-            functools.partial(factors_kernel, odd, length_y), (place, scalar),
-            [of((length_x, block), F32)] * 2, flops=400 * cells, name="factors", scalars=2,
+            functools.partial(factors_kernel, odd, length_y, stage), (settings,),
+            [of((length_x, block), F32)] * 2, flops=400 * cells, name="factors", scalars=1,
+            behind=behind,
         )
 
-    def phases(scalar):
+    def phases(stage, behind):
         return call(
-            phase_kernel, (place, scalar, slowness[0], slowness_other),
-            [of((rows, length_y), F32)] * 2, flops=800 * cells, name="phases", scalars=2,
+            functools.partial(phase_kernel, stage), (settings, mine, other),
+            [of((rows, length_y), F32)] * 2, flops=800 * cells, name="phases", scalars=1,
+            behind=behind,
         )
 
     pieces_of = [of((rows, 2 * block))] * chips
@@ -338,77 +365,73 @@
     flops = 2 * 2 * rows * half * half
     x_part = pltpu.VMEM((length_x, 2 * block), BF16)
 
-    def exchange(pieces, moving=None):
+    def exchange(pieces, down=0):
         got = []
         for k, piece in zip(partners(chips), pieces):
-            if k == 0 and moving is None:
-                got.append(piece)
-                continue
-            pairs = []
-            for d in range(slabs):
-                for z in range(chips):
-                    for c in range(2):
-                        there = (d + 1) % slabs if c == moving else d
-                        pairs.append(
-                            ((d * chips + z) * 2 + c, (there * chips + (z ^ k)) * 2 + c)
-                        )
-            got.append(lax.ppermute(piece, ("depth", "z", "core"), pairs))
+            if down:
+                pairs = [
+                    (d * chips + z, (d + down) % slabs * chips + (z ^ k))
+                    for d in range(slabs)
+                    for z in range(chips)
+                ]
+                got.append(lax.ppermute(piece, ("depth", "z"), pairs))
+            else:
+                pairs = [(z, z ^ k) for z in range(chips)]
+                got.append(lax.ppermute(piece, "z", pairs) if k else piece)
         return got
 
-    def to_modes(odd):
+    def to_modes(odd, behind=()):
         return call(
             functools.partial(to_modes_kernel, odd),
-            (place, fields, fields_other, turned_y if odd else even_y),
-            pieces_of, [part, part], flops, "to_modes",
+            (fields, fields_other, odd_y_t if odd else even_y_t),
+            pieces_of, [part, part], flops, "to_modes", behind=behind,
         )
 
-    def along_x(pieces, factor):
+    def along_x(pieces, factor, behind=()):
         return call(
-            functools.partial(along_x_kernel, chips),
-            (place, *factor, even_x, odd_x, turned_x, *pieces),
-            pieces_of, [x_part, x_part], 2 * flops, "along_x",
+            functools.partial(along_x_kernel, chips), (*factor, *tables_x, *pieces),
+            pieces_of, [x_part, x_part], 2 * flops, "along_x", behind=behind,
         )
 
     def even_part(pieces):
         return call(
-            even_part_kernel, (place, even_y, *pieces), [of(lines, F32)], [part], flops, "even_part"
+            even_part_kernel, (even_y, *pieces), [of(lines, F32)], [part], flops, "even_part"
         )[0]
 
-    evens = exchange(to_modes(0))
-    odds = exchange(to_modes(1))
-    slowness_other = other_core(slowness[0])
-    top_other = other_field(top_fields)
-    evens = exchange(along_x(evens, factors(first_scalars, 0)))
-    odds = exchange(along_x(odds, factors(first_scalars, 1)))
+    evens = to_modes(0)
+    odds = to_modes(1, (top_other, other, below))
+    ready = (odds[-1],)
+    even_factors, odd_factors = factors(0, 0, ready), factors(0, 1, ready)
+    first_phases = phases(0, ready)
+    evens, odds = exchange(evens), exchange(odds)
+    evens = exchange(along_x(evens, even_factors, (odd_factors[0], first_phases[0])))
+    odds = exchange(along_x(odds, odd_factors))
     *evens, folded, first_keep, first_give = call(
         functools.partial(turn_around_kernel, chips),
-        (
-            place, *phases(first_scalars), top_fields.reshape(2 * rows, length_y), top_other,
-            even_y, odd_y, even_part(evens), *odds,
-        ),
+        (*first_phases, top, top_other, even_y_t, odd_y, even_part(evens), *odds),
         pieces_of + [of(lines)] + [of((rows, length_y))] * 2,
         [part, pltpu.VMEM((2 * rows, length_y), BF16), part], 2 * flops, "turn_around",
     )
-    evens = exchange(evens, 1)
-    odds = exchange(
-        call(odd_modes_kernel, (place, folded, turned_y), pieces_of, [part], flops, "odd_modes"), 1
-    )
+    odds = call(odd_modes_kernel, (folded, odd_y_t), pieces_of, [part], flops, "odd_modes")
+    ready = (odds[-1],)
+    even_factors, odd_factors = factors(1, 0, ready), factors(2, 1, ready)
+    second_phases = phases(1, ready)
+    evens, odds = exchange(evens, 1), exchange(odds)
     first_got = other_core(first_give)
-    evens = exchange(along_x(evens, factors(target_scalars, 0)), 0)
-    odds = exchange(along_x(odds, factors(target_scalars, 1)), 0)
-    second_phases = phases(second_scalars)
+    evens = exchange(along_x(evens, even_factors, (odd_factors[0], second_phases[0])))
+    odds = exchange(along_x(odds, odd_factors), 1)
     first_part = even_part(evens)
     give, keep = [
         call(
             functools.partial(half_space_kernel, index),
-            (place, *second_phases, odd_y, first_part, *odds),
+            (*second_phases, odd_y, first_part, *odds),
             [of((rows, length_y))], [pltpu.VMEM((rows, half), BF16)], flops // 2, "half_space",
         )[0]
         for index in (1, 0)
     ]
     got = other_core(give)
     fields, image = call(
-        finish_kernel, (place, first_keep, first_got, keep, got),
+        finish_kernel, (first_keep, first_got, keep, got),
         [of((2 * rows, length_y)), of((own, length_y), F32)], flops=8 * cells, name="finish",
     )
     return image[None], fields.reshape(flight_fields.shape)

time: 119 us -> 116 us (0.975)
  waiting for transfers between devices: 27.2 us -> 38.3 us
  Pallas kernels: 31.7 us -> 21.1 us
    ppermute x28 -> x26, waiting for transfers between devices: 24.1 us -> 36.7 us  [the longest x18 24 us: exchange(): got.append(lax.ppermute(piece, 'z', pairs) if k else piece)]
    pallas_call x19, Pallas kernels: 31.7 us -> 21.1 us  [call(): pl.pallas_call(functools.partial(after, len(behind), kernel), out_shape=t...]
    ppermute x28 -> x26, starting transfers between devices: 39.3 us -> 37.2 us  [the longest x18 20.5 us: exchange(): got.append(lax.ppermute(piece, 'z', pairs) if k else piece)]
    dynamic_slice x3 -> x1, local copies, waits for them, and re-layouts: 2.59 us -> 0.65 us  [per_device(): flight_blocks[jnp.maximum(depth - 1, 0)]]
    unnamed x18 -> x20, local copies, waits for them, and re-layouts: 2.56 us -> 2.95 us
  transfers between devices with their start and end apart: 34 -> 32, of which waited for: 12 -> 12; matrix products, arithmetic and copies ran while one was open for 1% -> 1% of each run, Pallas kernels for 23% -> 15%
where the time goes in v1:
time: 116 us; the launch traced here: 115 us
  starting transfers between devices  46.9 us (40%)
  waiting for transfers between devices  38.3 us (33%)
  Pallas kernels  21.1 us (18%)
  local copies, waits for them, and re-layouts  4.3 us (4%)
  between operations  3.96 us (3%)
    ppermute x18, waiting for transfers between devices, exchange(): got.append(lax.ppermute(piece, 'z', pairs) if k else piece)  24 us
    pallas_call x19, Pallas kernels, call(): pl.pallas_call(functools.partial(after, len(behind), kernel), out_shape=t...  21.1 us
    ppermute x18, starting transfers between devices, exchange(): got.append(lax.ppermute(piece, 'z', pairs) if k else piece)  20.5 us
    ppermute x8, starting transfers between devices, exchange(): got.append(lax.ppermute(piece, ('depth', 'z'), pairs))  16.7 us
    ppermute x8, waiting for transfers between devices, exchange(): got.append(lax.ppermute(piece, ('depth', 'z'), pairs))  12.8 us
    ppermute x5, starting transfers between devices, other_core(): return lax.ppermute(value, 'core', [(0, 1), (1, 0)])  7.49 us
    unnamed x20, local copies, waits for them, and re-layouts  2.95 us
  transfers between devices with their start and end apart: 32, of which 12 were waited for; matrix products, arithmetic and copies ran while one was open for 1% of the time, Pallas kernels for 15%

profile of v1, /device:TPU:9, one launch (start us, length us, event | category | flops | bytes accessed | tf_op | source)
XLA Modules:
  0.0 114.5 jit_solution(9536005634610345119)
XLA Ops:
  1.9 2.2 %collective-permute-start.2 = (f32[1]{0:T(128)}, f32[1]{0:T(128)}, u32[]{:S(2)}, u32[]{:S(2)}) collective-permute-start(f32[1]{0:T(128)} %param.13), channel_id=1, source_target_pairs={{8,0},{16,8},{24,16},{0,24},{9,1},{17,9},{25,17},{1,25},{10,2},{18... | collective-permute-start | bytes 20 | tf_op jit(solution)/shard_map/ppermute | solution.py:333
  6.9 1.3 %to_modes.3 = (bf16[256,256]{1,0:T(8,128)(2,1)}, bf16[256,256]{1,0:T(8,128)(2,1)}, bf16[256,256]{1,0:T(8,128)(2,1)}, bf16[256,256]{1,0:T(8,128)(2,1)S(1)}) custom-call(bf16[512,1024]{1,0:T(8,128)(2,1)S(1)} %bitcast.14, bf16[512,1024]{1,0:T(8,128)(2,1)S(1)} %collective-permute-done.3.refs_4_.refs_1_, bf16[512,512]{1,0:T(8,128)(2,1)S(1)} %copy-done.3), custom_call_target="tpu_custom_call" | custom-call | flops 268435456 | bytes 3145728 | tf_op jit(solution)/shard_map/to_modes/pallas_call | solution.py:300
  8.1 2.3 %collective-permute-start.4 = (bf16[256,256]{1,0:T(8,128)(2,1)}, bf16[256,256]{1,0:T(8,128)(2,1)S(1)}, u32[]{:S(2)}, u32[]{:S(2)}) collective-permute-start(bf16[256,256]{1,0:T(8,128)(2,1)} %get-tuple-element.57), channel_id=1, source_target_pairs={{0,4},{2,6},{4,0},{6,2},{1,5},{3,7},{5,1},{7,3},{8,12},{10,14},{12... | collective-permute-start | bytes 393224 | tf_op jit(solution)/shard_map/ppermute | solution.py:380
  10.5 1.2 %collective-permute-start.6 = (bf16[256,256]{1,0:T(8,128)(2,1)}, bf16[256,256]{1,0:T(8,128)(2,1)}, u32[]{:S(2)}, u32[]{:S(2)}) collective-permute-start(bf16[256,256]{1,0:T(8,128)(2,1)} %get-tuple-element.59), channel_id=1, source_target_pairs={{0,2},{2,0},{4,6},{6,4},{1,3},{3,1},{5,7},{7,5},{8,10},{10,8},{12,... | collective-permute-start | bytes 393224 | tf_op jit(solution)/shard_map/ppermute | solution.py:380
  16.8 1.3 %to_modes.2 = (bf16[256,256]{1,0:T(8,128)(2,1)S(1)}, bf16[256,256]{1,0:T(8,128)(2,1)S(1)}, bf16[256,256]{1,0:T(8,128)(2,1)S(1)}, bf16[256,256]{1,0:T(8,128)(2,1)S(1)}) custom-call(bf16[512,1024]{1,0:T(8,128)(2,1)} %collective-permute-done.refs_0_.refs_3_, f32[128,1024]{1,0:T(8,128)S(1)} %collective-permute-done.1.refs_1_.refs_3_, ...), custom_call_target="tpu_custom_call" | custom-call | flops 268435456 | bytes 3145728 | tf_op jit(solution)/shard_map/to_modes/pallas_call | solution.py:300
  18.1 1.5 %collective-permute-start.10 = (bf16[256,256]{1,0:T(8,128)(2,1)S(1)}, bf16[256,256]{1,0:T(8,128)(2,1)S(1)}, u32[]{:S(2)}, u32[]{:S(2)}) collective-permute-start(bf16[256,256]{1,0:T(8,128)(2,1)S(1)} %get-tuple-element.66), channel_id=1, source_target_pairs={{0,4},{2,6},{4,0},{6,2},{1,5},{3,7},{5,1},{7,3},{8,12},{10,14},{12... | collective-permute-start | bytes 393224 | tf_op jit(solution)/shard_map/ppermute | solution.py:380
  21.6 1.7 %phases.2 = (f32[256,1024]{1,0:T(8,128)S(1)}, f32[256,1024]{1,0:T(8,128)S(1)}) custom-call(bf16[256,256]{1,0:T(8,128)(2,1)S(1)} %get-tuple-element.51.refs_0_.refs_9_, f32[6]{0:T(128)S(1)} %stack.15.refs_1_, f32[128,1024]{1,0:T(8,128)S(1)} %bitcast.17, f32[128,1024]{1,0:T(8,128)S(1)} %collective-permute-done.1.refs_1_.refs_3_), custom_call_target="tpu_custom_call" | custom-call | flops 104857600 | bytes 3145752 | tf_op jit(solution)/shard_map/phases/pallas_call | solution.py:300
  23.3 2.2 %collective-permute-start.12 = (bf16[256,256]{1,0:T(8,128)(2,1)S(1)}, bf16[256,256]{1,0:T(8,128)(2,1)S(1)}, u32[]{:S(2)}, u32[]{:S(2)}) collective-permute-start(bf16[256,256]{1,0:T(8,128)(2,1)S(1)} %get-tuple-element.68), channel_id=1, source_target_pairs={{0,2},{2,0},{4,6},{6,4},{1,3},{3,1},{5,7},{7,5},{8,10},{10,8},{12,... | collective-permute-start | bytes 393224 | tf_op jit(solution)/shard_map/ppermute | solution.py:380
  25.5 2.4 %collective-permute-done.5.refs_9_ = bf16[256,256]{1,0:T(8,128)(2,1)S(1)} collective-permute-done((bf16[256,256]{1,0:T(8,128)(2,1)}, bf16[256,256]{1,0:T(8,128)(2,1)S(1)}, u32[]{:S(2)}, u32[]{:S(2)}) %collective-permute-start.5) | collective-permute-done | bytes 131104 | tf_op jit(solution)/shard_map/ppermute | solution.py:380
  27.9 1.9 %along_x.4 = (bf16[256,256]{1,0:T(8,128)(2,1)S(1)}, bf16[256,256]{1,0:T(8,128)(2,1)S(1)}, bf16[256,256]{1,0:T(8,128)(2,1)S(1)}, bf16[256,256]{1,0:T(8,128)(2,1)S(1)}) custom-call(f32[1024,128]{1,0:T(8,128)S(1)} %get-tuple-element.54.refs_0_, f32[256,1024]{1,0:T(8,128)S(1)} %get-tuple-element.52.refs_1_.refs_0_, f32[1024,128]{1,0:T(8,128)S(1)} %get-tuple-element.55.refs_2_, ...), custom_call_target="tpu_custom_call" | custom-call | flops 536870912 | bytes 4194304 | tf_op jit(solution)/shard_map/along_x/pallas_call | solution.py:300
  29.8 2.3 %collective-permute-start.8 = (bf16[256,256]{1,0:T(8,128)(2,1)S(1)}, bf16[256,256]{1,0:T(8,128)(2,1)S(1)}, u32[]{:S(2)}, u32[]{:S(2)}) collective-permute-start(bf16[256,256]{1,0:T(8,128)(2,1)S(1)} %get-tuple-element.62), channel_id=1, source_target_pairs={{0,6},{2,4},{4,2},{6,0},{1,7},{3,5},{5,3},{7,1},{8,14},{10,12},{12... | collective-permute-start | bytes 393224 | tf_op jit(solution)/shard_map/ppermute | solution.py:380
  32.1 1.2 %collective-permute-start.9 = (bf16[256,256]{1,0:T(8,128)(2,1)S(1)}, bf16[256,256]{1,0:T(8,128)(2,1)S(1)}, u32[]{:S(2)}, u32[]{:S(2)}) collective-permute-start(bf16[256,256]{1,0:T(8,128)(2,1)S(1)} %get-tuple-element.63), channel_id=1, source_target_pairs={{0,2},{2,0},{4,6},{6,4},{1,3},{3,1},{5,7},{7,5},{8,10},{10,8},{12,... | collective-permute-start | bytes 393224 | tf_op jit(solution)/shard_map/ppermute | solution.py:380
  34.5 1.9 %collective-permute-start.13 = (bf16[256,256]{1,0:T(8,128)(2,1)S(1)}, bf16[256,256]{1,0:T(8,128)(2,1)S(1)}, u32[]{:S(2)}, u32[]{:S(2)}) collective-permute-start(bf16[256,256]{1,0:T(8,128)(2,1)S(1)} %get-tuple-element.69), channel_id=1, source_target_pairs={{0,4},{2,6},{4,0},{6,2},{1,5},{3,7},{5,1},{7,3},{8,12},{10,14},{12... | collective-permute-start | bytes 393224 | tf_op jit(solution)/shard_map/ppermute | solution.py:380
  36.9 5.7 %collective-permute-done.7.refs_1_ = bf16[256,256]{1,0:T(8,128)(2,1)S(1)} collective-permute-done((bf16[256,256]{1,0:T(8,128)(2,1)S(1)}, bf16[256,256]{1,0:T(8,128)(2,1)S(1)}, u32[]{:S(2)}, u32[]{:S(2)}) %collective-permute-start.7) | collective-permute-done | bytes 131104 | tf_op jit(solution)/shard_map/ppermute | solution.py:380
  42.5 1.4 %collective-permute-start.15 = (bf16[256,256]{1,0:T(8,128)(2,1)S(1)}, bf16[256,256]{1,0:T(8,128)(2,1)S(1)}, u32[]{:S(2)}, u32[]{:S(2)}) collective-permute-start(bf16[256,256]{1,0:T(8,128)(2,1)S(1)} %get-tuple-element.71), channel_id=1, source_target_pairs={{0,2},{2,0},{4,6},{6,4},{1,3},{3,1},{5,7},{7,5},{8,10},{10,8},{12,... | collective-permute-start | bytes 393224 | tf_op jit(solution)/shard_map/ppermute | solution.py:380
  43.9 6.5 %collective-permute-done.8.refs_2_ = bf16[256,256]{1,0:T(8,128)(2,1)S(1)} collective-permute-done((bf16[256,256]{1,0:T(8,128)(2,1)S(1)}, bf16[256,256]{1,0:T(8,128)(2,1)S(1)}, u32[]{:S(2)}, u32[]{:S(2)}) %collective-permute-start.8) | collective-permute-done | bytes 131104 | tf_op jit(solution)/shard_map/ppermute | solution.py:380
  50.9 2.3 %collective-permute-done.13.refs_7_ = bf16[256,256]{1,0:T(8,128)(2,1)S(1)} collective-permute-done((bf16[256,256]{1,0:T(8,128)(2,1)S(1)}, bf16[256,256]{1,0:T(8,128)(2,1)S(1)}, u32[]{:S(2)}, u32[]{:S(2)}) %collective-permute-start.13) | collective-permute-done | bytes 131104 | tf_op jit(solution)/shard_map/ppermute | solution.py:380
  53.3 2.8 %collective-permute-done.14.refs_8_ = bf16[256,256]{1,0:T(8,128)(2,1)S(1)} collective-permute-done((bf16[256,256]{1,0:T(8,128)(2,1)S(1)}, bf16[256,256]{1,0:T(8,128)(2,1)S(1)}, u32[]{:S(2)}, u32[]{:S(2)}) %collective-permute-start.14) | collective-permute-done | bytes 131104 | tf_op jit(solution)/shard_map/ppermute | solution.py:380
  56.1 2.7 %turn_around.1 = (bf16[256,256]{1,0:T(8,128)(2,1)S(1)}, bf16[256,256]{1,0:T(8,128)(2,1)S(1)}, bf16[256,256]{1,0:T(8,128)(2,1)S(1)}, bf16[256,256]{1,0:T(8,128)(2...) custom-call(f32[256,1024]{1,0:T(8,128)S(1)} %get-tuple-element.52.refs_1_.refs_0, ...), custom_call_target="tpu_custom_call" | custom-call | flops 536870912 | bytes 8912896 | tf_op jit(solution)/shard_map/turn_around/pallas_call | solution.py:300
  58.8 1.3 %collective-permute-start.17 = (bf16[256,256]{1,0:T(8,128)(2,1)S(1)}, bf16[256,256]{1,0:T(8,128)(2,1)S(1)}, u32[]{:S(2)}, u32[]{:S(2)}) collective-permute-start(bf16[256,256]{1,0:T(8,128)(2,1)S(1)} %get-tuple-element.82), channel_id=1, source_target_pairs={{0,12},{2,14},{4,8},{6,10},{8,20},{10,22},{12,16},{14,18},{16,28},... | collective-permute-start | bytes 393224 | tf_op jit(solution)/shard_map/ppermute | solution.py:377
  60.1 2.0 %collective-permute-start.18 = (bf16[256,256]{1,0:T(8,128)(2,1)S(1)}, bf16[256,256]{1,0:T(8,128)(2,1)S(1)}, u32[]{:S(2)}, u32[]{:S(2)}) collective-permute-start(bf16[256,256]{1,0:T(8,128)(2,1)S(1)} %get-tuple-element.83), channel_id=1, source_target_pairs={{0,14},{2,12},{4,10},{6,8},{8,22},{10,20},{12,18},{14,16},{16,30},... | collective-permute-start | bytes 393224 | tf_op jit(solution)/shard_map/ppermute | solution.py:377
  62.0 3.2 %collective-permute-start.19 = (bf16[256,256]{1,0:T(8,128)(2,1)S(1)}, bf16[256,256]{1,0:T(8,128)(2,1)S(1)}, u32[]{:S(2)}, u32[]{:S(2)}) collective-permute-start(bf16[256,256]{1,0:T(8,128)(2,1)S(1)} %get-tuple-element.84), channel_id=1, source_target_pairs={{0,10},{2,8},{4,14},{6,12},{8,18},{10,16},{12,22},{14,20},{16,26},... | collective-permute-start | bytes 393224 | tf_op jit(solution)/shard_map/ppermute | solution.py:377
  66.0 2.2 %collective-permute-start.24 = (bf16[256,256]{1,0:T(8,128)(2,1)S(1)}, bf16[256,256]{1,0:T(8,128)(2,1)S(1)}, u32[]{:S(2)}, u32[]{:S(2)}) collective-permute-start(bf16[256,256]{1,0:T(8,128)(2,1)S(1)} %get-tuple-element.91), channel_id=1, source_target_pairs={{0,4},{2,6},{4,0},{6,2},{1,5},{3,7},{5,1},{7,3},{8,12},{10,14},{12... | collective-permute-start | bytes 393224 | tf_op jit(solution)/shard_map/ppermute | solution.py:380
  70.1 1.7 %phases.3 = (f32[256,1024]{1,0:T(8,128)S(1)}, f32[256,1024]{1,0:T(8,128)S(1)}) custom-call(bf16[256,256]{1,0:T(8,128)(2,1)S(1)} %get-tuple-element.76.refs_0_.refs_9_, f32[6]{0:T(128)S(1)} %stack.15.refs_1_, f32[128,1024]{1,0:T(8,128)S(1)} %bitcast.18, f32[128,1024]{1,0:T(8,128)S(1)} %collective-permute-done.1.refs_1_.refs_3_), custom_call_target="tpu_custom_call" | custom-call | flops 104857600 | bytes 3145752 | tf_op jit(solution)/shard_map/phases/pallas_call | solution.py:300
  72.0 6.3 %collective-permute-done.18.refs_9_ = bf16[256,256]{1,0:T(8,128)(2,1)S(1)} collective-permute-done((bf16[256,256]{1,0:T(8,128)(2,1)S(1)}, bf16[256,256]{1,0:T(8,128)(2,1)S(1)}, u32[]{:S(2)}, u32[]{:S(2)}) %collective-permute-start.18) | collective-permute-done | bytes 131104 | tf_op jit(solution)/shard_map/ppermute | solution.py:377
  79.4 2.6 %collective-permute-start.22 = (bf16[256,256]{1,0:T(8,128)(2,1)S(1)}, bf16[256,256]{1,0:T(8,128)(2,1)S(1)}, u32[]{:S(2)}, u32[]{:S(2)}) collective-permute-start(bf16[256,256]{1,0:T(8,128)(2,1)S(1)} %get-tuple-element.87), channel_id=1, source_target_pairs={{0,6},{2,4},{4,2},{6,0},{1,7},{3,5},{5,3},{7,1},{8,14},{10,12},{12... | collective-permute-start | bytes 393224 | tf_op jit(solution)/shard_map/ppermute | solution.py:380
  82.9 4.1 %collective-permute-done.25.refs_7_ = bf16[256,256]{1,0:T(8,128)(2,1)S(1)} collective-permute-done((bf16[256,256]{1,0:T(8,128)(2,1)S(1)}, bf16[256,256]{1,0:T(8,128)(2,1)S(1)}, u32[]{:S(2)}, u32[]{:S(2)}) %collective-permute-start.25) | collective-permute-done | bytes 131104 | tf_op jit(solution)/shard_map/ppermute | solution.py:380
  88.1 3.9 %collective-permute-start.28 = (bf16[256,256]{1,0:T(8,128)(2,1)S(1)}, bf16[256,256]{1,0:T(8,128)(2,1)S(1)}, u32[]{:S(2)}, u32[]{:S(2)}) collective-permute-start(bf16[256,256]{1,0:T(8,128)(2,1)S(1)} %get-tuple-element.95), channel_id=1, source_target_pairs={{0,14},{2,12},{4,10},{6,8},{8,22},{10,20},{12,18},{14,16},{16,30},... | collective-permute-start | bytes 393224 | tf_op jit(solution)/shard_map/ppermute | solution.py:377
  92.0 6.0 %collective-permute-start.29 = (bf16[256,256]{1,0:T(8,128)(2,1)S(1)}, bf16[256,256]{1,0:T(8,128)(2,1)S(1)}, u32[]{:S(2)}, u32[]{:S(2)}) collective-permute-start(bf16[256,256]{1,0:T(8,128)(2,1)S(1)} %get-tuple-element.96), channel_id=1, source_target_pairs={{0,10},{2,8},{4,14},{6,12},{8,18},{10,16},{12,22},{14,20},{16,26},... | collective-permute-start | bytes 393224 | tf_op jit(solution)/shard_map/ppermute | solution.py:377
  98.1 5.1 %collective-permute-start.16 = (bf16[256,1024]{1,0:T(8,128)(2,1)S(1)}, bf16[256,1024]{1,0:T(8,128)(2,1)S(1)}, u32[]{:S(2)}, u32[]{:S(2)}) collective-permute-start(bf16[256,1024]{1,0:T(8,128)(2,1)S(1)} %get-tuple-element.74), channel_id=1, source_target_pairs={{0,1},{1,0},{2,3},{3,2},{4,5},{5,4},{6,7},{7,6},{8,9},{9,8},{10,11... | collective-permute-start | bytes 1572872 | tf_op jit(solution)/shard_map/ppermute | solution.py:327
  103.8 5.6 %collective-permute-done.28.refs_5_ = bf16[256,256]{1,0:T(8,128)(2,1)S(1)} collective-permute-done((bf16[256,256]{1,0:T(8,128)(2,1)S(1)}, bf16[256,256]{1,0:T(8,128)(2,1)S(1)}, u32[]{:S(2)}, u32[]{:S(2)}) %collective-permute-start.28) | collective-permute-done | bytes 131104 | tf_op jit(solution)/shard_map/ppermute | solution.py:377
  113.3 1.3 %finish.1 = (bf16[512,1024]{1,0:T(8,128)(2,1)}, f32[128,1024]{1,0:T(8,128)}) custom-call(bf16[256,1024]{1,0:T(8,128)(2,1)S(1)} %get-tuple-element.73.refs_0_, bf16[256,1024]{1,0:T(8,128)(2,1)S(1)} %collective-permute-done.16.refs_1_, bf16[256,1024]{1,0:T(8,128)(2,1)S(1)} %half_space.2.refs_2_, bf16[256,1024]{1,0:T(8,128)(2,1)S(1)} %collective-permute-done.31.refs_3_), custom_call_target="tpu_custom_call" | custom-call | flops 1048576 | bytes 3670016 | tf_op jit(solution)/shard_map/finish/pallas_call | solution.py:300
  (73 shorter events, 20.7 us)
Async XLA Ops:
  0.6 4.0 %collective-permute-start.3 = (bf16[512,1024]{1,0:T(8,128)(2,1)}, bf16[512,1024]{1,0:T(8,128)(2,1)S(1)}, u32[]{:S(2)}, u32[]{:S(2)}) collective-permute-start(bf16[512,1024]{1,0:T(8,128)(2,1)} %bitcast.13), channel_id=1, source_target_pairs={{0,1},{1,0},{2,3},{3,2},{4,5},{5,4},{6,7},{7,6},{8,9},{9,8},{10,11... | collective-permute-start | bytes 3145736 | tf_op jit(solution)/shard_map/ppermute | solution.py:327
  1.4 15.4 %collective-permute-start = (bf16[512,1024]{1,0:T(8,128)(2,1)}, bf16[512,1024]{1,0:T(8,128)(2,1)}, u32[]{:S(2)}, u32[]{:S(2)}) collective-permute-start(bf16[512,1024]{1,0:T(8,128)(2,1)} %bitcast.19), channel_id=1, source_target_pairs={{0,1},{1,0},{2,3},{3,2},{4,5},{5,4},{6,7},{7,6},{8,9},{9,8},{10,11... | collective-permute-start | bytes 3145736 | tf_op jit(solution)/shard_map/ppermute | solution.py:327
  1.4 15.3 %collective-permute-start.1 = (f32[128,1024]{1,0:T(8,128)}, f32[128,1024]{1,0:T(8,128)S(1)}, u32[]{:S(2)}, u32[]{:S(2)}) collective-permute-start(f32[128,1024]{1,0:T(8,128)} %bitcast.16), channel_id=1, source_target_pairs={{0,1},{1,0},{2,3},{3,2},{4,5},{5,4},{6,7},{7,6},{8,9},{9,8},{10,11... | collective-permute-start | bytes 1572872 | tf_op jit(solution)/shard_map/ppermute | solution.py:327
  1.9 8.6 %collective-permute-start.2 = (f32[1]{0:T(128)}, f32[1]{0:T(128)}, u32[]{:S(2)}, u32[]{:S(2)}) collective-permute-start(f32[1]{0:T(128)} %param.13), channel_id=1, source_target_pairs={{8,0},{16,8},{24,16},{0,24},{9,1},{17,9},{25,17},{1,25},{10,2},{18... | collective-permute-start | bytes 20 | tf_op jit(solution)/shard_map/ppermute | solution.py:333
  8.1 15.2 %collective-permute-start.4 = (bf16[256,256]{1,0:T(8,128)(2,1)}, bf16[256,256]{1,0:T(8,128)(2,1)S(1)}, u32[]{:S(2)}, u32[]{:S(2)}) collective-permute-start(bf16[256,256]{1,0:T(8,128)(2,1)} %get-tuple-element.57), channel_id=1, source_target_pairs={{0,4},{2,6},{4,0},{6,2},{1,5},{3,7},{5,1},{7,3},{8,12},{10,14},{12... | collective-permute-start | bytes 393224 | tf_op jit(solution)/shard_map/ppermute | solution.py:380
  10.5 17.4 %collective-permute-start.5 = (bf16[256,256]{1,0:T(8,128)(2,1)}, bf16[256,256]{1,0:T(8,128)(2,1)S(1)}, u32[]{:S(2)}, u32[]{:S(2)}) collective-permute-start(bf16[256,256]{1,0:T(8,128)(2,1)} %get-tuple-element.58), channel_id=1, source_target_pairs={{0,6},{2,4},{4,2},{6,0},{1,7},{3,5},{5,3},{7,1},{8,14},{10,12},{12... | collective-permute-start | bytes 393224 | tf_op jit(solution)/shard_map/ppermute | solution.py:380
  10.5 17.4 %collective-permute-start.6 = (bf16[256,256]{1,0:T(8,128)(2,1)}, bf16[256,256]{1,0:T(8,128)(2,1)}, u32[]{:S(2)}, u32[]{:S(2)}) collective-permute-start(bf16[256,256]{1,0:T(8,128)(2,1)} %get-tuple-element.59), channel_id=1, source_target_pairs={{0,2},{2,0},{4,6},{6,4},{1,3},{3,1},{5,7},{7,5},{8,10},{10,8},{12,... | collective-permute-start | bytes 393224 | tf_op jit(solution)/shard_map/ppermute | solution.py:380
  18.1 14.0 %collective-permute-start.10 = (bf16[256,256]{1,0:T(8,128)(2,1)S(1)}, bf16[256,256]{1,0:T(8,128)(2,1)S(1)}, u32[]{:S(2)}, u32[]{:S(2)}) collective-permute-start(bf16[256,256]{1,0:T(8,128)(2,1)S(1)} %get-tuple-element.66), channel_id=1, source_target_pairs={{0,4},{2,6},{4,0},{6,2},{1,5},{3,7},{5,1},{7,3},{8,12},{10,14},{12... | collective-permute-start | bytes 393224 | tf_op jit(solution)/shard_map/ppermute | solution.py:380
  19.6 13.9 %collective-permute-start.11 = (bf16[256,256]{1,0:T(8,128)(2,1)S(1)}, bf16[256,256]{1,0:T(8,128)(2,1)S(1)}, u32[]{:S(2)}, u32[]{:S(2)}) collective-permute-start(bf16[256,256]{1,0:T(8,128)(2,1)S(1)} %get-tuple-element.67), channel_id=1, source_target_pairs={{0,6},{2,4},{4,2},{6,0},{1,7},{3,5},{5,3},{7,1},{8,14},{10,12},{12... | collective-permute-start | bytes 393224 | tf_op jit(solution)/shard_map/ppermute | solution.py:380
  23.3 10.2 %collective-permute-start.12 = (bf16[256,256]{1,0:T(8,128)(2,1)S(1)}, bf16[256,256]{1,0:T(8,128)(2,1)S(1)}, u32[]{:S(2)}, u32[]{:S(2)}) collective-permute-start(bf16[256,256]{1,0:T(8,128)(2,1)S(1)} %get-tuple-element.68), channel_id=1, source_target_pairs={{0,2},{2,0},{4,6},{6,4},{1,3},{3,1},{5,7},{7,5},{8,10},{10,8},{12,... | collective-permute-start | bytes 393224 | tf_op jit(solution)/shard_map/ppermute | solution.py:380
  29.7 12.8 %collective-permute-start.7 = (bf16[256,256]{1,0:T(8,128)(2,1)S(1)}, bf16[256,256]{1,0:T(8,128)(2,1)S(1)}, u32[]{:S(2)}, u32[]{:S(2)}) collective-permute-start(bf16[256,256]{1,0:T(8,128)(2,1)S(1)} %get-tuple-element.61), channel_id=1, source_target_pairs={{0,4},{2,6},{4,0},{6,2},{1,5},{3,7},{5,1},{7,3},{8,12},{10,14},{12... | collective-permute-start | bytes 393224 | tf_op jit(solution)/shard_map/ppermute | solution.py:380
  29.8 20.6 %collective-permute-start.8 = (bf16[256,256]{1,0:T(8,128)(2,1)S(1)}, bf16[256,256]{1,0:T(8,128)(2,1)S(1)}, u32[]{:S(2)}, u32[]{:S(2)}) collective-permute-start(bf16[256,256]{1,0:T(8,128)(2,1)S(1)} %get-tuple-element.62), channel_id=1, source_target_pairs={{0,6},{2,4},{4,2},{6,0},{1,7},{3,5},{5,3},{7,1},{8,14},{10,12},{12... | collective-permute-start | bytes 393224 | tf_op jit(solution)/shard_map/ppermute | solution.py:380
  32.1 18.3 %collective-permute-start.9 = (bf16[256,256]{1,0:T(8,128)(2,1)S(1)}, bf16[256,256]{1,0:T(8,128)(2,1)S(1)}, u32[]{:S(2)}, u32[]{:S(2)}) collective-permute-start(bf16[256,256]{1,0:T(8,128)(2,1)S(1)} %get-tuple-element.63), channel_id=1, source_target_pairs={{0,2},{2,0},{4,6},{6,4},{1,3},{3,1},{5,7},{7,5},{8,10},{10,8},{12,... | collective-permute-start | bytes 393224 | tf_op jit(solution)/shard_map/ppermute | solution.py:380
  34.5 18.7 %collective-permute-start.13 = (bf16[256,256]{1,0:T(8,128)(2,1)S(1)}, bf16[256,256]{1,0:T(8,128)(2,1)S(1)}, u32[]{:S(2)}, u32[]{:S(2)}) collective-permute-start(bf16[256,256]{1,0:T(8,128)(2,1)S(1)} %get-tuple-element.69), channel_id=1, source_target_pairs={{0,4},{2,6},{4,0},{6,2},{1,5},{3,7},{5,1},{7,3},{8,12},{10,14},{12... | collective-permute-start | bytes 393224 | tf_op jit(solution)/shard_map/ppermute | solution.py:380
  36.4 19.7 %collective-permute-start.14 = (bf16[256,256]{1,0:T(8,128)(2,1)S(1)}, bf16[256,256]{1,0:T(8,128)(2,1)S(1)}, u32[]{:S(2)}, u32[]{:S(2)}) collective-permute-start(bf16[256,256]{1,0:T(8,128)(2,1)S(1)} %get-tuple-element.70), channel_id=1, source_target_pairs={{0,6},{2,4},{4,2},{6,0},{1,7},{3,5},{5,3},{7,1},{8,14},{10,12},{12... | collective-permute-start | bytes 393224 | tf_op jit(solution)/shard_map/ppermute | solution.py:380
  42.5 13.6 %collective-permute-start.15 = (bf16[256,256]{1,0:T(8,128)(2,1)S(1)}, bf16[256,256]{1,0:T(8,128)(2,1)S(1)}, u32[]{:S(2)}, u32[]{:S(2)}) collective-permute-start(bf16[256,256]{1,0:T(8,128)(2,1)S(1)} %get-tuple-element.71), channel_id=1, source_target_pairs={{0,2},{2,0},{4,6},{6,4},{1,3},{3,1},{5,7},{7,5},{8,10},{10,8},{12,... | collective-permute-start | bytes 393224 | tf_op jit(solution)/shard_map/ppermute | solution.py:380
  58.8 13.0 %collective-permute-start.17 = (bf16[256,256]{1,0:T(8,128)(2,1)S(1)}, bf16[256,256]{1,0:T(8,128)(2,1)S(1)}, u32[]{:S(2)}, u32[]{:S(2)}) collective-permute-start(bf16[256,256]{1,0:T(8,128)(2,1)S(1)} %get-tuple-element.82), channel_id=1, source_target_pairs={{0,12},{2,14},{4,8},{6,10},{8,20},{10,22},{12,16},{14,18},{16,28},... | collective-permute-start | bytes 393224 | tf_op jit(solution)/shard_map/ppermute | solution.py:377
  60.1 18.2 %collective-permute-start.18 = (bf16[256,256]{1,0:T(8,128)(2,1)S(1)}, bf16[256,256]{1,0:T(8,128)(2,1)S(1)}, u32[]{:S(2)}, u32[]{:S(2)}) collective-permute-start(bf16[256,256]{1,0:T(8,128)(2,1)S(1)} %get-tuple-element.83), channel_id=1, source_target_pairs={{0,14},{2,12},{4,10},{6,8},{8,22},{10,20},{12,18},{14,16},{16,30},... | collective-permute-start | bytes 393224 | tf_op jit(solution)/shard_map/ppermute | solution.py:377
  62.0 16.3 %collective-permute-start.19 = (bf16[256,256]{1,0:T(8,128)(2,1)S(1)}, bf16[256,256]{1,0:T(8,128)(2,1)S(1)}, u32[]{:S(2)}, u32[]{:S(2)}) collective-permute-start(bf16[256,256]{1,0:T(8,128)(2,1)S(1)} %get-tuple-element.84), channel_id=1, source_target_pairs={{0,10},{2,8},{4,14},{6,12},{8,18},{10,16},{12,22},{14,20},{16,26},... | collective-permute-start | bytes 393224 | tf_op jit(solution)/shard_map/ppermute | solution.py:377
  65.3 13.1 %collective-permute-start.20 = (bf16[256,256]{1,0:T(8,128)(2,1)S(1)}, bf16[256,256]{1,0:T(8,128)(2,1)S(1)}, u32[]{:S(2)}, u32[]{:S(2)}) collective-permute-start(bf16[256,256]{1,0:T(8,128)(2,1)S(1)} %get-tuple-element.85), channel_id=1, source_target_pairs={{0,8},{2,10},{4,12},{6,14},{8,16},{10,18},{12,20},{14,22},{16,24},... | collective-permute-start | bytes 393224 | tf_op jit(solution)/shard_map/ppermute | solution.py:377
  66.0 16.1 %collective-permute-start.24 = (bf16[256,256]{1,0:T(8,128)(2,1)S(1)}, bf16[256,256]{1,0:T(8,128)(2,1)S(1)}, u32[]{:S(2)}, u32[]{:S(2)}) collective-permute-start(bf16[256,256]{1,0:T(8,128)(2,1)S(1)} %get-tuple-element.91), channel_id=1, source_target_pairs={{0,4},{2,6},{4,0},{6,2},{1,5},{3,7},{5,1},{7,3},{8,12},{10,14},{12... | collective-permute-start | bytes 393224 | tf_op jit(solution)/shard_map/ppermute | solution.py:380
  71.8 15.2 %collective-permute-start.25 = (bf16[256,256]{1,0:T(8,128)(2,1)S(1)}, bf16[256,256]{1,0:T(8,128)(2,1)S(1)}, u32[]{:S(2)}, u32[]{:S(2)}) collective-permute-start(bf16[256,256]{1,0:T(8,128)(2,1)S(1)} %get-tuple-element.92), channel_id=1, source_target_pairs={{0,6},{2,4},{4,2},{6,0},{1,7},{3,5},{5,3},{7,1},{8,14},{10,12},{12... | collective-permute-start | bytes 393224 | tf_op jit(solution)/shard_map/ppermute | solution.py:380
  78.3 8.7 %collective-permute-start.26 = (bf16[256,256]{1,0:T(8,128)(2,1)S(1)}, bf16[256,256]{1,0:T(8,128)(2,1)S(1)}, u32[]{:S(2)}, u32[]{:S(2)}) collective-permute-start(bf16[256,256]{1,0:T(8,128)(2,1)S(1)} %get-tuple-element.93), channel_id=1, source_target_pairs={{0,2},{2,0},{4,6},{6,4},{1,3},{3,1},{5,7},{7,5},{8,10},{10,8},{12,... | collective-permute-start | bytes 393224 | tf_op jit(solution)/shard_map/ppermute | solution.py:380
  79.3 12.7 %collective-permute-start.21 = (bf16[256,256]{1,0:T(8,128)(2,1)S(1)}, bf16[256,256]{1,0:T(8,128)(2,1)S(1)}, u32[]{:S(2)}, u32[]{:S(2)}) collective-permute-start(bf16[256,256]{1,0:T(8,128)(2,1)S(1)} %get-tuple-element.86), channel_id=1, source_target_pairs={{0,4},{2,6},{4,0},{6,2},{1,5},{3,7},{5,1},{7,3},{8,12},{10,14},{12... | collective-permute-start | bytes 393224 | tf_op jit(solution)/shard_map/ppermute | solution.py:380
  79.4 18.6 %collective-permute-start.22 = (bf16[256,256]{1,0:T(8,128)(2,1)S(1)}, bf16[256,256]{1,0:T(8,128)(2,1)S(1)}, u32[]{:S(2)}, u32[]{:S(2)}) collective-permute-start(bf16[256,256]{1,0:T(8,128)(2,1)S(1)} %get-tuple-element.87), channel_id=1, source_target_pairs={{0,6},{2,4},{4,2},{6,0},{1,7},{3,5},{5,3},{7,1},{8,14},{10,12},{12... | collective-permute-start | bytes 393224 | tf_op jit(solution)/shard_map/ppermute | solution.py:380
  82.0 16.1 %collective-permute-start.23 = (bf16[256,256]{1,0:T(8,128)(2,1)S(1)}, bf16[256,256]{1,0:T(8,128)(2,1)S(1)}, u32[]{:S(2)}, u32[]{:S(2)}) collective-permute-start(bf16[256,256]{1,0:T(8,128)(2,1)S(1)} %get-tuple-element.88), channel_id=1, source_target_pairs={{0,2},{2,0},{4,6},{6,4},{1,3},{3,1},{5,7},{7,5},{8,10},{10,8},{12,... | collective-permute-start | bytes 393224 | tf_op jit(solution)/shard_map/ppermute | solution.py:380
  88.0 15.8 %collective-permute-start.27 = (bf16[256,256]{1,0:T(8,128)(2,1)S(1)}, bf16[256,256]{1,0:T(8,128)(2,1)S(1)}, u32[]{:S(2)}, u32[]{:S(2)}) collective-permute-start(bf16[256,256]{1,0:T(8,128)(2,1)S(1)} %get-tuple-element.94), channel_id=1, source_target_pairs={{0,12},{2,14},{4,8},{6,10},{8,20},{10,22},{12,16},{14,18},{16,28},... | collective-permute-start | bytes 393224 | tf_op jit(solution)/shard_map/ppermute | solution.py:377
  88.1 21.3 %collective-permute-start.28 = (bf16[256,256]{1,0:T(8,128)(2,1)S(1)}, bf16[256,256]{1,0:T(8,128)(2,1)S(1)}, u32[]{:S(2)}, u32[]{:S(2)}) collective-permute-start(bf16[256,256]{1,0:T(8,128)(2,1)S(1)} %get-tuple-element.95), channel_id=1, source_target_pairs={{0,14},{2,12},{4,10},{6,8},{8,22},{10,20},{12,18},{14,16},{16,30},... | collective-permute-start | bytes 393224 | tf_op jit(solution)/shard_map/ppermute | solution.py:377
  92.0 17.4 %collective-permute-start.29 = (bf16[256,256]{1,0:T(8,128)(2,1)S(1)}, bf16[256,256]{1,0:T(8,128)(2,1)S(1)}, u32[]{:S(2)}, u32[]{:S(2)}) collective-permute-start(bf16[256,256]{1,0:T(8,128)(2,1)S(1)} %get-tuple-element.96), channel_id=1, source_target_pairs={{0,10},{2,8},{4,14},{6,12},{8,18},{10,16},{12,22},{14,20},{16,26},... | collective-permute-start | bytes 393224 | tf_op jit(solution)/shard_map/ppermute | solution.py:377
  98.0 12.2 %collective-permute-start.30 = (bf16[256,256]{1,0:T(8,128)(2,1)S(1)}, bf16[256,256]{1,0:T(8,128)(2,1)S(1)}, u32[]{:S(2)}, u32[]{:S(2)}) collective-permute-start(bf16[256,256]{1,0:T(8,128)(2,1)S(1)} %get-tuple-element.97), channel_id=1, source_target_pairs={{0,8},{2,10},{4,12},{6,14},{8,16},{10,18},{12,20},{14,22},{16,24},... | collective-permute-start | bytes 393224 | tf_op jit(solution)/shard_map/ppermute | solution.py:377
  98.1 14.1 %collective-permute-start.16 = (bf16[256,1024]{1,0:T(8,128)(2,1)S(1)}, bf16[256,1024]{1,0:T(8,128)(2,1)S(1)}, u32[]{:S(2)}, u32[]{:S(2)}) collective-permute-start(bf16[256,1024]{1,0:T(8,128)(2,1)S(1)} %get-tuple-element.74), channel_id=1, source_target_pairs={{0,1},{1,0},{2,3},{3,2},{4,5},{5,4},{6,7},{7,6},{8,9},{9,8},{10,11... | collective-permute-start | bytes 1572872 | tf_op jit(solution)/shard_map/ppermute | solution.py:327
  110.7 2.6 %collective-permute-start.31 = (bf16[256,1024]{1,0:T(8,128)(2,1)S(1)}, bf16[256,1024]{1,0:T(8,128)(2,1)S(1)}, u32[]{:S(2)}, u32[]{:S(2)}) collective-permute-start(bf16[256,1024]{1,0:T(8,128)(2,1)S(1)} %half_space.3), channel_id=1, source_target_pairs={{0,1},{1,0},{2,3},{3,2},{4,5},{5,4},{6,7},{7,6},{8,9},{9,8},{10,11... | collective-permute-start | bytes 1572872 | tf_op jit(solution)/shard_map/ppermute | solution.py:327
  (10 other events, 59.4 us)

commit v2 on v1

--- a/solution.py
+++ b/solution.py
@@ -17,6 +17,7 @@
 VMEM = pl.BlockSpec(memory_space=pltpu.VMEM)
 SMEM = pl.BlockSpec(memory_space=pltpu.SMEM)
 ANY = pl.BlockSpec(memory_space=pl.ANY)
+HBM = pl.BlockSpec(memory_space=pltpu.HBM)
 F32 = jnp.float32
 BF16 = jnp.bfloat16
 
@@ -149,19 +150,52 @@
             ]
 
 
-def to_modes_kernel(odd, fields_ref, other_ref, table_ref, *refs):
-    outs, (folded, modes) = refs[:-2], refs[-2:]
-    rows = other_ref.shape[0] // 4
-    half = table_ref.shape[0]
+def own_modes_kernel(fields_ref, even_ref, odd_ref, evens_ref, odds_ref, held, tables, sems):
+    rows, half = evens_ref.shape
+    copies = [
+        pltpu.make_async_copy(
+            fields_ref.at[rows_of(lax.axis_index("core") * rows, rows), :], held, sems.at[0]
+        ),
+        pltpu.make_async_copy(even_ref, tables.at[0], sems.at[1]),
+        pltpu.make_async_copy(odd_ref, tables.at[1], sems.at[2]),
+    ]
+    for copy in copies:
+        copy.start()
+    copies[0].wait()
+    low, high = held[:, :half], held[:, half:]
+    copies[1].wait()
+    evens_ref[...] = dot(low + high, tables[0]).astype(BF16)
+    copies[2].wait()
+    odds_ref[...] = dot(low - high, tables[1]).astype(BF16)
+
+
+def to_modes_kernel(odd, other_ref, own_ref, table_ref, *refs):
+    outs, modes = refs[:-1], refs[-1]
+    rows, half = own_ref.shape
+    own = rows // 2
     core = lax.axis_index("core")
-    for part in range(2):
-        mine = rows_of((2 * core + part) * rows, rows)
-        for index, source in enumerate((fields_ref, other_ref)):
-            low, high = source[mine, :half], source[mine, half:]
-            there = rows_of(2 * part * rows + (core ^ index) * rows, rows)
-            folded[there, :] = low - high if odd else low + high
-    modes[...] = dot(folded[...], table_ref[...]).astype(BF16)
-    split_modes(lax.axis_index("z"), modes, outs)
+    theirs = rows_of(core * rows, rows)
+    low, high = other_ref[theirs, :half], other_ref[theirs, half:]
+    modes[...] = dot(low - high if odd else low + high, table_ref[...]).astype(BF16)
+    block = half // len(outs)
+    for k, out in zip(partners(len(outs)), outs):
+        columns = rows_of((lax.axis_index("z") ^ k) * block, block)
+        for part in range(2):
+            lanes = slice(part * block, (part + 1) * block)
+            lines = slice(part * own, (part + 1) * own)
+            out[rows_of(core * own, own), lanes] = own_ref[lines, columns]
+            out[rows_of((core ^ 1) * own, own), lanes] = modes[lines, columns]
+
+
+def odd_to_modes_kernel(blocks_ref, top_block_ref, reference_ref, *refs):
+    settings_ref = refs[-2]
+    depth = lax.axis_index("depth")
+    above = blocks_ref[jnp.maximum(depth - 1, 0)]
+    second = jnp.where(depth == 0, top_block_ref[0], above)
+    for index, block in enumerate((blocks_ref[depth], second)):
+        settings_ref[2 * index] = omega_top * (block.astype(F32) + 1.0) / NFREQ
+        settings_ref[2 * index + 1] = reference_ref[0]
+    to_modes_kernel(1, *refs[:-2], refs[-1])
 
 
 def along_x_kernel(
@@ -205,7 +239,7 @@
     count, cos_ref, sin_ref, top_ref, top_other_ref, even_t_ref, odd_ref, part_ref, *refs
 ):
     pieces, outs = refs[:count], refs[count : 2 * count]
-    folded_ref, keep_ref, give_ref, modes, space, sums = refs[2 * count :]
+    folded_ref, both_ref, modes, sums = refs[2 * count :]
     here, core = lax.axis_index("z"), lax.axis_index("core")
     rows = pieces[0].shape[0]
     own = rows // 2
@@ -216,29 +250,30 @@
         columns = slice(start, start + step)
         second = dot(modes[...], odd_ref[:, columns])
         first = part_ref[:, columns]
+        stepped = []
         for values, at in ((first + second, start), (first - second, start + half)):
             lanes = slice(at, at + step)
-            real, imag = turned(values[:rows], values[rows:], cos_ref[:, lanes], sin_ref[:, lanes])
-            space[:rows, lanes] = real
-            space[rows:, lanes] = imag
-    for index, out in enumerate((keep_ref, give_ref)):
+            fields = turned(values[:rows], values[rows:], cos_ref[:, lanes], sin_ref[:, lanes])
+            stepped.append(fields)
+            for index in range(2):
+                for part, field in enumerate(fields):
+                    there = (2 * index + part) * own
+                    both_ref[there : there + own, lanes] = field[index * own : (index + 1) * own]
         for part in range(2):
-            out[part * own : (part + 1) * own, :] = space[
-                rows_of(part * rows + (core ^ index) * own, own), :
-            ]
+            lines = slice(part * rows, (part + 1) * rows)
+            sums[lines, columns] = stepped[0][part] + stepped[1][part]
+            folded_ref[lines, columns] = stepped[0][part] - stepped[1][part]
 
     @pl.when(lax.axis_index("depth") == lax.axis_size("depth") - 1)
     def _():
-        for part in range(2):
-            space[rows_of(part * rows + core * own, own), :] = top_ref[
-                rows_of((2 * core + part) * own, own), :
-            ]
-            space[rows_of(part * rows + (core ^ 1) * own, own), :] = top_other_ref[
-                rows_of((2 * core + part) * own, own), :
-            ]
-
-    sums[...] = space[:, :half] + space[:, half:]
-    folded_ref[...] = space[:, :half] - space[:, half:]
+        for index, source in enumerate((top_ref, top_other_ref)):
+            for part in range(2):
+                lines = rows_of((2 * core + part) * own, own)
+                low, high = source[lines, :half], source[lines, half:]
+                there = rows_of(part * rows + (core ^ index) * own, own)
+                sums[there, :] = low + high
+                folded_ref[there, :] = low - high
+
     modes[...] = dot(sums[...], even_t_ref[...]).astype(BF16)
     split_modes(here, modes, outs)
 
@@ -273,6 +308,11 @@
             )
 
 
+def other_rows_kernel(both_ref, out_ref):
+    rows = out_ref.shape[0]
+    out_ref[...] = both_ref[rows_of((lax.axis_index("core") ^ 1) * rows, rows), :]
+
+
 def finish_kernel(first_ref, first_other_ref, keep_ref, got_ref, fields_ref, image_ref):
     rows = keep_ref.shape[0]
     own = rows // 2
@@ -282,10 +322,14 @@
     step = 16
     for start in range(0, own, step):
         total = None
-        for one, two in ((first_ref, first_other_ref), (keep_ref, got_ref)):
-            for part in range(2):
-                lines = slice(part * own + start, part * own + start + step)
-                term = one[lines, :].astype(F32) * two[lines, :].astype(F32)
+        for part in range(2):
+            lines = slice(part * own + start, part * own + start + step)
+            mine = rows_of(core * rows + part * own + start, step)
+            for one, two in (
+                (first_ref[mine, :], first_other_ref[lines, :]),
+                (keep_ref[lines, :], got_ref[lines, :]),
+            ):
+                term = one.astype(F32) * two.astype(F32)
                 total = term if total is None else total + term
         image_ref[start : start + step, :] = total
 
@@ -294,16 +338,20 @@
     return kernel(*refs[count:])
 
 
-def call(kernel, operands, outs, scratch=(), flops=0, name=None, scalars=0, behind=()):
+def call(
+    kernel, operands, outs, scratch=(), flops=0, name=None, scalars=0, behind=(), ins=None, puts=None,
+    grant=24,
+):
     moved = sum(math.prod(a.shape) * a.dtype.itemsize for a in operands)
     moved += sum(math.prod(a.shape) * a.dtype.itemsize for a in outs)
     return pl.pallas_call(
         functools.partial(after, len(behind), kernel),
         out_shape=tuple(outs),
-        in_specs=[ANY] * len(behind) + [SMEM] * scalars + [VMEM] * (len(operands) - scalars),
-        out_specs=tuple(VMEM for _ in outs),
+        in_specs=[ANY] * len(behind)
+        + (ins or [SMEM] * scalars + [VMEM] * (len(operands) - scalars)),
+        out_specs=tuple(puts or [VMEM] * len(outs)),
         scratch_shapes=list(scratch),
-        compiler_params=pltpu.CompilerParams(vmem_limit_bytes=24 * 1024 * 1024),
+        compiler_params=pltpu.CompilerParams(vmem_limit_bytes=grant * 1024 * 1024),
         cost_estimate=pl.CostEstimate(flops=flops, bytes_accessed=moved, transcendentals=0),
         name=name,
     )(*behind, *operands)
@@ -330,21 +378,6 @@
     top = top_fields.reshape(2 * rows, length_y)
     mine = slowness[0]
     fields_other, top_other, other = other_core(fields), other_core(top), other_core(mine)
-    below = lax.ppermute(ref_slowness, "depth", [((d + 1) % slabs, d) for d in range(slabs)])
-
-    depth = lax.axis_index("depth")
-
-    def angular(block_id):
-        return omega_top * (block_id.astype(F32) + 1.0) / NFREQ
-
-    second = jnp.where(depth == 0, top_block[0], flight_blocks[jnp.maximum(depth - 1, 0)])
-    odd_second = jnp.where(depth == slabs - 1, top_block[0], flight_blocks[depth])
-    settings = jnp.stack([
-        angular(flight_blocks[depth]), ref_slowness[0],
-        angular(second), ref_slowness[0],
-        angular(odd_second), below[0],
-    ])
-
     def factors(stage, odd, behind):
         return call(
             functools.partial(factors_kernel, odd, length_y, stage), (settings,),
@@ -380,13 +413,6 @@
                 got.append(lax.ppermute(piece, "z", pairs) if k else piece)
         return got
 
-    def to_modes(odd, behind=()):
-        return call(
-            functools.partial(to_modes_kernel, odd),
-            (fields, fields_other, odd_y_t if odd else even_y_t),
-            pieces_of, [part, part], flops, "to_modes", behind=behind,
-        )
-
     def along_x(pieces, factor, behind=()):
         return call(
             functools.partial(along_x_kernel, chips), (*factor, *tables_x, *pieces),
@@ -398,28 +424,46 @@
             even_part_kernel, (even_y, *pieces), [of(lines, F32)], [part], flops, "even_part"
         )[0]
 
-    evens = to_modes(0)
-    odds = to_modes(1, (top_other, other, below))
-    ready = (odds[-1],)
-    even_factors, odd_factors = factors(0, 0, ready), factors(0, 1, ready)
-    first_phases = phases(0, ready)
+    share = (rows, half)
+    own_evens, own_odds = call(
+        own_modes_kernel, (fields, even_y_t, odd_y_t), [of(share)] * 2,
+        [
+            pltpu.VMEM((rows, length_y), BF16), pltpu.VMEM((2, half, half), BF16),
+            pltpu.SemaphoreType.DMA((3,)),
+        ],
+        flops, "own_modes", ins=[HBM] * 3, grant=58,
+    )
+    evens = call(
+        functools.partial(to_modes_kernel, 0), (fields_other, own_evens, even_y_t),
+        pieces_of, [pltpu.VMEM(share, BF16)], flops // 2, "even_to_modes",
+    )
+    *odds, settings = call(
+        odd_to_modes_kernel,
+        (flight_blocks, top_block, ref_slowness, fields_other, own_odds, odd_y_t),
+        pieces_of + [of((4,), F32)], [pltpu.VMEM(share, BF16)], flops // 2, "odd_to_modes",
+        scalars=3, behind=(top_other, other), puts=[VMEM] * chips + [SMEM],
+    )
+    even_factors, odd_factors = factors(0, 0, ()), factors(0, 1, ())
+    first_phases = phases(0, ())
     evens, odds = exchange(evens), exchange(odds)
     evens = exchange(along_x(evens, even_factors, (odd_factors[0], first_phases[0])))
     odds = exchange(along_x(odds, odd_factors))
-    *evens, folded, first_keep, first_give = call(
+    *evens, folded, first = call(
         functools.partial(turn_around_kernel, chips),
         (*first_phases, top, top_other, even_y_t, odd_y, even_part(evens), *odds),
-        pieces_of + [of(lines)] + [of((rows, length_y))] * 2,
-        [part, pltpu.VMEM((2 * rows, length_y), BF16), part], 2 * flops, "turn_around",
+        pieces_of + [of(lines), of((2 * rows, length_y))], [part, part], 2 * flops, "turn_around",
     )
     odds = call(odd_modes_kernel, (folded, odd_y_t), pieces_of, [part], flops, "odd_modes")
     ready = (odds[-1],)
-    even_factors, odd_factors = factors(1, 0, ready), factors(2, 1, ready)
+    even_factors, odd_factors = factors(1, 0, ready), factors(1, 1, ready)
     second_phases = phases(1, ready)
-    evens, odds = exchange(evens, 1), exchange(odds)
-    first_got = other_core(first_give)
+    evens, odds = exchange(evens, 1), exchange(odds, 1)
     evens = exchange(along_x(evens, even_factors, (odd_factors[0], second_phases[0])))
-    odds = exchange(along_x(odds, odd_factors), 1)
+    odds = along_x(odds, odd_factors)
+    first_other = other_core(
+        call(other_rows_kernel, (first,), [of((rows, length_y))], name="other_rows", behind=odds[-1:])[0]
+    )
+    odds = exchange(odds)
     first_part = even_part(evens)
     give, keep = [
         call(
@@ -431,7 +475,7 @@
     ]
     got = other_core(give)
     fields, image = call(
-        finish_kernel, (first_keep, first_got, keep, got),
+        finish_kernel, (first, first_other, keep, got),
         [of((2 * rows, length_y)), of((own, length_y), F32)], flops=8 * cells, name="finish",
     )
     return image[None], fields.reshape(flight_fields.shape)

time: 116 us -> 109 us (0.940)
  starting transfers between devices: 46.9 us -> 37.9 us
  waiting for transfers between devices: 38.3 us -> 46.1 us
  local copies, waits for them, and re-layouts: 4.3 us -> 1.59 us
  between operations: 3.96 us -> 2.23 us
    ppermute x8, starting transfers between devices: 16.7 us -> 9.81 us  [exchange(): got.append(lax.ppermute(piece, ('depth', 'z'), pairs))]
    ppermute x18, waiting for transfers between devices: 24 us -> 30.8 us  [exchange(): got.append(lax.ppermute(piece, 'z', pairs) if k else piece)]
    ppermute x1 -> x0, starting transfers between devices: 2.18 us -> none  [per_device(): lax.ppermute(ref_slowness, 'depth', [((d + 1) % slabs, d) for d in range(...]
    ppermute x8, waiting for transfers between devices: 12.8 us -> 14.2 us  [exchange(): got.append(lax.ppermute(piece, ('depth', 'z'), pairs))]
    unnamed x20 -> x18, local copies, waits for them, and re-layouts: 2.95 us -> 1.59 us
    pallas_call x19 -> x21, Pallas kernels: 21.1 us -> 20.7 us  [call(): pl.pallas_call(functools.partial(after, len(behind), kernel), out_shape=t...]
  transfers between devices with their start and end apart: 32 -> 31, of which waited for: 12 -> 10; matrix products, arithmetic and copies ran while one was open for 1% -> 0% of each run, Pallas kernels for 15% -> 17%
where the time goes in v2:
time: 109 us
  waiting for transfers between devices  46.1 us (42%)
  starting transfers between devices  37.9 us (35%)
  Pallas kernels  20.7 us (19%)
  between operations  2.23 us (2%)
  local copies, waits for them, and re-layouts  1.59 us (1%)
    ppermute x18, waiting for transfers between devices, exchange(): got.append(lax.ppermute(piece, 'z', pairs) if k else piece)  30.8 us
    pallas_call x21, Pallas kernels, call(): pl.pallas_call(functools.partial(after, len(behind), kernel), out_shape=t...  20.7 us
    ppermute x18, starting transfers between devices, exchange(): got.append(lax.ppermute(piece, 'z', pairs) if k else piece)  20.4 us
    ppermute x8, waiting for transfers between devices, exchange(): got.append(lax.ppermute(piece, ('depth', 'z'), pairs))  14.2 us
    ppermute x8, starting transfers between devices, exchange(): got.append(lax.ppermute(piece, ('depth', 'z'), pairs))  9.81 us
    ppermute x5, starting transfers between devices, other_core(): return lax.ppermute(value, 'core', [(0, 1), (1, 0)])  7.68 us
  transfers between devices with their start and end apart: 31, of which 10 were waited for; matrix products, arithmetic and copies ran while one was open for 0% of the time, Pallas kernels for 17%

profile of v2, /device:TPU:9, one launch (start us, length us, event | category | flops | bytes accessed | tf_op | source)
XLA Modules:
  0.0 108.5 jit_solution(7743363994540817991)
XLA Ops:
  1.9 2.5 %own_modes.1 = (bf16[256,512]{1,0:T(8,128)(2,1)}, bf16[256,512]{1,0:T(8,128)(2,1)}) custom-call(bf16[512,1024]{1,0:T(8,128)(2,1)} %bitcast.11, bf16[512,512]{1,0:T(8,128)(2,1)} %constant.9.clone.refs_1_.refs_2_.refs_5_.refs_3_.refs_4_, bf16[512,512]{1,0:T(8,128)(2,1)} %constant.11.clone.refs_2_.refs_7_.refs_5_.refs_1_), custom_call_target="tpu_custom_call" | custom-call | flops 268435456 | bytes 2621440 | tf_op jit(solution)/shard_map/own_modes/pallas_call | solution.py:347
  5.8 2.4 %collective-permute-start.3 = (bf16[256,256]{1,0:T(8,128)(2,1)S(1)}, bf16[256,256]{1,0:T(8,128)(2,1)S(1)}, u32[]{:S(2)}, u32[]{:S(2)}) collective-permute-start(bf16[256,256]{1,0:T(8,128)(2,1)S(1)} %get-tuple-element.61), channel_id=1, source_target_pairs={{0,4},{2,6},{4,0},{6,2},{1,5},{3,7},{5,1},{7,3},{8,12},{10,14},{12... | collective-permute-start | bytes 393224 | tf_op jit(solution)/shard_map/ppermute | solution.py:413
  8.2 1.2 %collective-permute-start.5 = (bf16[256,256]{1,0:T(8,128)(2,1)S(1)}, bf16[256,256]{1,0:T(8,128)(2,1)S(1)}, u32[]{:S(2)}, u32[]{:S(2)}) collective-permute-start(bf16[256,256]{1,0:T(8,128)(2,1)S(1)} %get-tuple-element.63), channel_id=1, source_target_pairs={{0,2},{2,0},{4,6},{6,4},{1,3},{3,1},{5,7},{7,5},{8,10},{10,8},{12,... | collective-permute-start | bytes 393224 | tf_op jit(solution)/shard_map/ppermute | solution.py:413
  11.4 1.3 %odd_to_modes.1 = (bf16[256,256]{1,0:T(8,128)(2,1)S(1)}, bf16[256,256]{1,0:T(8,128)(2,1)S(1)}, bf16[256,256]{1,0:T(8,128)(2,1)S(1)}, bf16[256,256]{1,0:T(8,128)(2,1)S(1)}, f32[4]{0:T(128)S(1)}) custom-call(bf16[512,1024]{1,0:T(8,128)(2,1)S(1)} %collective-permute-done.refs_0_.refs_3_, f32[128,1024]{1,0:T(8,128)S(1)} %collective-permute-done.1.refs_1_.refs_2_.refs_3_, ...), custom_call_target="tpu_custom_call" | custom-call | flops 134217728 | bytes 2359336 | tf_op jit(solution)/shard_map/odd_to_modes/pallas_call | solution.py:347
  12.7 1.5 %collective-permute-start.9 = (bf16[256,256]{1,0:T(8,128)(2,1)S(1)}, bf16[256,256]{1,0:T(8,128)(2,1)S(1)}, u32[]{:S(2)}, u32[]{:S(2)}) collective-permute-start(bf16[256,256]{1,0:T(8,128)(2,1)S(1)} %get-tuple-element.70), channel_id=1, source_target_pairs={{0,4},{2,6},{4,0},{6,2},{1,5},{3,7},{5,1},{7,3},{8,12},{10,14},{12... | collective-permute-start | bytes 393224 | tf_op jit(solution)/shard_map/ppermute | solution.py:413
  16.2 1.7 %phases.2 = (f32[256,1024]{1,0:T(8,128)S(1)}, f32[256,1024]{1,0:T(8,128)S(1)}) custom-call(f32[4]{0:T(128)S(1)} %get-tuple-element.54.refs_0_.refs_1_, f32[128,1024]{1,0:T(8,128)S(1)} %bitcast.6, f32[128,1024]{1,0:T(8,128)S(1)} %collective-permute-done.1.refs_1_.refs_2_.refs_3_), custom_call_target="tpu_custom_call" | custom-call | flops 104857600 | bytes 3145744 | tf_op jit(solution)/shard_map/phases/pallas_call | solution.py:347
  17.9 2.2 %collective-permute-start.11 = (bf16[256,256]{1,0:T(8,128)(2,1)S(1)}, bf16[256,256]{1,0:T(8,128)(2,1)S(1)}, u32[]{:S(2)}, u32[]{:S(2)}) collective-permute-start(bf16[256,256]{1,0:T(8,128)(2,1)S(1)} %get-tuple-element.72), channel_id=1, source_target_pairs={{0,2},{2,0},{4,6},{6,4},{1,3},{3,1},{5,7},{7,5},{8,10},{10,8},{12,... | collective-permute-start | bytes 393224 | tf_op jit(solution)/shard_map/ppermute | solution.py:413
  20.1 5.4 %collective-permute-done.4.refs_9_ = bf16[256,256]{1,0:T(8,128)(2,1)S(1)} collective-permute-done((bf16[256,256]{1,0:T(8,128)(2,1)S(1)}, bf16[256,256]{1,0:T(8,128)(2,1)S(1)}, u32[]{:S(2)}, u32[]{:S(2)}) %collective-permute-start.4) | collective-permute-done | bytes 131104 | tf_op jit(solution)/shard_map/ppermute | solution.py:413
  26.5 2.3 %collective-permute-start.7 = (bf16[256,256]{1,0:T(8,128)(2,1)S(1)}, bf16[256,256]{1,0:T(8,128)(2,1)S(1)}, u32[]{:S(2)}, u32[]{:S(2)}) collective-permute-start(bf16[256,256]{1,0:T(8,128)(2,1)S(1)} %get-tuple-element.66), channel_id=1, source_target_pairs={{0,6},{2,4},{4,2},{6,0},{1,7},{3,5},{5,3},{7,1},{8,14},{10,12},{12... | collective-permute-start | bytes 393224 | tf_op jit(solution)/shard_map/ppermute | solution.py:413
  28.8 1.3 %collective-permute-start.8 = (bf16[256,256]{1,0:T(8,128)(2,1)S(1)}, bf16[256,256]{1,0:T(8,128)(2,1)S(1)}, u32[]{:S(2)}, u32[]{:S(2)}) collective-permute-start(bf16[256,256]{1,0:T(8,128)(2,1)S(1)} %get-tuple-element.67), channel_id=1, source_target_pairs={{0,2},{2,0},{4,6},{6,4},{1,3},{3,1},{5,7},{7,5},{8,10},{10,8},{12,... | collective-permute-start | bytes 393224 | tf_op jit(solution)/shard_map/ppermute | solution.py:413
  30.1 6.2 %collective-permute-done.10.refs_7_ = bf16[256,256]{1,0:T(8,128)(2,1)S(1)} collective-permute-done((bf16[256,256]{1,0:T(8,128)(2,1)S(1)}, bf16[256,256]{1,0:T(8,128)(2,1)S(1)}, u32[]{:S(2)}, u32[]{:S(2)}) %collective-permute-start.10) | collective-permute-done | bytes 131104 | tf_op jit(solution)/shard_map/ppermute | solution.py:413
  37.3 2.7 %collective-permute-start.13 = (bf16[256,256]{1,0:T(8,128)(2,1)S(1)}, bf16[256,256]{1,0:T(8,128)(2,1)S(1)}, u32[]{:S(2)}, u32[]{:S(2)}) collective-permute-start(bf16[256,256]{1,0:T(8,128)(2,1)S(1)} %get-tuple-element.75), channel_id=1, source_target_pairs={{0,6},{2,4},{4,2},{6,0},{1,7},{3,5},{5,3},{7,1},{8,14},{10,12},{12... | collective-permute-start | bytes 393224 | tf_op jit(solution)/shard_map/ppermute | solution.py:413
  40.1 1.1 %collective-permute-start.14 = (bf16[256,256]{1,0:T(8,128)(2,1)S(1)}, bf16[256,256]{1,0:T(8,128)(2,1)S(1)}, u32[]{:S(2)}, u32[]{:S(2)}) collective-permute-start(bf16[256,256]{1,0:T(8,128)(2,1)S(1)} %get-tuple-element.76), channel_id=1, source_target_pairs={{0,2},{2,0},{4,6},{6,4},{1,3},{3,1},{5,7},{7,5},{8,10},{10,8},{12,... | collective-permute-start | bytes 393224 | tf_op jit(solution)/shard_map/ppermute | solution.py:413
  41.2 6.3 %collective-permute-done.7.refs_2_ = bf16[256,256]{1,0:T(8,128)(2,1)S(1)} collective-permute-done((bf16[256,256]{1,0:T(8,128)(2,1)S(1)}, bf16[256,256]{1,0:T(8,128)(2,1)S(1)}, u32[]{:S(2)}, u32[]{:S(2)}) %collective-permute-start.7) | collective-permute-done | bytes 131104 | tf_op jit(solution)/shard_map/ppermute | solution.py:413
  48.0 2.8 %collective-permute-done.12.refs_7_ = bf16[256,256]{1,0:T(8,128)(2,1)S(1)} collective-permute-done((bf16[256,256]{1,0:T(8,128)(2,1)S(1)}, bf16[256,256]{1,0:T(8,128)(2,1)S(1)}, u32[]{:S(2)}, u32[]{:S(2)}) %collective-permute-start.12) | collective-permute-done | bytes 131104 | tf_op jit(solution)/shard_map/ppermute | solution.py:413
  50.8 2.8 %collective-permute-done.13.refs_8_ = bf16[256,256]{1,0:T(8,128)(2,1)S(1)} collective-permute-done((bf16[256,256]{1,0:T(8,128)(2,1)S(1)}, bf16[256,256]{1,0:T(8,128)(2,1)S(1)}, u32[]{:S(2)}, u32[]{:S(2)}) %collective-permute-start.13) | collective-permute-done | bytes 131104 | tf_op jit(solution)/shard_map/ppermute | solution.py:413
  53.6 1.4 %turn_around.1 = (bf16[256,256]{1,0:T(8,128)(2,1)S(1)}, bf16[256,256]{1,0:T(8,128)(2,1)S(1)}, bf16[256,256]{1,0:T(8,128)(2,1)S(1)}, bf16[256,256]{1,0:T(8,128)(2...) custom-call(f32[256,1024]{1,0:T(8,128)S(1)} %get-tuple-element.55.refs_1_.refs_0_, ...), custom_call_target="tpu_custom_call" | custom-call | flops 536870912 | bytes 8912896 | tf_op jit(solution)/shard_map/turn_around/pallas_call | solution.py:347
  55.0 1.3 %collective-permute-start.20 = (bf16[256,256]{1,0:T(8,128)(2,1)S(1)}, bf16[256,256]{1,0:T(8,128)(2,1)S(1)}, u32[]{:S(2)}, u32[]{:S(2)}) collective-permute-start(bf16[256,256]{1,0:T(8,128)(2,1)S(1)} %get-tuple-element.91), channel_id=1, source_target_pairs={{0,12},{2,14},{4,8},{6,10},{8,20},{10,22},{12,16},{14,18},{16,28},... | collective-permute-start | bytes 393224 | tf_op jit(solution)/shard_map/ppermute | solution.py:410
  56.3 2.0 %collective-permute-start.21 = (bf16[256,256]{1,0:T(8,128)(2,1)S(1)}, bf16[256,256]{1,0:T(8,128)(2,1)S(1)}, u32[]{:S(2)}, u32[]{:S(2)}) collective-permute-start(bf16[256,256]{1,0:T(8,128)(2,1)S(1)} %get-tuple-element.92), channel_id=1, source_target_pairs={{0,14},{2,12},{4,10},{6,8},{8,22},{10,20},{12,18},{14,16},{16,30},... | collective-permute-start | bytes 393224 | tf_op jit(solution)/shard_map/ppermute | solution.py:410
  58.3 3.2 %collective-permute-start.22 = (bf16[256,256]{1,0:T(8,128)(2,1)S(1)}, bf16[256,256]{1,0:T(8,128)(2,1)S(1)}, u32[]{:S(2)}, u32[]{:S(2)}) collective-permute-start(bf16[256,256]{1,0:T(8,128)(2,1)S(1)} %get-tuple-element.93), channel_id=1, source_target_pairs={{0,10},{2,8},{4,14},{6,12},{8,18},{10,16},{12,22},{14,20},{16,26},... | collective-permute-start | bytes 393224 | tf_op jit(solution)/shard_map/ppermute | solution.py:410
  62.2 1.2 %collective-permute-start.18 = (bf16[256,256]{1,0:T(8,128)(2,1)S(1)}, bf16[256,256]{1,0:T(8,128)(2,1)S(1)}, u32[]{:S(2)}, u32[]{:S(2)}) collective-permute-start(bf16[256,256]{1,0:T(8,128)(2,1)S(1)} %get-tuple-element.80.refs_0_), channel_id=1, source_target_pairs={{0,8},{2,10},{4,12},{6,14},{8,16},{10,18},{12,20},{14,22},{16,24},... | collective-permute-start | bytes 393224 | tf_op jit(solution)/shard_map/ppermute | solution.py:410
  65.4 1.7 %phases.3 = (f32[256,1024]{1,0:T(8,128)S(1)}, f32[256,1024]{1,0:T(8,128)S(1)}) custom-call(bf16[256,256]{1,0:T(8,128)(2,1)S(1)} %get-tuple-element.80.refs_0_, f32[4]{0:T(128)S(1)} %get-tuple-element.54.refs_0_.refs_1_, f32[128,1024]{1,0:T(8,128)S(1)} %bitcast.7, f32[128,1024]{1,0:T(8,128)S(1)} %collective-permute-done.1.refs_1_.refs_2_.refs_3_), custom_call_target="tpu_custom_call" | custom-call | flops 104857600 | bytes 3145744 | tf_op jit(solution)/shard_map/phases/pallas_call | solution.py:347
  67.1 2.0 %collective-permute-start.15 = (bf16[256,256]{1,0:T(8,128)(2,1)S(1)}, bf16[256,256]{1,0:T(8,128)(2,1)S(1)}, u32[]{:S(2)}, u32[]{:S(2)}) collective-permute-start(bf16[256,256]{1,0:T(8,128)(2,1)S(1)} %get-tuple-element.83), channel_id=1, source_target_pairs={{0,12},{2,14},{4,8},{6,10},{8,20},{10,22},{12,16},{14,18},{16,28},... | collective-permute-start | bytes 393224 | tf_op jit(solution)/shard_map/ppermute | solution.py:410
  69.1 5.0 %collective-permute-done.21.refs_9_ = bf16[256,256]{1,0:T(8,128)(2,1)S(1)} collective-permute-done((bf16[256,256]{1,0:T(8,128)(2,1)S(1)}, bf16[256,256]{1,0:T(8,128)(2,1)S(1)}, u32[]{:S(2)}, u32[]{:S(2)}) %collective-permute-start.21) | collective-permute-done | bytes 131104 | tf_op jit(solution)/shard_map/ppermute | solution.py:410
  75.1 1.8 %collective-permute-start.24 = (bf16[256,256]{1,0:T(8,128)(2,1)S(1)}, bf16[256,256]{1,0:T(8,128)(2,1)S(1)}, u32[]{:S(2)}, u32[]{:S(2)}) collective-permute-start(bf16[256,256]{1,0:T(8,128)(2,1)S(1)} %get-tuple-element.95), channel_id=1, source_target_pairs={{0,4},{2,6},{4,0},{6,2},{1,5},{3,7},{5,1},{7,3},{8,12},{10,14},{12... | collective-permute-start | bytes 393224 | tf_op jit(solution)/shard_map/ppermute | solution.py:413
  77.1 9.2 %collective-permute-done.16.refs_7_ = bf16[256,256]{1,0:T(8,128)(2,1)S(1)} collective-permute-done((bf16[256,256]{1,0:T(8,128)(2,1)S(1)}, bf16[256,256]{1,0:T(8,128)(2,1)S(1)}, u32[]{:S(2)}, u32[]{:S(2)}) %collective-permute-start.16) | collective-permute-done | bytes 131104 | tf_op jit(solution)/shard_map/ppermute | solution.py:410
  87.4 2.6 %collective-permute-start.28 = (bf16[256,256]{1,0:T(8,128)(2,1)S(1)}, bf16[256,256]{1,0:T(8,128)(2,1)S(1)}, u32[]{:S(2)}, u32[]{:S(2)}) collective-permute-start(bf16[256,256]{1,0:T(8,128)(2,1)S(1)} %get-tuple-element.100), channel_id=1, source_target_pairs={{0,6},{2,4},{4,2},{6,0},{1,7},{3,5},{5,3},{7,1},{8,14},{10,12},{12... | collective-permute-start | bytes 393224 | tf_op jit(solution)/shard_map/ppermute | solution.py:413
  90.9 4.4 %collective-permute-done.25.refs_2_ = bf16[256,256]{1,0:T(8,128)(2,1)S(1)} collective-permute-done((bf16[256,256]{1,0:T(8,128)(2,1)S(1)}, bf16[256,256]{1,0:T(8,128)(2,1)S(1)}, u32[]{:S(2)}, u32[]{:S(2)}) %collective-permute-start.25) | collective-permute-done | bytes 131104 | tf_op jit(solution)/shard_map/ppermute | solution.py:413
  95.4 5.1 %collective-permute-start.19 = (bf16[256,1024]{1,0:T(8,128)(2,1)S(1)}, bf16[256,1024]{1,0:T(8,128)(2,1)S(1)}, u32[]{:S(2)}, u32[]{:S(2)}) collective-permute-start(bf16[256,1024]{1,0:T(8,128)(2,1)S(1)} %other_rows.1), channel_id=1, source_target_pairs={{0,1},{1,0},{2,3},{3,2},{4,5},{5,4},{6,7},{7,6},{8,9},{9,8},{10,11... | collective-permute-start | bytes 1572872 | tf_op jit(solution)/shard_map/ppermute | solution.py:375
  101.0 2.9 %collective-permute-done.28.refs_5_ = bf16[256,256]{1,0:T(8,128)(2,1)S(1)} collective-permute-done((bf16[256,256]{1,0:T(8,128)(2,1)S(1)}, bf16[256,256]{1,0:T(8,128)(2,1)S(1)}, u32[]{:S(2)}, u32[]{:S(2)}) %collective-permute-start.28) | collective-permute-done | bytes 131104 | tf_op jit(solution)/shard_map/ppermute | solution.py:413
  104.3 1.4 %collective-permute-start.30 = (bf16[256,1024]{1,0:T(8,128)(2,1)S(1)}, bf16[256,1024]{1,0:T(8,128)(2,1)S(1)}, u32[]{:S(2)}, u32[]{:S(2)}) collective-permute-start(bf16[256,1024]{1,0:T(8,128)(2,1)S(1)} %half_space.3), channel_id=1, source_target_pairs={{0,1},{1,0},{2,3},{3,2},{4,5},{5,4},{6,7},{7,6},{8,9},{9,8},{10,11... | collective-permute-start | bytes 1572872 | tf_op jit(solution)/shard_map/ppermute | solution.py:375
  107.2 1.3 %finish.1 = (bf16[512,1024]{1,0:T(8,128)(2,1)}, f32[128,1024]{1,0:T(8,128)}) custom-call(bf16[512,1024]{1,0:T(8,128)(2,1)S(1)} %get-tuple-element.78.refs_1_.refs_0_, bf16[256,1024]{1,0:T(8,128)(2,1)S(1)} %collective-permute-done.19.refs_1_, bf16[256,1024]{1,0:T(8,128)(2,1)S(1)} %half_space.2.refs_2_, bf16[256,1024]{1,0:T(8,128)(2,1)S(1)} %collective-permute-done.30.refs_3_), custom_call_target="tpu_custom_call" | custom-call | flops 1048576 | bytes 4194304 | tf_op jit(solution)/shard_map/finish/pallas_call | solution.py:347
  (69 shorter events, 16.1 us)
Async XLA Ops:
  0.6 3.8 %collective-permute-start.2 = (bf16[512,1024]{1,0:T(8,128)(2,1)}, bf16[512,1024]{1,0:T(8,128)(2,1)S(1)}, u32[]{:S(2)}, u32[]{:S(2)}) collective-permute-start(bf16[512,1024]{1,0:T(8,128)(2,1)} %bitcast.10), channel_id=1, source_target_pairs={{0,1},{1,0},{2,3},{3,2},{4,5},{5,4},{6,7},{7,6},{8,9},{9,8},{10,11... | collective-permute-start | bytes 3145736 | tf_op jit(solution)/shard_map/ppermute | solution.py:375
  1.4 9.4 %collective-permute-start = (bf16[512,1024]{1,0:T(8,128)(2,1)}, bf16[512,1024]{1,0:T(8,128)(2,1)S(1)}, u32[]{:S(2)}, u32[]{:S(2)}) collective-permute-start(bf16[512,1024]{1,0:T(8,128)(2,1)} %bitcast.8), channel_id=1, source_target_pairs={{0,1},{1,0},{2,3},{3,2},{4,5},{5,4},{6,7},{7,6},{8,9},{9,8},{10,11... | collective-permute-start | bytes 3145736 | tf_op jit(solution)/shard_map/ppermute | solution.py:375
  1.4 9.3 %collective-permute-start.1 = (f32[128,1024]{1,0:T(8,128)}, f32[128,1024]{1,0:T(8,128)S(1)}, u32[]{:S(2)}, u32[]{:S(2)}) collective-permute-start(f32[128,1024]{1,0:T(8,128)} %bitcast.5), channel_id=1, source_target_pairs={{0,1},{1,0},{2,3},{3,2},{4,5},{5,4},{6,7},{7,6},{8,9},{9,8},{10,11... | collective-permute-start | bytes 1572872 | tf_op jit(solution)/shard_map/ppermute | solution.py:375
  5.8 12.1 %collective-permute-start.3 = (bf16[256,256]{1,0:T(8,128)(2,1)S(1)}, bf16[256,256]{1,0:T(8,128)(2,1)S(1)}, u32[]{:S(2)}, u32[]{:S(2)}) collective-permute-start(bf16[256,256]{1,0:T(8,128)(2,1)S(1)} %get-tuple-element.61), channel_id=1, source_target_pairs={{0,4},{2,6},{4,0},{6,2},{1,5},{3,7},{5,1},{7,3},{8,12},{10,14},{12... | collective-permute-start | bytes 393224 | tf_op jit(solution)/shard_map/ppermute | solution.py:413
  8.2 17.2 %collective-permute-start.4 = (bf16[256,256]{1,0:T(8,128)(2,1)S(1)}, bf16[256,256]{1,0:T(8,128)(2,1)S(1)}, u32[]{:S(2)}, u32[]{:S(2)}) collective-permute-start(bf16[256,256]{1,0:T(8,128)(2,1)S(1)} %get-tuple-element.62), channel_id=1, source_target_pairs={{0,6},{2,4},{4,2},{6,0},{1,7},{3,5},{5,3},{7,1},{8,14},{10,12},{12... | collective-permute-start | bytes 393224 | tf_op jit(solution)/shard_map/ppermute | solution.py:413
  8.2 17.2 %collective-permute-start.5 = (bf16[256,256]{1,0:T(8,128)(2,1)S(1)}, bf16[256,256]{1,0:T(8,128)(2,1)S(1)}, u32[]{:S(2)}, u32[]{:S(2)}) collective-permute-start(bf16[256,256]{1,0:T(8,128)(2,1)S(1)} %get-tuple-element.63), channel_id=1, source_target_pairs={{0,2},{2,0},{4,6},{6,4},{1,3},{3,1},{5,7},{7,5},{8,10},{10,8},{12,... | collective-permute-start | bytes 393224 | tf_op jit(solution)/shard_map/ppermute | solution.py:413
  12.7 16.1 %collective-permute-start.9 = (bf16[256,256]{1,0:T(8,128)(2,1)S(1)}, bf16[256,256]{1,0:T(8,128)(2,1)S(1)}, u32[]{:S(2)}, u32[]{:S(2)}) collective-permute-start(bf16[256,256]{1,0:T(8,128)(2,1)S(1)} %get-tuple-element.70), channel_id=1, source_target_pairs={{0,4},{2,6},{4,0},{6,2},{1,5},{3,7},{5,1},{7,3},{8,12},{10,14},{12... | collective-permute-start | bytes 393224 | tf_op jit(solution)/shard_map/ppermute | solution.py:413
  14.2 22.1 %collective-permute-start.10 = (bf16[256,256]{1,0:T(8,128)(2,1)S(1)}, bf16[256,256]{1,0:T(8,128)(2,1)S(1)}, u32[]{:S(2)}, u32[]{:S(2)}) collective-permute-start(bf16[256,256]{1,0:T(8,128)(2,1)S(1)} %get-tuple-element.71), channel_id=1, source_target_pairs={{0,6},{2,4},{4,2},{6,0},{1,7},{3,5},{5,3},{7,1},{8,14},{10,12},{12... | collective-permute-start | bytes 393224 | tf_op jit(solution)/shard_map/ppermute | solution.py:413
  16.1 9.3 %copy-start = (bf16[512,512]{1,0:T(8,128)(2,1)S(1)}, bf16[512,512]{1,0:T(8,128)(2,1)}, u32[]{:S(2)}) copy-start(bf16[512,512]{1,0:T(8,128)(2,1)} %constant.10.clone.refs_6_.refs_4_.refs_5_.refs_2_) | copy-start | bytes 1572868
  17.9 18.4 %collective-permute-start.11 = (bf16[256,256]{1,0:T(8,128)(2,1)S(1)}, bf16[256,256]{1,0:T(8,128)(2,1)S(1)}, u32[]{:S(2)}, u32[]{:S(2)}) collective-permute-start(bf16[256,256]{1,0:T(8,128)(2,1)S(1)} %get-tuple-element.72), channel_id=1, source_target_pairs={{0,2},{2,0},{4,6},{6,4},{1,3},{3,1},{5,7},{7,5},{8,10},{10,8},{12,... | collective-permute-start | bytes 393224 | tf_op jit(solution)/shard_map/ppermute | solution.py:413
  26.5 13.6 %collective-permute-start.6 = (bf16[256,256]{1,0:T(8,128)(2,1)S(1)}, bf16[256,256]{1,0:T(8,128)(2,1)S(1)}, u32[]{:S(2)}, u32[]{:S(2)}) collective-permute-start(bf16[256,256]{1,0:T(8,128)(2,1)S(1)} %get-tuple-element.65), channel_id=1, source_target_pairs={{0,4},{2,6},{4,0},{6,2},{1,5},{3,7},{5,1},{7,3},{8,12},{10,14},{12... | collective-permute-start | bytes 393224 | tf_op jit(solution)/shard_map/ppermute | solution.py:413
  26.5 20.9 %collective-permute-start.7 = (bf16[256,256]{1,0:T(8,128)(2,1)S(1)}, bf16[256,256]{1,0:T(8,128)(2,1)S(1)}, u32[]{:S(2)}, u32[]{:S(2)}) collective-permute-start(bf16[256,256]{1,0:T(8,128)(2,1)S(1)} %get-tuple-element.66), channel_id=1, source_target_pairs={{0,6},{2,4},{4,2},{6,0},{1,7},{3,5},{5,3},{7,1},{8,14},{10,12},{12... | collective-permute-start | bytes 393224 | tf_op jit(solution)/shard_map/ppermute | solution.py:413
  28.8 18.7 %collective-permute-start.8 = (bf16[256,256]{1,0:T(8,128)(2,1)S(1)}, bf16[256,256]{1,0:T(8,128)(2,1)S(1)}, u32[]{:S(2)}, u32[]{:S(2)}) collective-permute-start(bf16[256,256]{1,0:T(8,128)(2,1)S(1)} %get-tuple-element.67), channel_id=1, source_target_pairs={{0,2},{2,0},{4,6},{6,4},{1,3},{3,1},{5,7},{7,5},{8,10},{10,8},{12,... | collective-permute-start | bytes 393224 | tf_op jit(solution)/shard_map/ppermute | solution.py:413
  37.2 13.5 %collective-permute-start.12 = (bf16[256,256]{1,0:T(8,128)(2,1)S(1)}, bf16[256,256]{1,0:T(8,128)(2,1)S(1)}, u32[]{:S(2)}, u32[]{:S(2)}) collective-permute-start(bf16[256,256]{1,0:T(8,128)(2,1)S(1)} %get-tuple-element.74), channel_id=1, source_target_pairs={{0,4},{2,6},{4,0},{6,2},{1,5},{3,7},{5,1},{7,3},{8,12},{10,14},{12... | collective-permute-start | bytes 393224 | tf_op jit(solution)/shard_map/ppermute | solution.py:413
  37.3 16.3 %collective-permute-start.13 = (bf16[256,256]{1,0:T(8,128)(2,1)S(1)}, bf16[256,256]{1,0:T(8,128)(2,1)S(1)}, u32[]{:S(2)}, u32[]{:S(2)}) collective-permute-start(bf16[256,256]{1,0:T(8,128)(2,1)S(1)} %get-tuple-element.75), channel_id=1, source_target_pairs={{0,6},{2,4},{4,2},{6,0},{1,7},{3,5},{5,3},{7,1},{8,14},{10,12},{12... | collective-permute-start | bytes 393224 | tf_op jit(solution)/shard_map/ppermute | solution.py:413
  40.1 13.5 %collective-permute-start.14 = (bf16[256,256]{1,0:T(8,128)(2,1)S(1)}, bf16[256,256]{1,0:T(8,128)(2,1)S(1)}, u32[]{:S(2)}, u32[]{:S(2)}) collective-permute-start(bf16[256,256]{1,0:T(8,128)(2,1)S(1)} %get-tuple-element.76), channel_id=1, source_target_pairs={{0,2},{2,0},{4,6},{6,4},{1,3},{3,1},{5,7},{7,5},{8,10},{10,8},{12,... | collective-permute-start | bytes 393224 | tf_op jit(solution)/shard_map/ppermute | solution.py:413
  55.0 12.0 %collective-permute-start.20 = (bf16[256,256]{1,0:T(8,128)(2,1)S(1)}, bf16[256,256]{1,0:T(8,128)(2,1)S(1)}, u32[]{:S(2)}, u32[]{:S(2)}) collective-permute-start(bf16[256,256]{1,0:T(8,128)(2,1)S(1)} %get-tuple-element.91), channel_id=1, source_target_pairs={{0,12},{2,14},{4,8},{6,10},{8,20},{10,22},{12,16},{14,18},{16,28},... | collective-permute-start | bytes 393224 | tf_op jit(solution)/shard_map/ppermute | solution.py:410
  56.3 17.8 %collective-permute-start.21 = (bf16[256,256]{1,0:T(8,128)(2,1)S(1)}, bf16[256,256]{1,0:T(8,128)(2,1)S(1)}, u32[]{:S(2)}, u32[]{:S(2)}) collective-permute-start(bf16[256,256]{1,0:T(8,128)(2,1)S(1)} %get-tuple-element.92), channel_id=1, source_target_pairs={{0,14},{2,12},{4,10},{6,8},{8,22},{10,20},{12,18},{14,16},{16,30},... | collective-permute-start | bytes 393224 | tf_op jit(solution)/shard_map/ppermute | solution.py:410
  58.3 15.9 %collective-permute-start.22 = (bf16[256,256]{1,0:T(8,128)(2,1)S(1)}, bf16[256,256]{1,0:T(8,128)(2,1)S(1)}, u32[]{:S(2)}, u32[]{:S(2)}) collective-permute-start(bf16[256,256]{1,0:T(8,128)(2,1)S(1)} %get-tuple-element.93), channel_id=1, source_target_pairs={{0,10},{2,8},{4,14},{6,12},{8,18},{10,16},{12,22},{14,20},{16,26},... | collective-permute-start | bytes 393224 | tf_op jit(solution)/shard_map/ppermute | solution.py:410
  61.4 12.7 %collective-permute-start.23 = (bf16[256,256]{1,0:T(8,128)(2,1)S(1)}, bf16[256,256]{1,0:T(8,128)(2,1)S(1)}, u32[]{:S(2)}, u32[]{:S(2)}) collective-permute-start(bf16[256,256]{1,0:T(8,128)(2,1)S(1)} %get-tuple-element.94), channel_id=1, source_target_pairs={{0,8},{2,10},{4,12},{6,14},{8,16},{10,18},{12,20},{14,22},{16,24},... | collective-permute-start | bytes 393224 | tf_op jit(solution)/shard_map/ppermute | solution.py:410
  62.2 24.1 %collective-permute-start.18 = (bf16[256,256]{1,0:T(8,128)(2,1)S(1)}, bf16[256,256]{1,0:T(8,128)(2,1)S(1)}, u32[]{:S(2)}, u32[]{:S(2)}) collective-permute-start(bf16[256,256]{1,0:T(8,128)(2,1)S(1)} %get-tuple-element.80.refs_0_), channel_id=1, source_target_pairs={{0,8},{2,10},{4,12},{6,14},{8,16},{10,18},{12,20},{14,22},{16,24},... | collective-permute-start | bytes 393224 | tf_op jit(solution)/shard_map/ppermute | solution.py:410
  67.1 9.9 %collective-permute-start.15 = (bf16[256,256]{1,0:T(8,128)(2,1)S(1)}, bf16[256,256]{1,0:T(8,128)(2,1)S(1)}, u32[]{:S(2)}, u32[]{:S(2)}) collective-permute-start(bf16[256,256]{1,0:T(8,128)(2,1)S(1)} %get-tuple-element.83), channel_id=1, source_target_pairs={{0,12},{2,14},{4,8},{6,10},{8,20},{10,22},{12,16},{14,18},{16,28},... | collective-permute-start | bytes 393224 | tf_op jit(solution)/shard_map/ppermute | solution.py:410
  74.1 12.2 %collective-permute-start.16 = (bf16[256,256]{1,0:T(8,128)(2,1)S(1)}, bf16[256,256]{1,0:T(8,128)(2,1)S(1)}, u32[]{:S(2)}, u32[]{:S(2)}) collective-permute-start(bf16[256,256]{1,0:T(8,128)(2,1)S(1)} %get-tuple-element.84), channel_id=1, source_target_pairs={{0,14},{2,12},{4,10},{6,8},{8,22},{10,20},{12,18},{14,16},{16,30},... | collective-permute-start | bytes 393224 | tf_op jit(solution)/shard_map/ppermute | solution.py:410
  74.1 12.2 %collective-permute-start.17 = (bf16[256,256]{1,0:T(8,128)(2,1)S(1)}, bf16[256,256]{1,0:T(8,128)(2,1)S(1)}, u32[]{:S(2)}, u32[]{:S(2)}) collective-permute-start(bf16[256,256]{1,0:T(8,128)(2,1)S(1)} %get-tuple-element.85), channel_id=1, source_target_pairs={{0,10},{2,8},{4,14},{6,12},{8,18},{10,16},{12,22},{14,20},{16,26},... | collective-permute-start | bytes 393224 | tf_op jit(solution)/shard_map/ppermute | solution.py:410
  75.1 14.8 %collective-permute-start.24 = (bf16[256,256]{1,0:T(8,128)(2,1)S(1)}, bf16[256,256]{1,0:T(8,128)(2,1)S(1)}, u32[]{:S(2)}, u32[]{:S(2)}) collective-permute-start(bf16[256,256]{1,0:T(8,128)(2,1)S(1)} %get-tuple-element.95), channel_id=1, source_target_pairs={{0,4},{2,6},{4,0},{6,2},{1,5},{3,7},{5,1},{7,3},{8,12},{10,14},{12... | collective-permute-start | bytes 393224 | tf_op jit(solution)/shard_map/ppermute | solution.py:413
  77.0 18.4 %collective-permute-start.25 = (bf16[256,256]{1,0:T(8,128)(2,1)S(1)}, bf16[256,256]{1,0:T(8,128)(2,1)S(1)}, u32[]{:S(2)}, u32[]{:S(2)}) collective-permute-start(bf16[256,256]{1,0:T(8,128)(2,1)S(1)} %get-tuple-element.96), channel_id=1, source_target_pairs={{0,6},{2,4},{4,2},{6,0},{1,7},{3,5},{5,3},{7,1},{8,14},{10,12},{12... | collective-permute-start | bytes 393224 | tf_op jit(solution)/shard_map/ppermute | solution.py:413
  86.3 14.2 %collective-permute-start.26 = (bf16[256,256]{1,0:T(8,128)(2,1)S(1)}, bf16[256,256]{1,0:T(8,128)(2,1)S(1)}, u32[]{:S(2)}, u32[]{:S(2)}) collective-permute-start(bf16[256,256]{1,0:T(8,128)(2,1)S(1)} %get-tuple-element.97), channel_id=1, source_target_pairs={{0,2},{2,0},{4,6},{6,4},{1,3},{3,1},{5,7},{7,5},{8,10},{10,8},{12,... | collective-permute-start | bytes 393224 | tf_op jit(solution)/shard_map/ppermute | solution.py:413
  87.3 13.7 %collective-permute-start.27 = (bf16[256,256]{1,0:T(8,128)(2,1)S(1)}, bf16[256,256]{1,0:T(8,128)(2,1)S(1)}, u32[]{:S(2)}, u32[]{:S(2)}) collective-permute-start(bf16[256,256]{1,0:T(8,128)(2,1)S(1)} %get-tuple-element.99), channel_id=1, source_target_pairs={{0,4},{2,6},{4,0},{6,2},{1,5},{3,7},{5,1},{7,3},{8,12},{10,14},{12... | collective-permute-start | bytes 393224 | tf_op jit(solution)/shard_map/ppermute | solution.py:413
  87.4 16.5 %collective-permute-start.28 = (bf16[256,256]{1,0:T(8,128)(2,1)S(1)}, bf16[256,256]{1,0:T(8,128)(2,1)S(1)}, u32[]{:S(2)}, u32[]{:S(2)}) collective-permute-start(bf16[256,256]{1,0:T(8,128)(2,1)S(1)} %get-tuple-element.100), channel_id=1, source_target_pairs={{0,6},{2,4},{4,2},{6,0},{1,7},{3,5},{5,3},{7,1},{8,14},{10,12},{12... | collective-permute-start | bytes 393224 | tf_op jit(solution)/shard_map/ppermute | solution.py:413
  90.0 13.9 %collective-permute-start.29 = (bf16[256,256]{1,0:T(8,128)(2,1)S(1)}, bf16[256,256]{1,0:T(8,128)(2,1)S(1)}, u32[]{:S(2)}, u32[]{:S(2)}) collective-permute-start(bf16[256,256]{1,0:T(8,128)(2,1)S(1)} %get-tuple-element.101), channel_id=1, source_target_pairs={{0,2},{2,0},{4,6},{6,4},{1,3},{3,1},{5,7},{7,5},{8,10},{10,8},{12,... | collective-permute-start | bytes 393224 | tf_op jit(solution)/shard_map/ppermute | solution.py:413
  95.4 10.8 %collective-permute-start.19 = (bf16[256,1024]{1,0:T(8,128)(2,1)S(1)}, bf16[256,1024]{1,0:T(8,128)(2,1)S(1)}, u32[]{:S(2)}, u32[]{:S(2)}) collective-permute-start(bf16[256,1024]{1,0:T(8,128)(2,1)S(1)} %other_rows.1), channel_id=1, source_target_pairs={{0,1},{1,0},{2,3},{3,2},{4,5},{5,4},{6,7},{7,6},{8,9},{9,8},{10,11... | collective-permute-start | bytes 1572872 | tf_op jit(solution)/shard_map/ppermute | solution.py:375
  104.3 2.9 %collective-permute-start.30 = (bf16[256,1024]{1,0:T(8,128)(2,1)S(1)}, bf16[256,1024]{1,0:T(8,128)(2,1)S(1)}, u32[]{:S(2)}, u32[]{:S(2)}) collective-permute-start(bf16[256,1024]{1,0:T(8,128)(2,1)S(1)} %half_space.3), channel_id=1, source_target_pairs={{0,1},{1,0},{2,3},{3,2},{4,5},{5,4},{6,7},{7,6},{8,9},{9,8},{10,11... | collective-permute-start | bytes 1572872 | tf_op jit(solution)/shard_map/ppermute | solution.py:375
  (8 other events, 35.6 us)

commit v3 on v2

--- a/solution.py
+++ b/solution.py
@@ -150,33 +150,19 @@
             ]
 
 
-def own_modes_kernel(fields_ref, even_ref, odd_ref, evens_ref, odds_ref, held, tables, sems):
-    rows, half = evens_ref.shape
-    copies = [
-        pltpu.make_async_copy(
-            fields_ref.at[rows_of(lax.axis_index("core") * rows, rows), :], held, sems.at[0]
-        ),
-        pltpu.make_async_copy(even_ref, tables.at[0], sems.at[1]),
-        pltpu.make_async_copy(odd_ref, tables.at[1], sems.at[2]),
-    ]
-    for copy in copies:
-        copy.start()
-    copies[0].wait()
-    low, high = held[:, :half], held[:, half:]
-    copies[1].wait()
-    evens_ref[...] = dot(low + high, tables[0]).astype(BF16)
-    copies[2].wait()
-    odds_ref[...] = dot(low - high, tables[1]).astype(BF16)
-
-
-def to_modes_kernel(odd, other_ref, own_ref, table_ref, *refs):
+def own_modes_kernel(fields_ref, table_ref, out_ref):
+    rows, half = out_ref.shape
+    mine = rows_of(lax.axis_index("core") * rows, rows)
+    out_ref[...] = dot(fields_ref[mine, :half] + fields_ref[mine, half:], table_ref[...]).astype(BF16)
+
+
+def even_to_modes_kernel(other_ref, own_ref, table_ref, *refs):
     outs, modes = refs[:-1], refs[-1]
     rows, half = own_ref.shape
     own = rows // 2
     core = lax.axis_index("core")
     theirs = rows_of(core * rows, rows)
-    low, high = other_ref[theirs, :half], other_ref[theirs, half:]
-    modes[...] = dot(low - high if odd else low + high, table_ref[...]).astype(BF16)
+    modes[...] = dot(other_ref[theirs, :half] + other_ref[theirs, half:], table_ref[...]).astype(BF16)
     block = half // len(outs)
     for k, out in zip(partners(len(outs)), outs):
         columns = rows_of((lax.axis_index("z") ^ k) * block, block)
@@ -187,15 +173,29 @@
             out[rows_of((core ^ 1) * own, own), lanes] = modes[lines, columns]
 
 
+def odd_pieces(fields_ref, other_ref, table_ref, *refs):
+    outs, (folded, modes) = refs[:-2], refs[-2:]
+    half = table_ref.shape[0]
+    own = folded.shape[0] // 4
+    core = lax.axis_index("core")
+    for part in range(2):
+        mine = rows_of((2 * core + part) * own, own)
+        for index, source in enumerate((fields_ref, other_ref)):
+            there = rows_of(2 * part * own + (core ^ index) * own, own)
+            folded[there, :] = source[mine, :half] - source[mine, half:]
+    modes[...] = dot(folded[...], table_ref[...]).astype(BF16)
+    split_modes(lax.axis_index("z"), modes, outs)
+
+
 def odd_to_modes_kernel(blocks_ref, top_block_ref, reference_ref, *refs):
-    settings_ref = refs[-2]
+    settings_ref = refs[-3]
     depth = lax.axis_index("depth")
     above = blocks_ref[jnp.maximum(depth - 1, 0)]
     second = jnp.where(depth == 0, top_block_ref[0], above)
     for index, block in enumerate((blocks_ref[depth], second)):
         settings_ref[2 * index] = omega_top * (block.astype(F32) + 1.0) / NFREQ
         settings_ref[2 * index + 1] = reference_ref[0]
-    to_modes_kernel(1, *refs[:-2], refs[-1])
+    odd_pieces(*refs[:-3], *refs[-2:])
 
 
 def along_x_kernel(
@@ -425,22 +425,17 @@
         )[0]
 
     share = (rows, half)
-    own_evens, own_odds = call(
-        own_modes_kernel, (fields, even_y_t, odd_y_t), [of(share)] * 2,
-        [
-            pltpu.VMEM((rows, length_y), BF16), pltpu.VMEM((2, half, half), BF16),
-            pltpu.SemaphoreType.DMA((3,)),
-        ],
-        flops, "own_modes", ins=[HBM] * 3, grant=58,
-    )
+    own_evens = call(
+        own_modes_kernel, (fields, even_y_t), [of(share)], flops=flops // 2, name="own_modes"
+    )[0]
     evens = call(
-        functools.partial(to_modes_kernel, 0), (fields_other, own_evens, even_y_t),
+        even_to_modes_kernel, (fields_other, own_evens, even_y_t),
         pieces_of, [pltpu.VMEM(share, BF16)], flops // 2, "even_to_modes",
     )
     *odds, settings = call(
         odd_to_modes_kernel,
-        (flight_blocks, top_block, ref_slowness, fields_other, own_odds, odd_y_t),
-        pieces_of + [of((4,), F32)], [pltpu.VMEM(share, BF16)], flops // 2, "odd_to_modes",
+        (flight_blocks, top_block, ref_slowness, fields, fields_other, odd_y_t),
+        pieces_of + [of((4,), F32)], [part, part], flops, "odd_to_modes",
         scalars=3, behind=(top_other, other), puts=[VMEM] * chips + [SMEM],
     )
     even_factors, odd_factors = factors(0, 0, ()), factors(0, 1, ())

time: 109 us -> 109 us (level)
  Pallas kernels: 20.7 us -> 18.4 us
  starting transfers between devices: 37.9 us -> 39 us
    pallas_call x21, Pallas kernels: 20.7 us -> 18.4 us  [call(): pl.pallas_call(functools.partial(after, len(behind), kernel), out_shape=t...]
    ppermute x18, waiting for transfers between devices: 30.8 us -> 28.7 us  [exchange(): got.append(lax.ppermute(piece, 'z', pairs) if k else piece)]
    ppermute x8, waiting for transfers between devices: 14.2 us -> 15.7 us  [exchange(): got.append(lax.ppermute(piece, ('depth', 'z'), pairs))]
    unnamed x18 -> x20, local copies, waits for them, and re-layouts: 1.59 us -> 2.32 us
  transfers between devices with their start and end apart: 31 -> 31, of which waited for: 10 -> 10; matrix products, arithmetic and copies ran while one was open for 0% -> 0% of each run, Pallas kernels for 17% -> 15%
where the time goes in v3:
time: 109 us; the launch traced here: 107 us
  waiting for transfers between devices  45.5 us (42%)
  starting transfers between devices  39 us (36%)
  Pallas kernels  18.4 us (17%)
  local copies, waits for them, and re-layouts  2.32 us (2%)
  between operations  2.27 us (2%)
    ppermute x18, waiting for transfers between devices, exchange(): got.append(lax.ppermute(piece, 'z', pairs) if k else piece)  28.7 us
    ppermute x18, starting transfers between devices, exchange(): got.append(lax.ppermute(piece, 'z', pairs) if k else piece)  20.5 us
    pallas_call x21, Pallas kernels, call(): pl.pallas_call(functools.partial(after, len(behind), kernel), out_shape=t...  18.4 us
    ppermute x8, waiting for transfers between devices, exchange(): got.append(lax.ppermute(piece, ('depth', 'z'), pairs))  15.7 us
    ppermute x8, starting transfers between devices, exchange(): got.append(lax.ppermute(piece, ('depth', 'z'), pairs))  9.84 us
    ppermute x5, starting transfers between devices, other_core(): return lax.ppermute(value, 'core', [(0, 1), (1, 0)])  8.72 us
    unnamed x20, local copies, waits for them, and re-layouts  2.32 us
  transfers between devices with their start and end apart: 31, of which 10 were waited for; matrix products, arithmetic and copies ran while one was open for 0% of the time, Pallas kernels for 15%

profile of v3, /device:TPU:9, one launch (start us, length us, event | category | flops | bytes accessed | tf_op | source)
XLA Modules:
  0.0 107.5 jit_solution(2941159346960967082)
XLA Ops:
  2.9 1.2 %copy-done.5 = bf16[1,2,2,128,1024]{4,3,2,1,0:T(8,128)(2,1)S(1)} copy-done((bf16[1,2,2,128,1024]{4,3,2,1,0:T(8,128)(2,1)S(1)}, bf16[1,2,2,128,1024]{4,3,2,1,0:T(8,128)(2,1)}, u32[]{:S(2)}) %copy-start.5) | copy-done | bytes 1048600
  4.9 2.4 %collective-permute-start.3 = (bf16[256,256]{1,0:T(8,128)(2,1)S(1)}, bf16[256,256]{1,0:T(8,128)(2,1)S(1)}, u32[]{:S(2)}, u32[]{:S(2)}) collective-permute-start(bf16[256,256]{1,0:T(8,128)(2,1)S(1)} %get-tuple-element.57), channel_id=1, source_target_pairs={{0,4},{2,6},{4,0},{6,2},{1,5},{3,7},{5,1},{7,3},{8,12},{10,14},{12... | collective-permute-start | bytes 393224 | tf_op jit(solution)/shard_map/ppermute | solution.py:413
  7.3 1.2 %collective-permute-start.5 = (bf16[256,256]{1,0:T(8,128)(2,1)S(1)}, bf16[256,256]{1,0:T(8,128)(2,1)S(1)}, u32[]{:S(2)}, u32[]{:S(2)}) collective-permute-start(bf16[256,256]{1,0:T(8,128)(2,1)S(1)} %get-tuple-element.59), channel_id=1, source_target_pairs={{0,2},{2,0},{4,6},{6,4},{1,3},{3,1},{5,7},{7,5},{8,10},{10,8},{12,... | collective-permute-start | bytes 393224 | tf_op jit(solution)/shard_map/ppermute | solution.py:413
  9.9 1.2 %odd_to_modes.1 = (bf16[256,256]{1,0:T(8,128)(2,1)S(1)}, bf16[256,256]{1,0:T(8,128)(2,1)S(1)}, bf16[256,256]{1,0:T(8,128)(2,1)S(1)}, bf16[256,256]{1,0:T(8,128)(2,1)S(1)}, f32[4]{0:T(128)S(1)}) custom-call(bf16[512,1024]{1,0:T(8,128)(2,1)S(1)} %collective-permute-done.refs_0_.refs_3_, f32[128,1024]{1,0:T(8,128)S(1)} %collective-permute-done.1.refs_1_.refs_2_.refs_3_, ...), custom_call_target="tpu_custom_call" | custom-call | flops 268435456 | bytes 3145768 | tf_op jit(solution)/shard_map/odd_to_modes/pallas_call | solution.py:347
  11.2 1.5 %collective-permute-start.9 = (bf16[256,256]{1,0:T(8,128)(2,1)S(1)}, bf16[256,256]{1,0:T(8,128)(2,1)S(1)}, u32[]{:S(2)}, u32[]{:S(2)}) collective-permute-start(bf16[256,256]{1,0:T(8,128)(2,1)S(1)} %get-tuple-element.66), channel_id=1, source_target_pairs={{0,4},{2,6},{4,0},{6,2},{1,5},{3,7},{5,1},{7,3},{8,12},{10,14},{12... | collective-permute-start | bytes 393224 | tf_op jit(solution)/shard_map/ppermute | solution.py:413
  14.6 1.7 %phases.2 = (f32[256,1024]{1,0:T(8,128)S(1)}, f32[256,1024]{1,0:T(8,128)S(1)}) custom-call(f32[4]{0:T(128)S(1)} %get-tuple-element.51.refs_0_.refs_1_, f32[128,1024]{1,0:T(8,128)S(1)} %bitcast.9, f32[128,1024]{1,0:T(8,128)S(1)} %collective-permute-done.1.refs_1_.refs_2_.refs_3_), custom_call_target="tpu_custom_call" | custom-call | flops 104857600 | bytes 3145744 | tf_op jit(solution)/shard_map/phases/pallas_call | solution.py:347
  16.3 2.2 %collective-permute-start.11 = (bf16[256,256]{1,0:T(8,128)(2,1)S(1)}, bf16[256,256]{1,0:T(8,128)(2,1)S(1)}, u32[]{:S(2)}, u32[]{:S(2)}) collective-permute-start(bf16[256,256]{1,0:T(8,128)(2,1)S(1)} %get-tuple-element.68), channel_id=1, source_target_pairs={{0,2},{2,0},{4,6},{6,4},{1,3},{3,1},{5,7},{7,5},{8,10},{10,8},{12,... | collective-permute-start | bytes 393224 | tf_op jit(solution)/shard_map/ppermute | solution.py:413
  18.6 6.0 %collective-permute-done.4.refs_9_ = bf16[256,256]{1,0:T(8,128)(2,1)S(1)} collective-permute-done((bf16[256,256]{1,0:T(8,128)(2,1)S(1)}, bf16[256,256]{1,0:T(8,128)(2,1)S(1)}, u32[]{:S(2)}, u32[]{:S(2)}) %collective-permute-start.4) | collective-permute-done | bytes 131104 | tf_op jit(solution)/shard_map/ppermute | solution.py:413
  25.6 2.3 %collective-permute-start.7 = (bf16[256,256]{1,0:T(8,128)(2,1)S(1)}, bf16[256,256]{1,0:T(8,128)(2,1)S(1)}, u32[]{:S(2)}, u32[]{:S(2)}) collective-permute-start(bf16[256,256]{1,0:T(8,128)(2,1)S(1)} %get-tuple-element.62), channel_id=1, source_target_pairs={{0,6},{2,4},{4,2},{6,0},{1,7},{3,5},{5,3},{7,1},{8,14},{10,12},{12... | collective-permute-start | bytes 393224 | tf_op jit(solution)/shard_map/ppermute | solution.py:413
  27.9 1.3 %collective-permute-start.8 = (bf16[256,256]{1,0:T(8,128)(2,1)S(1)}, bf16[256,256]{1,0:T(8,128)(2,1)S(1)}, u32[]{:S(2)}, u32[]{:S(2)}) collective-permute-start(bf16[256,256]{1,0:T(8,128)(2,1)S(1)} %get-tuple-element.63), channel_id=1, source_target_pairs={{0,2},{2,0},{4,6},{6,4},{1,3},{3,1},{5,7},{7,5},{8,10},{10,8},{12,... | collective-permute-start | bytes 393224 | tf_op jit(solution)/shard_map/ppermute | solution.py:413
  29.1 6.1 %collective-permute-done.10.refs_7_ = bf16[256,256]{1,0:T(8,128)(2,1)S(1)} collective-permute-done((bf16[256,256]{1,0:T(8,128)(2,1)S(1)}, bf16[256,256]{1,0:T(8,128)(2,1)S(1)}, u32[]{:S(2)}, u32[]{:S(2)}) %collective-permute-start.10) | collective-permute-done | bytes 131104 | tf_op jit(solution)/shard_map/ppermute | solution.py:413
  36.3 2.8 %collective-permute-start.13 = (bf16[256,256]{1,0:T(8,128)(2,1)S(1)}, bf16[256,256]{1,0:T(8,128)(2,1)S(1)}, u32[]{:S(2)}, u32[]{:S(2)}) collective-permute-start(bf16[256,256]{1,0:T(8,128)(2,1)S(1)} %get-tuple-element.71), channel_id=1, source_target_pairs={{0,6},{2,4},{4,2},{6,0},{1,7},{3,5},{5,3},{7,1},{8,14},{10,12},{12... | collective-permute-start | bytes 393224 | tf_op jit(solution)/shard_map/ppermute | solution.py:413
  39.1 1.1 %collective-permute-start.14 = (bf16[256,256]{1,0:T(8,128)(2,1)S(1)}, bf16[256,256]{1,0:T(8,128)(2,1)S(1)}, u32[]{:S(2)}, u32[]{:S(2)}) collective-permute-start(bf16[256,256]{1,0:T(8,128)(2,1)S(1)} %get-tuple-element.72), channel_id=1, source_target_pairs={{0,2},{2,0},{4,6},{6,4},{1,3},{3,1},{5,7},{7,5},{8,10},{10,8},{12,... | collective-permute-start | bytes 393224 | tf_op jit(solution)/shard_map/ppermute | solution.py:413
  40.2 6.3 %collective-permute-done.7.refs_2_ = bf16[256,256]{1,0:T(8,128)(2,1)S(1)} collective-permute-done((bf16[256,256]{1,0:T(8,128)(2,1)S(1)}, bf16[256,256]{1,0:T(8,128)(2,1)S(1)}, u32[]{:S(2)}, u32[]{:S(2)}) %collective-permute-start.7) | collective-permute-done | bytes 131104 | tf_op jit(solution)/shard_map/ppermute | solution.py:413
  47.0 2.8 %collective-permute-done.12.refs_7_ = bf16[256,256]{1,0:T(8,128)(2,1)S(1)} collective-permute-done((bf16[256,256]{1,0:T(8,128)(2,1)S(1)}, bf16[256,256]{1,0:T(8,128)(2,1)S(1)}, u32[]{:S(2)}, u32[]{:S(2)}) %collective-permute-start.12) | collective-permute-done | bytes 131104 | tf_op jit(solution)/shard_map/ppermute | solution.py:413
  49.8 2.8 %collective-permute-done.13.refs_8_ = bf16[256,256]{1,0:T(8,128)(2,1)S(1)} collective-permute-done((bf16[256,256]{1,0:T(8,128)(2,1)S(1)}, bf16[256,256]{1,0:T(8,128)(2,1)S(1)}, u32[]{:S(2)}, u32[]{:S(2)}) %collective-permute-start.13) | collective-permute-done | bytes 131104 | tf_op jit(solution)/shard_map/ppermute | solution.py:413
  52.6 1.4 %turn_around.1 = (bf16[256,256]{1,0:T(8,128)(2,1)S(1)}, bf16[256,256]{1,0:T(8,128)(2,1)S(1)}, bf16[256,256]{1,0:T(8,128)(2,1)S(1)}, bf16[256,256]{1,0:T(8,128)(2...) custom-call(f32[256,1024]{1,0:T(8,128)S(1)} %get-tuple-element.52.refs_1_.refs_0_, ...), custom_call_target="tpu_custom_call" | custom-call | flops 536870912 | bytes 8912896 | tf_op jit(solution)/shard_map/turn_around/pallas_call | solution.py:347
  54.1 1.3 %collective-permute-start.20 = (bf16[256,256]{1,0:T(8,128)(2,1)S(1)}, bf16[256,256]{1,0:T(8,128)(2,1)S(1)}, u32[]{:S(2)}, u32[]{:S(2)}) collective-permute-start(bf16[256,256]{1,0:T(8,128)(2,1)S(1)} %get-tuple-element.87), channel_id=1, source_target_pairs={{0,12},{2,14},{4,8},{6,10},{8,20},{10,22},{12,16},{14,18},{16,28},... | collective-permute-start | bytes 393224 | tf_op jit(solution)/shard_map/ppermute | solution.py:410
  55.4 2.0 %collective-permute-start.21 = (bf16[256,256]{1,0:T(8,128)(2,1)S(1)}, bf16[256,256]{1,0:T(8,128)(2,1)S(1)}, u32[]{:S(2)}, u32[]{:S(2)}) collective-permute-start(bf16[256,256]{1,0:T(8,128)(2,1)S(1)} %get-tuple-element.88), channel_id=1, source_target_pairs={{0,14},{2,12},{4,10},{6,8},{8,22},{10,20},{12,18},{14,16},{16,30},... | collective-permute-start | bytes 393224 | tf_op jit(solution)/shard_map/ppermute | solution.py:410
  57.3 3.2 %collective-permute-start.22 = (bf16[256,256]{1,0:T(8,128)(2,1)S(1)}, bf16[256,256]{1,0:T(8,128)(2,1)S(1)}, u32[]{:S(2)}, u32[]{:S(2)}) collective-permute-start(bf16[256,256]{1,0:T(8,128)(2,1)S(1)} %get-tuple-element.89), channel_id=1, source_target_pairs={{0,10},{2,8},{4,14},{6,12},{8,18},{10,16},{12,22},{14,20},{16,26},... | collective-permute-start | bytes 393224 | tf_op jit(solution)/shard_map/ppermute | solution.py:410
  61.2 1.3 %collective-permute-start.18 = (bf16[256,256]{1,0:T(8,128)(2,1)S(1)}, bf16[256,256]{1,0:T(8,128)(2,1)S(1)}, u32[]{:S(2)}, u32[]{:S(2)}) collective-permute-start(bf16[256,256]{1,0:T(8,128)(2,1)S(1)} %get-tuple-element.76.refs_0_), channel_id=1, source_target_pairs={{0,8},{2,10},{4,12},{6,14},{8,16},{10,18},{12,20},{14,22},{16,24},... | collective-permute-start | bytes 393224 | tf_op jit(solution)/shard_map/ppermute | solution.py:410
  64.4 1.7 %phases.3 = (f32[256,1024]{1,0:T(8,128)S(1)}, f32[256,1024]{1,0:T(8,128)S(1)}) custom-call(bf16[256,256]{1,0:T(8,128)(2,1)S(1)} %get-tuple-element.76.refs_0_, f32[4]{0:T(128)S(1)} %get-tuple-element.51.refs_0_.refs_1_, f32[128,1024]{1,0:T(8,128)S(1)} %bitcast.10, f32[128,1024]{1,0:T(8,128)S(1)} %collective-permute-done.1.refs_1_.refs_2_.refs_3_), custom_call_target="tpu_custom_call" | custom-call | flops 104857600 | bytes 3145744 | tf_op jit(solution)/shard_map/phases/pallas_call | solution.py:347
  66.1 2.0 %collective-permute-start.15 = (bf16[256,256]{1,0:T(8,128)(2,1)S(1)}, bf16[256,256]{1,0:T(8,128)(2,1)S(1)}, u32[]{:S(2)}, u32[]{:S(2)}) collective-permute-start(bf16[256,256]{1,0:T(8,128)(2,1)S(1)} %get-tuple-element.79), channel_id=1, source_target_pairs={{0,12},{2,14},{4,8},{6,10},{8,20},{10,22},{12,16},{14,18},{16,28},... | collective-permute-start | bytes 393224 | tf_op jit(solution)/shard_map/ppermute | solution.py:410
  68.1 5.1 %collective-permute-done.21.refs_9_ = bf16[256,256]{1,0:T(8,128)(2,1)S(1)} collective-permute-done((bf16[256,256]{1,0:T(8,128)(2,1)S(1)}, bf16[256,256]{1,0:T(8,128)(2,1)S(1)}, u32[]{:S(2)}, u32[]{:S(2)}) %collective-permute-start.21) | collective-permute-done | bytes 131104 | tf_op jit(solution)/shard_map/ppermute | solution.py:410
  74.3 1.8 %collective-permute-start.24 = (bf16[256,256]{1,0:T(8,128)(2,1)S(1)}, bf16[256,256]{1,0:T(8,128)(2,1)S(1)}, u32[]{:S(2)}, u32[]{:S(2)}) collective-permute-start(bf16[256,256]{1,0:T(8,128)(2,1)S(1)} %get-tuple-element.91), channel_id=1, source_target_pairs={{0,4},{2,6},{4,0},{6,2},{1,5},{3,7},{5,1},{7,3},{8,12},{10,14},{12... | collective-permute-start | bytes 393224 | tf_op jit(solution)/shard_map/ppermute | solution.py:413
  76.2 10.6 %collective-permute-done.16.refs_7_ = bf16[256,256]{1,0:T(8,128)(2,1)S(1)} collective-permute-done((bf16[256,256]{1,0:T(8,128)(2,1)S(1)}, bf16[256,256]{1,0:T(8,128)(2,1)S(1)}, u32[]{:S(2)}, u32[]{:S(2)}) %collective-permute-start.16) | collective-permute-done | bytes 131104 | tf_op jit(solution)/shard_map/ppermute | solution.py:410
  88.0 2.6 %collective-permute-start.28 = (bf16[256,256]{1,0:T(8,128)(2,1)S(1)}, bf16[256,256]{1,0:T(8,128)(2,1)S(1)}, u32[]{:S(2)}, u32[]{:S(2)}) collective-permute-start(bf16[256,256]{1,0:T(8,128)(2,1)S(1)} %get-tuple-element.96), channel_id=1, source_target_pairs={{0,6},{2,4},{4,2},{6,0},{1,7},{3,5},{5,3},{7,1},{8,14},{10,12},{12... | collective-permute-start | bytes 393224 | tf_op jit(solution)/shard_map/ppermute | solution.py:413
  91.6 6.3 %collective-permute-start.19 = (bf16[256,1024]{1,0:T(8,128)(2,1)S(1)}, bf16[256,1024]{1,0:T(8,128)(2,1)S(1)}, u32[]{:S(2)}, u32[]{:S(2)}) collective-permute-start(bf16[256,1024]{1,0:T(8,128)(2,1)S(1)} %other_rows.1), channel_id=1, source_target_pairs={{0,1},{1,0},{2,3},{3,2},{4,5},{5,4},{6,7},{7,6},{8,9},{9,8},{10,11... | collective-permute-start | bytes 1572872 | tf_op jit(solution)/shard_map/ppermute | solution.py:375
  98.8 4.2 %collective-permute-done.28.refs_5_ = bf16[256,256]{1,0:T(8,128)(2,1)S(1)} collective-permute-done((bf16[256,256]{1,0:T(8,128)(2,1)S(1)}, bf16[256,256]{1,0:T(8,128)(2,1)S(1)}, u32[]{:S(2)}, u32[]{:S(2)}) %collective-permute-start.28) | collective-permute-done | bytes 131104 | tf_op jit(solution)/shard_map/ppermute | solution.py:413
  103.4 1.2 %collective-permute-start.30 = (bf16[256,1024]{1,0:T(8,128)(2,1)S(1)}, bf16[256,1024]{1,0:T(8,128)(2,1)S(1)}, u32[]{:S(2)}, u32[]{:S(2)}) collective-permute-start(bf16[256,1024]{1,0:T(8,128)(2,1)S(1)} %half_space.3), channel_id=1, source_target_pairs={{0,1},{1,0},{2,3},{3,2},{4,5},{5,4},{6,7},{7,6},{8,9},{9,8},{10,11... | collective-permute-start | bytes 1572872 | tf_op jit(solution)/shard_map/ppermute | solution.py:375
  105.1 1.1 collective-permute-done.30.refs_3_
  106.2 1.3 %finish.1 = (bf16[512,1024]{1,0:T(8,128)(2,1)}, f32[128,1024]{1,0:T(8,128)}) custom-call(bf16[512,1024]{1,0:T(8,128)(2,1)S(1)} %get-tuple-element.74.refs_1_.refs_0_, bf16[256,1024]{1,0:T(8,128)(2,1)S(1)} %collective-permute-done.19.refs_1_, bf16[256,1024]{1,0:T(8,128)(2,1)S(1)} %half_space.2.refs_2_, bf16[256,1024]{1,0:T(8,128)(2,1)S(1)} %collective-permute-done.30.refs_3_), custom_call_target="tpu_custom_call" | custom-call | flops 1048576 | bytes 4194304 | tf_op jit(solution)/shard_map/finish/pallas_call | solution.py:347
  (71 shorter events, 15.3 us)
Async XLA Ops:
  0.6 3.9 %collective-permute-start.2 = (bf16[512,1024]{1,0:T(8,128)(2,1)}, bf16[512,1024]{1,0:T(8,128)(2,1)S(1)}, u32[]{:S(2)}, u32[]{:S(2)}) collective-permute-start(bf16[512,1024]{1,0:T(8,128)(2,1)} %bitcast.5), channel_id=1, source_target_pairs={{0,1},{1,0},{2,3},{3,2},{4,5},{5,4},{6,7},{7,6},{8,9},{9,8},{10,11... | collective-permute-start | bytes 3145736 | tf_op jit(solution)/shard_map/ppermute | solution.py:375
  1.4 8.5 %collective-permute-start = (bf16[512,1024]{1,0:T(8,128)(2,1)}, bf16[512,1024]{1,0:T(8,128)(2,1)S(1)}, u32[]{:S(2)}, u32[]{:S(2)}) collective-permute-start(bf16[512,1024]{1,0:T(8,128)(2,1)} %bitcast.11), channel_id=1, source_target_pairs={{0,1},{1,0},{2,3},{3,2},{4,5},{5,4},{6,7},{7,6},{8,9},{9,8},{10,11... | collective-permute-start | bytes 3145736 | tf_op jit(solution)/shard_map/ppermute | solution.py:375
  1.5 8.4 %collective-permute-start.1 = (f32[128,1024]{1,0:T(8,128)}, f32[128,1024]{1,0:T(8,128)S(1)}, u32[]{:S(2)}, u32[]{:S(2)}) collective-permute-start(f32[128,1024]{1,0:T(8,128)} %bitcast.8), channel_id=1, source_target_pairs={{0,1},{1,0},{2,3},{3,2},{4,5},{5,4},{6,7},{7,6},{8,9},{9,8},{10,11... | collective-permute-start | bytes 1572872 | tf_op jit(solution)/shard_map/ppermute | solution.py:375
  4.9 11.5 %collective-permute-start.3 = (bf16[256,256]{1,0:T(8,128)(2,1)S(1)}, bf16[256,256]{1,0:T(8,128)(2,1)S(1)}, u32[]{:S(2)}, u32[]{:S(2)}) collective-permute-start(bf16[256,256]{1,0:T(8,128)(2,1)S(1)} %get-tuple-element.57), channel_id=1, source_target_pairs={{0,4},{2,6},{4,0},{6,2},{1,5},{3,7},{5,1},{7,3},{8,12},{10,14},{12... | collective-permute-start | bytes 393224 | tf_op jit(solution)/shard_map/ppermute | solution.py:413
  7.3 17.2 %collective-permute-start.4 = (bf16[256,256]{1,0:T(8,128)(2,1)S(1)}, bf16[256,256]{1,0:T(8,128)(2,1)S(1)}, u32[]{:S(2)}, u32[]{:S(2)}) collective-permute-start(bf16[256,256]{1,0:T(8,128)(2,1)S(1)} %get-tuple-element.58), channel_id=1, source_target_pairs={{0,6},{2,4},{4,2},{6,0},{1,7},{3,5},{5,3},{7,1},{8,14},{10,12},{12... | collective-permute-start | bytes 393224 | tf_op jit(solution)/shard_map/ppermute | solution.py:413
  7.3 17.2 %collective-permute-start.5 = (bf16[256,256]{1,0:T(8,128)(2,1)S(1)}, bf16[256,256]{1,0:T(8,128)(2,1)S(1)}, u32[]{:S(2)}, u32[]{:S(2)}) collective-permute-start(bf16[256,256]{1,0:T(8,128)(2,1)S(1)} %get-tuple-element.59), channel_id=1, source_target_pairs={{0,2},{2,0},{4,6},{6,4},{1,3},{3,1},{5,7},{7,5},{8,10},{10,8},{12,... | collective-permute-start | bytes 393224 | tf_op jit(solution)/shard_map/ppermute | solution.py:413
  9.9 14.6 %copy-start.4 = (bf16[512,512]{1,0:T(8,128)(2,1)S(1)}, bf16[512,512]{1,0:T(8,128)(2,1)}, u32[]{:S(2)}) copy-start(bf16[512,512]{1,0:T(8,128)(2,1)} %constant.8.clone.refs_4_.refs_0_.refs_2_) | copy-start | bytes 1572868
  11.2 16.7 %collective-permute-start.9 = (bf16[256,256]{1,0:T(8,128)(2,1)S(1)}, bf16[256,256]{1,0:T(8,128)(2,1)S(1)}, u32[]{:S(2)}, u32[]{:S(2)}) collective-permute-start(bf16[256,256]{1,0:T(8,128)(2,1)S(1)} %get-tuple-element.66), channel_id=1, source_target_pairs={{0,4},{2,6},{4,0},{6,2},{1,5},{3,7},{5,1},{7,3},{8,12},{10,14},{12... | collective-permute-start | bytes 393224 | tf_op jit(solution)/shard_map/ppermute | solution.py:413
  12.7 22.6 %collective-permute-start.10 = (bf16[256,256]{1,0:T(8,128)(2,1)S(1)}, bf16[256,256]{1,0:T(8,128)(2,1)S(1)}, u32[]{:S(2)}, u32[]{:S(2)}) collective-permute-start(bf16[256,256]{1,0:T(8,128)(2,1)S(1)} %get-tuple-element.67), channel_id=1, source_target_pairs={{0,6},{2,4},{4,2},{6,0},{1,7},{3,5},{5,3},{7,1},{8,14},{10,12},{12... | collective-permute-start | bytes 393224 | tf_op jit(solution)/shard_map/ppermute | solution.py:413
  16.3 18.9 %collective-permute-start.11 = (bf16[256,256]{1,0:T(8,128)(2,1)S(1)}, bf16[256,256]{1,0:T(8,128)(2,1)S(1)}, u32[]{:S(2)}, u32[]{:S(2)}) collective-permute-start(bf16[256,256]{1,0:T(8,128)(2,1)S(1)} %get-tuple-element.68), channel_id=1, source_target_pairs={{0,2},{2,0},{4,6},{6,4},{1,3},{3,1},{5,7},{7,5},{8,10},{10,8},{12,... | collective-permute-start | bytes 393224 | tf_op jit(solution)/shard_map/ppermute | solution.py:413
  25.5 13.5 %collective-permute-start.6 = (bf16[256,256]{1,0:T(8,128)(2,1)S(1)}, bf16[256,256]{1,0:T(8,128)(2,1)S(1)}, u32[]{:S(2)}, u32[]{:S(2)}) collective-permute-start(bf16[256,256]{1,0:T(8,128)(2,1)S(1)} %get-tuple-element.61), channel_id=1, source_target_pairs={{0,4},{2,6},{4,0},{6,2},{1,5},{3,7},{5,1},{7,3},{8,12},{10,14},{12... | collective-permute-start | bytes 393224 | tf_op jit(solution)/shard_map/ppermute | solution.py:413
  25.6 20.9 %collective-permute-start.7 = (bf16[256,256]{1,0:T(8,128)(2,1)S(1)}, bf16[256,256]{1,0:T(8,128)(2,1)S(1)}, u32[]{:S(2)}, u32[]{:S(2)}) collective-permute-start(bf16[256,256]{1,0:T(8,128)(2,1)S(1)} %get-tuple-element.62), channel_id=1, source_target_pairs={{0,6},{2,4},{4,2},{6,0},{1,7},{3,5},{5,3},{7,1},{8,14},{10,12},{12... | collective-permute-start | bytes 393224 | tf_op jit(solution)/shard_map/ppermute | solution.py:413
  27.9 18.6 %collective-permute-start.8 = (bf16[256,256]{1,0:T(8,128)(2,1)S(1)}, bf16[256,256]{1,0:T(8,128)(2,1)S(1)}, u32[]{:S(2)}, u32[]{:S(2)}) collective-permute-start(bf16[256,256]{1,0:T(8,128)(2,1)S(1)} %get-tuple-element.63), channel_id=1, source_target_pairs={{0,2},{2,0},{4,6},{6,4},{1,3},{3,1},{5,7},{7,5},{8,10},{10,8},{12,... | collective-permute-start | bytes 393224 | tf_op jit(solution)/shard_map/ppermute | solution.py:413
  36.2 13.6 %collective-permute-start.12 = (bf16[256,256]{1,0:T(8,128)(2,1)S(1)}, bf16[256,256]{1,0:T(8,128)(2,1)S(1)}, u32[]{:S(2)}, u32[]{:S(2)}) collective-permute-start(bf16[256,256]{1,0:T(8,128)(2,1)S(1)} %get-tuple-element.70), channel_id=1, source_target_pairs={{0,4},{2,6},{4,0},{6,2},{1,5},{3,7},{5,1},{7,3},{8,12},{10,14},{12... | collective-permute-start | bytes 393224 | tf_op jit(solution)/shard_map/ppermute | solution.py:413
  36.3 16.3 %collective-permute-start.13 = (bf16[256,256]{1,0:T(8,128)(2,1)S(1)}, bf16[256,256]{1,0:T(8,128)(2,1)S(1)}, u32[]{:S(2)}, u32[]{:S(2)}) collective-permute-start(bf16[256,256]{1,0:T(8,128)(2,1)S(1)} %get-tuple-element.71), channel_id=1, source_target_pairs={{0,6},{2,4},{4,2},{6,0},{1,7},{3,5},{5,3},{7,1},{8,14},{10,12},{12... | collective-permute-start | bytes 393224 | tf_op jit(solution)/shard_map/ppermute | solution.py:413
  39.1 13.6 %collective-permute-start.14 = (bf16[256,256]{1,0:T(8,128)(2,1)S(1)}, bf16[256,256]{1,0:T(8,128)(2,1)S(1)}, u32[]{:S(2)}, u32[]{:S(2)}) collective-permute-start(bf16[256,256]{1,0:T(8,128)(2,1)S(1)} %get-tuple-element.72), channel_id=1, source_target_pairs={{0,2},{2,0},{4,6},{6,4},{1,3},{3,1},{5,7},{7,5},{8,10},{10,8},{12,... | collective-permute-start | bytes 393224 | tf_op jit(solution)/shard_map/ppermute | solution.py:413
  54.1 12.1 %collective-permute-start.20 = (bf16[256,256]{1,0:T(8,128)(2,1)S(1)}, bf16[256,256]{1,0:T(8,128)(2,1)S(1)}, u32[]{:S(2)}, u32[]{:S(2)}) collective-permute-start(bf16[256,256]{1,0:T(8,128)(2,1)S(1)} %get-tuple-element.87), channel_id=1, source_target_pairs={{0,12},{2,14},{4,8},{6,10},{8,20},{10,22},{12,16},{14,18},{16,28},... | collective-permute-start | bytes 393224 | tf_op jit(solution)/shard_map/ppermute | solution.py:410
  55.4 17.9 %collective-permute-start.21 = (bf16[256,256]{1,0:T(8,128)(2,1)S(1)}, bf16[256,256]{1,0:T(8,128)(2,1)S(1)}, u32[]{:S(2)}, u32[]{:S(2)}) collective-permute-start(bf16[256,256]{1,0:T(8,128)(2,1)S(1)} %get-tuple-element.88), channel_id=1, source_target_pairs={{0,14},{2,12},{4,10},{6,8},{8,22},{10,20},{12,18},{14,16},{16,30},... | collective-permute-start | bytes 393224 | tf_op jit(solution)/shard_map/ppermute | solution.py:410
  57.3 15.9 %collective-permute-start.22 = (bf16[256,256]{1,0:T(8,128)(2,1)S(1)}, bf16[256,256]{1,0:T(8,128)(2,1)S(1)}, u32[]{:S(2)}, u32[]{:S(2)}) collective-permute-start(bf16[256,256]{1,0:T(8,128)(2,1)S(1)} %get-tuple-element.89), channel_id=1, source_target_pairs={{0,10},{2,8},{4,14},{6,12},{8,18},{10,16},{12,22},{14,20},{16,26},... | collective-permute-start | bytes 393224 | tf_op jit(solution)/shard_map/ppermute | solution.py:410
  60.5 12.7 %collective-permute-start.23 = (bf16[256,256]{1,0:T(8,128)(2,1)S(1)}, bf16[256,256]{1,0:T(8,128)(2,1)S(1)}, u32[]{:S(2)}, u32[]{:S(2)}) collective-permute-start(bf16[256,256]{1,0:T(8,128)(2,1)S(1)} %get-tuple-element.90), channel_id=1, source_target_pairs={{0,8},{2,10},{4,12},{6,14},{8,16},{10,18},{12,20},{14,22},{16,24},... | collective-permute-start | bytes 393224 | tf_op jit(solution)/shard_map/ppermute | solution.py:410
  61.2 25.7 %collective-permute-start.18 = (bf16[256,256]{1,0:T(8,128)(2,1)S(1)}, bf16[256,256]{1,0:T(8,128)(2,1)S(1)}, u32[]{:S(2)}, u32[]{:S(2)}) collective-permute-start(bf16[256,256]{1,0:T(8,128)(2,1)S(1)} %get-tuple-element.76.refs_0_), channel_id=1, source_target_pairs={{0,8},{2,10},{4,12},{6,14},{8,16},{10,18},{12,20},{14,22},{16,24},... | collective-permute-start | bytes 393224 | tf_op jit(solution)/shard_map/ppermute | solution.py:410
  66.1 9.9 %collective-permute-start.15 = (bf16[256,256]{1,0:T(8,128)(2,1)S(1)}, bf16[256,256]{1,0:T(8,128)(2,1)S(1)}, u32[]{:S(2)}, u32[]{:S(2)}) collective-permute-start(bf16[256,256]{1,0:T(8,128)(2,1)S(1)} %get-tuple-element.79), channel_id=1, source_target_pairs={{0,12},{2,14},{4,8},{6,10},{8,20},{10,22},{12,16},{14,18},{16,28},... | collective-permute-start | bytes 393224 | tf_op jit(solution)/shard_map/ppermute | solution.py:410
  73.2 13.7 %collective-permute-start.16 = (bf16[256,256]{1,0:T(8,128)(2,1)S(1)}, bf16[256,256]{1,0:T(8,128)(2,1)S(1)}, u32[]{:S(2)}, u32[]{:S(2)}) collective-permute-start(bf16[256,256]{1,0:T(8,128)(2,1)S(1)} %get-tuple-element.80), channel_id=1, source_target_pairs={{0,14},{2,12},{4,10},{6,8},{8,22},{10,20},{12,18},{14,16},{16,30},... | collective-permute-start | bytes 393224 | tf_op jit(solution)/shard_map/ppermute | solution.py:410
  73.2 13.7 %collective-permute-start.17 = (bf16[256,256]{1,0:T(8,128)(2,1)S(1)}, bf16[256,256]{1,0:T(8,128)(2,1)S(1)}, u32[]{:S(2)}, u32[]{:S(2)}) collective-permute-start(bf16[256,256]{1,0:T(8,128)(2,1)S(1)} %get-tuple-element.81), channel_id=1, source_target_pairs={{0,10},{2,8},{4,14},{6,12},{8,18},{10,16},{12,22},{14,20},{16,26},... | collective-permute-start | bytes 393224 | tf_op jit(solution)/shard_map/ppermute | solution.py:410
  74.3 16.4 %collective-permute-start.24 = (bf16[256,256]{1,0:T(8,128)(2,1)S(1)}, bf16[256,256]{1,0:T(8,128)(2,1)S(1)}, u32[]{:S(2)}, u32[]{:S(2)}) collective-permute-start(bf16[256,256]{1,0:T(8,128)(2,1)S(1)} %get-tuple-element.91), channel_id=1, source_target_pairs={{0,4},{2,6},{4,0},{6,2},{1,5},{3,7},{5,1},{7,3},{8,12},{10,14},{12... | collective-permute-start | bytes 393224 | tf_op jit(solution)/shard_map/ppermute | solution.py:413
  76.0 15.5 %collective-permute-start.25 = (bf16[256,256]{1,0:T(8,128)(2,1)S(1)}, bf16[256,256]{1,0:T(8,128)(2,1)S(1)}, u32[]{:S(2)}, u32[]{:S(2)}) collective-permute-start(bf16[256,256]{1,0:T(8,128)(2,1)S(1)} %get-tuple-element.92), channel_id=1, source_target_pairs={{0,6},{2,4},{4,2},{6,0},{1,7},{3,5},{5,3},{7,1},{8,14},{10,12},{12... | collective-permute-start | bytes 393224 | tf_op jit(solution)/shard_map/ppermute | solution.py:413
  86.9 11.0 %collective-permute-start.26 = (bf16[256,256]{1,0:T(8,128)(2,1)S(1)}, bf16[256,256]{1,0:T(8,128)(2,1)S(1)}, u32[]{:S(2)}, u32[]{:S(2)}) collective-permute-start(bf16[256,256]{1,0:T(8,128)(2,1)S(1)} %get-tuple-element.93), channel_id=1, source_target_pairs={{0,2},{2,0},{4,6},{6,4},{1,3},{3,1},{5,7},{7,5},{8,10},{10,8},{12,... | collective-permute-start | bytes 393224 | tf_op jit(solution)/shard_map/ppermute | solution.py:413
  87.9 10.9 %collective-permute-start.27 = (bf16[256,256]{1,0:T(8,128)(2,1)S(1)}, bf16[256,256]{1,0:T(8,128)(2,1)S(1)}, u32[]{:S(2)}, u32[]{:S(2)}) collective-permute-start(bf16[256,256]{1,0:T(8,128)(2,1)S(1)} %get-tuple-element.95), channel_id=1, source_target_pairs={{0,4},{2,6},{4,0},{6,2},{1,5},{3,7},{5,1},{7,3},{8,12},{10,14},{12... | collective-permute-start | bytes 393224 | tf_op jit(solution)/shard_map/ppermute | solution.py:413
  88.0 15.0 %collective-permute-start.28 = (bf16[256,256]{1,0:T(8,128)(2,1)S(1)}, bf16[256,256]{1,0:T(8,128)(2,1)S(1)}, u32[]{:S(2)}, u32[]{:S(2)}) collective-permute-start(bf16[256,256]{1,0:T(8,128)(2,1)S(1)} %get-tuple-element.96), channel_id=1, source_target_pairs={{0,6},{2,4},{4,2},{6,0},{1,7},{3,5},{5,3},{7,1},{8,14},{10,12},{12... | collective-permute-start | bytes 393224 | tf_op jit(solution)/shard_map/ppermute | solution.py:413
  90.6 12.4 %collective-permute-start.29 = (bf16[256,256]{1,0:T(8,128)(2,1)S(1)}, bf16[256,256]{1,0:T(8,128)(2,1)S(1)}, u32[]{:S(2)}, u32[]{:S(2)}) collective-permute-start(bf16[256,256]{1,0:T(8,128)(2,1)S(1)} %get-tuple-element.97), channel_id=1, source_target_pairs={{0,2},{2,0},{4,6},{6,4},{1,3},{3,1},{5,7},{7,5},{8,10},{10,8},{12,... | collective-permute-start | bytes 393224 | tf_op jit(solution)/shard_map/ppermute | solution.py:413
  91.6 13.5 %collective-permute-start.19 = (bf16[256,1024]{1,0:T(8,128)(2,1)S(1)}, bf16[256,1024]{1,0:T(8,128)(2,1)S(1)}, u32[]{:S(2)}, u32[]{:S(2)}) collective-permute-start(bf16[256,1024]{1,0:T(8,128)(2,1)S(1)} %other_rows.1), channel_id=1, source_target_pairs={{0,1},{1,0},{2,3},{3,2},{4,5},{5,4},{6,7},{7,6},{8,9},{9,8},{10,11... | collective-permute-start | bytes 1572872 | tf_op jit(solution)/shard_map/ppermute | solution.py:375
  103.4 2.7 %collective-permute-start.30 = (bf16[256,1024]{1,0:T(8,128)(2,1)S(1)}, bf16[256,1024]{1,0:T(8,128)(2,1)S(1)}, u32[]{:S(2)}, u32[]{:S(2)}) collective-permute-start(bf16[256,1024]{1,0:T(8,128)(2,1)S(1)} %half_space.3), channel_id=1, source_target_pairs={{0,1},{1,0},{2,3},{3,2},{4,5},{5,4},{6,7},{7,6},{8,9},{9,8},{10,11... | collective-permute-start | bytes 1572872 | tf_op jit(solution)/shard_map/ppermute | solution.py:375
  (9 other events, 44.5 us)

commit v4 on v3

--- a/solution.py
+++ b/solution.py
@@ -245,7 +245,7 @@
     own = rows // 2
     half = odd_ref.shape[0]
     join_modes(here, pieces, modes)
-    step = 256
+    step = 512
     for start in range(0, half, step):
         columns = slice(start, start + step)
         second = dot(modes[...], odd_ref[:, columns])
@@ -292,7 +292,7 @@
     offset = (lax.axis_index("core") ^ index) * own
     lines = rows_of(offset, own)
     join_modes(lax.axis_index("z"), pieces, modes, lines)
-    step = 256
+    step = 512
     for start in range(0, half, step):
         columns = slice(start, start + step)
         second = dot(modes[...], odd_ref[:, columns])
@@ -313,12 +313,20 @@
     out_ref[...] = both_ref[rows_of((lax.axis_index("core") ^ 1) * rows, rows), :]
 
 
-def finish_kernel(first_ref, first_other_ref, keep_ref, got_ref, fields_ref, image_ref):
+def finish_kernel(
+    first_ref, first_other_ref, keep_ref, got_ref, fields_out, image_out, image, sems
+):
     rows = keep_ref.shape[0]
     own = rows // 2
     core = lax.axis_index("core")
-    fields_ref[rows_of(core * rows, rows), :] = keep_ref[...]
-    fields_ref[rows_of((core ^ 1) * rows, rows), :] = got_ref[...]
+    copies = [
+        pltpu.make_async_copy(keep_ref, fields_out.at[rows_of(core * rows, rows), :], sems.at[0]),
+        pltpu.make_async_copy(
+            got_ref, fields_out.at[rows_of((core ^ 1) * rows, rows), :], sems.at[1]
+        ),
+    ]
+    for copy in copies:
+        copy.start()
     step = 16
     for start in range(0, own, step):
         total = None
@@ -331,7 +339,17 @@
             ):
                 term = one.astype(F32) * two.astype(F32)
                 total = term if total is None else total + term
-        image_ref[start : start + step, :] = total
+        image[start : start + step, :] = total
+        if (start + step) % (own // 2) == 0:
+            done = slice(start + step - own // 2, start + step)
+            copies.append(
+                pltpu.make_async_copy(
+                    image.at[done, :], image_out.at[done, :], sems.at[len(copies)]
+                )
+            )
+            copies[-1].start()
+    for copy in copies:
+        copy.wait()
 
 
 def after(count, kernel, *refs):
@@ -471,7 +489,9 @@
     got = other_core(give)
     fields, image = call(
         finish_kernel, (first, first_other, keep, got),
-        [of((2 * rows, length_y)), of((own, length_y), F32)], flops=8 * cells, name="finish",
+        [of((2 * rows, length_y)), of((own, length_y), F32)],
+        [pltpu.VMEM((own, length_y), F32), pltpu.SemaphoreType.DMA((4,))],
+        flops=8 * cells, name="finish", puts=[HBM] * 2,
     )
     return image[None], fields.reshape(flight_fields.shape)
 

time: 109 us -> 108 us (level)
  no operation moved by 1% of the time
where the time goes in v4:
time: 108 us; the launch traced here: 107 us
  waiting for transfers between devices  45.5 us (42%)
  starting transfers between devices  39 us (36%)
  Pallas kernels  18.3 us (17%)
  local copies, waits for them, and re-layouts  2.32 us (2%)
  between operations  2.27 us (2%)
    ppermute x18, waiting for transfers between devices, exchange(): got.append(lax.ppermute(piece, 'z', pairs) if k else piece)  28.7 us
    ppermute x18, starting transfers between devices, exchange(): got.append(lax.ppermute(piece, 'z', pairs) if k else piece)  20.5 us
    pallas_call x21, Pallas kernels, call(): pl.pallas_call(functools.partial(after, len(behind), kernel), out_shape=t...  18.3 us
    ppermute x8, waiting for transfers between devices, exchange(): got.append(lax.ppermute(piece, ('depth', 'z'), pairs))  15.7 us
    ppermute x8, starting transfers between devices, exchange(): got.append(lax.ppermute(piece, ('depth', 'z'), pairs))  9.84 us
    ppermute x5, starting transfers between devices, other_core(): return lax.ppermute(value, 'core', [(0, 1), (1, 0)])  8.72 us
    unnamed x20, local copies, waits for them, and re-layouts  2.32 us
  transfers between devices with their start and end apart: 31, of which 10 were waited for; matrix products, arithmetic and copies ran while one was open for 0% of the time, Pallas kernels for 15%

profile of v4, /device:TPU:9, one launch (start us, length us, event | category | flops | bytes accessed | tf_op | source)
XLA Modules:
  0.0 107.4 jit_solution(7095960045271083660)
XLA Ops:
  2.9 1.2 %copy-done.5 = bf16[1,2,2,128,1024]{4,3,2,1,0:T(8,128)(2,1)S(1)} copy-done((bf16[1,2,2,128,1024]{4,3,2,1,0:T(8,128)(2,1)S(1)}, bf16[1,2,2,128,1024]{4,3,2,1,0:T(8,128)(2,1)}, u32[]{:S(2)}) %copy-start.5) | copy-done | bytes 1048600
  4.9 2.4 %collective-permute-start.3 = (bf16[256,256]{1,0:T(8,128)(2,1)S(1)}, bf16[256,256]{1,0:T(8,128)(2,1)S(1)}, u32[]{:S(2)}, u32[]{:S(2)}) collective-permute-start(bf16[256,256]{1,0:T(8,128)(2,1)S(1)} %get-tuple-element.57), channel_id=1, source_target_pairs={{0,4},{2,6},{4,0},{6,2},{1,5},{3,7},{5,1},{7,3},{8,12},{10,14},{12... | collective-permute-start | bytes 393224 | tf_op jit(solution)/shard_map/ppermute | solution.py:431
  7.3 1.2 %collective-permute-start.5 = (bf16[256,256]{1,0:T(8,128)(2,1)S(1)}, bf16[256,256]{1,0:T(8,128)(2,1)S(1)}, u32[]{:S(2)}, u32[]{:S(2)}) collective-permute-start(bf16[256,256]{1,0:T(8,128)(2,1)S(1)} %get-tuple-element.59), channel_id=1, source_target_pairs={{0,2},{2,0},{4,6},{6,4},{1,3},{3,1},{5,7},{7,5},{8,10},{10,8},{12,... | collective-permute-start | bytes 393224 | tf_op jit(solution)/shard_map/ppermute | solution.py:431
  9.9 1.2 %odd_to_modes.1 = (bf16[256,256]{1,0:T(8,128)(2,1)S(1)}, bf16[256,256]{1,0:T(8,128)(2,1)S(1)}, bf16[256,256]{1,0:T(8,128)(2,1)S(1)}, bf16[256,256]{1,0:T(8,128)(2,1)S(1)}, f32[4]{0:T(128)S(1)}) custom-call(bf16[512,1024]{1,0:T(8,128)(2,1)S(1)} %collective-permute-done.refs_0_.refs_3_, f32[128,1024]{1,0:T(8,128)S(1)} %collective-permute-done.1.refs_1_.refs_2_.refs_3_, ...), custom_call_target="tpu_custom_call" | custom-call | flops 268435456 | bytes 3145768 | tf_op jit(solution)/shard_map/odd_to_modes/pallas_call | solution.py:365
  11.2 1.5 %collective-permute-start.9 = (bf16[256,256]{1,0:T(8,128)(2,1)S(1)}, bf16[256,256]{1,0:T(8,128)(2,1)S(1)}, u32[]{:S(2)}, u32[]{:S(2)}) collective-permute-start(bf16[256,256]{1,0:T(8,128)(2,1)S(1)} %get-tuple-element.66), channel_id=1, source_target_pairs={{0,4},{2,6},{4,0},{6,2},{1,5},{3,7},{5,1},{7,3},{8,12},{10,14},{12... | collective-permute-start | bytes 393224 | tf_op jit(solution)/shard_map/ppermute | solution.py:431
  14.6 1.7 %phases.2 = (f32[256,1024]{1,0:T(8,128)S(1)}, f32[256,1024]{1,0:T(8,128)S(1)}) custom-call(f32[4]{0:T(128)S(1)} %get-tuple-element.51.refs_0_.refs_1_, f32[128,1024]{1,0:T(8,128)S(1)} %bitcast.9, f32[128,1024]{1,0:T(8,128)S(1)} %collective-permute-done.1.refs_1_.refs_2_.refs_3_), custom_call_target="tpu_custom_call" | custom-call | flops 104857600 | bytes 3145744 | tf_op jit(solution)/shard_map/phases/pallas_call | solution.py:365
  16.3 2.2 %collective-permute-start.11 = (bf16[256,256]{1,0:T(8,128)(2,1)S(1)}, bf16[256,256]{1,0:T(8,128)(2,1)S(1)}, u32[]{:S(2)}, u32[]{:S(2)}) collective-permute-start(bf16[256,256]{1,0:T(8,128)(2,1)S(1)} %get-tuple-element.68), channel_id=1, source_target_pairs={{0,2},{2,0},{4,6},{6,4},{1,3},{3,1},{5,7},{7,5},{8,10},{10,8},{12,... | collective-permute-start | bytes 393224 | tf_op jit(solution)/shard_map/ppermute | solution.py:431
  18.6 6.0 %collective-permute-done.4.refs_9_ = bf16[256,256]{1,0:T(8,128)(2,1)S(1)} collective-permute-done((bf16[256,256]{1,0:T(8,128)(2,1)S(1)}, bf16[256,256]{1,0:T(8,128)(2,1)S(1)}, u32[]{:S(2)}, u32[]{:S(2)}) %collective-permute-start.4) | collective-permute-done | bytes 131104 | tf_op jit(solution)/shard_map/ppermute | solution.py:431
  25.6 2.3 %collective-permute-start.7 = (bf16[256,256]{1,0:T(8,128)(2,1)S(1)}, bf16[256,256]{1,0:T(8,128)(2,1)S(1)}, u32[]{:S(2)}, u32[]{:S(2)}) collective-permute-start(bf16[256,256]{1,0:T(8,128)(2,1)S(1)} %get-tuple-element.62), channel_id=1, source_target_pairs={{0,6},{2,4},{4,2},{6,0},{1,7},{3,5},{5,3},{7,1},{8,14},{10,12},{12... | collective-permute-start | bytes 393224 | tf_op jit(solution)/shard_map/ppermute | solution.py:431
  27.9 1.3 %collective-permute-start.8 = (bf16[256,256]{1,0:T(8,128)(2,1)S(1)}, bf16[256,256]{1,0:T(8,128)(2,1)S(1)}, u32[]{:S(2)}, u32[]{:S(2)}) collective-permute-start(bf16[256,256]{1,0:T(8,128)(2,1)S(1)} %get-tuple-element.63), channel_id=1, source_target_pairs={{0,2},{2,0},{4,6},{6,4},{1,3},{3,1},{5,7},{7,5},{8,10},{10,8},{12,... | collective-permute-start | bytes 393224 | tf_op jit(solution)/shard_map/ppermute | solution.py:431
  29.1 6.1 %collective-permute-done.10.refs_7_ = bf16[256,256]{1,0:T(8,128)(2,1)S(1)} collective-permute-done((bf16[256,256]{1,0:T(8,128)(2,1)S(1)}, bf16[256,256]{1,0:T(8,128)(2,1)S(1)}, u32[]{:S(2)}, u32[]{:S(2)}) %collective-permute-start.10) | collective-permute-done | bytes 131104 | tf_op jit(solution)/shard_map/ppermute | solution.py:431
  36.3 2.8 %collective-permute-start.13 = (bf16[256,256]{1,0:T(8,128)(2,1)S(1)}, bf16[256,256]{1,0:T(8,128)(2,1)S(1)}, u32[]{:S(2)}, u32[]{:S(2)}) collective-permute-start(bf16[256,256]{1,0:T(8,128)(2,1)S(1)} %get-tuple-element.71), channel_id=1, source_target_pairs={{0,6},{2,4},{4,2},{6,0},{1,7},{3,5},{5,3},{7,1},{8,14},{10,12},{12... | collective-permute-start | bytes 393224 | tf_op jit(solution)/shard_map/ppermute | solution.py:431
  39.1 1.1 %collective-permute-start.14 = (bf16[256,256]{1,0:T(8,128)(2,1)S(1)}, bf16[256,256]{1,0:T(8,128)(2,1)S(1)}, u32[]{:S(2)}, u32[]{:S(2)}) collective-permute-start(bf16[256,256]{1,0:T(8,128)(2,1)S(1)} %get-tuple-element.72), channel_id=1, source_target_pairs={{0,2},{2,0},{4,6},{6,4},{1,3},{3,1},{5,7},{7,5},{8,10},{10,8},{12,... | collective-permute-start | bytes 393224 | tf_op jit(solution)/shard_map/ppermute | solution.py:431
  40.2 6.3 %collective-permute-done.7.refs_2_ = bf16[256,256]{1,0:T(8,128)(2,1)S(1)} collective-permute-done((bf16[256,256]{1,0:T(8,128)(2,1)S(1)}, bf16[256,256]{1,0:T(8,128)(2,1)S(1)}, u32[]{:S(2)}, u32[]{:S(2)}) %collective-permute-start.7) | collective-permute-done | bytes 131104 | tf_op jit(solution)/shard_map/ppermute | solution.py:431
  47.0 2.8 %collective-permute-done.12.refs_7_ = bf16[256,256]{1,0:T(8,128)(2,1)S(1)} collective-permute-done((bf16[256,256]{1,0:T(8,128)(2,1)S(1)}, bf16[256,256]{1,0:T(8,128)(2,1)S(1)}, u32[]{:S(2)}, u32[]{:S(2)}) %collective-permute-start.12) | collective-permute-done | bytes 131104 | tf_op jit(solution)/shard_map/ppermute | solution.py:431
  49.8 2.8 %collective-permute-done.13.refs_8_ = bf16[256,256]{1,0:T(8,128)(2,1)S(1)} collective-permute-done((bf16[256,256]{1,0:T(8,128)(2,1)S(1)}, bf16[256,256]{1,0:T(8,128)(2,1)S(1)}, u32[]{:S(2)}, u32[]{:S(2)}) %collective-permute-start.13) | collective-permute-done | bytes 131104 | tf_op jit(solution)/shard_map/ppermute | solution.py:431
  52.6 1.4 %turn_around.1 = (bf16[256,256]{1,0:T(8,128)(2,1)S(1)}, bf16[256,256]{1,0:T(8,128)(2,1)S(1)}, bf16[256,256]{1,0:T(8,128)(2,1)S(1)}, bf16[256,256]{1,0:T(8,128)(2...) custom-call(f32[256,1024]{1,0:T(8,128)S(1)} %get-tuple-element.52.refs_1_.refs_0_, ...), custom_call_target="tpu_custom_call" | custom-call | flops 536870912 | bytes 8912896 | tf_op jit(solution)/shard_map/turn_around/pallas_call | solution.py:365
  54.1 1.3 %collective-permute-start.20 = (bf16[256,256]{1,0:T(8,128)(2,1)S(1)}, bf16[256,256]{1,0:T(8,128)(2,1)S(1)}, u32[]{:S(2)}, u32[]{:S(2)}) collective-permute-start(bf16[256,256]{1,0:T(8,128)(2,1)S(1)} %get-tuple-element.87), channel_id=1, source_target_pairs={{0,12},{2,14},{4,8},{6,10},{8,20},{10,22},{12,16},{14,18},{16,28},... | collective-permute-start | bytes 393224 | tf_op jit(solution)/shard_map/ppermute | solution.py:428
  55.4 2.0 %collective-permute-start.21 = (bf16[256,256]{1,0:T(8,128)(2,1)S(1)}, bf16[256,256]{1,0:T(8,128)(2,1)S(1)}, u32[]{:S(2)}, u32[]{:S(2)}) collective-permute-start(bf16[256,256]{1,0:T(8,128)(2,1)S(1)} %get-tuple-element.88), channel_id=1, source_target_pairs={{0,14},{2,12},{4,10},{6,8},{8,22},{10,20},{12,18},{14,16},{16,30},... | collective-permute-start | bytes 393224 | tf_op jit(solution)/shard_map/ppermute | solution.py:428
  57.3 3.2 %collective-permute-start.22 = (bf16[256,256]{1,0:T(8,128)(2,1)S(1)}, bf16[256,256]{1,0:T(8,128)(2,1)S(1)}, u32[]{:S(2)}, u32[]{:S(2)}) collective-permute-start(bf16[256,256]{1,0:T(8,128)(2,1)S(1)} %get-tuple-element.89), channel_id=1, source_target_pairs={{0,10},{2,8},{4,14},{6,12},{8,18},{10,16},{12,22},{14,20},{16,26},... | collective-permute-start | bytes 393224 | tf_op jit(solution)/shard_map/ppermute | solution.py:428
  61.2 1.3 %collective-permute-start.18 = (bf16[256,256]{1,0:T(8,128)(2,1)S(1)}, bf16[256,256]{1,0:T(8,128)(2,1)S(1)}, u32[]{:S(2)}, u32[]{:S(2)}) collective-permute-start(bf16[256,256]{1,0:T(8,128)(2,1)S(1)} %get-tuple-element.76.refs_0_), channel_id=1, source_target_pairs={{0,8},{2,10},{4,12},{6,14},{8,16},{10,18},{12,20},{14,22},{16,24},... | collective-permute-start | bytes 393224 | tf_op jit(solution)/shard_map/ppermute | solution.py:428
  64.4 1.7 %phases.3 = (f32[256,1024]{1,0:T(8,128)S(1)}, f32[256,1024]{1,0:T(8,128)S(1)}) custom-call(bf16[256,256]{1,0:T(8,128)(2,1)S(1)} %get-tuple-element.76.refs_0_, f32[4]{0:T(128)S(1)} %get-tuple-element.51.refs_0_.refs_1_, f32[128,1024]{1,0:T(8,128)S(1)} %bitcast.10, f32[128,1024]{1,0:T(8,128)S(1)} %collective-permute-done.1.refs_1_.refs_2_.refs_3_), custom_call_target="tpu_custom_call" | custom-call | flops 104857600 | bytes 3145744 | tf_op jit(solution)/shard_map/phases/pallas_call | solution.py:365
  66.1 2.0 %collective-permute-start.15 = (bf16[256,256]{1,0:T(8,128)(2,1)S(1)}, bf16[256,256]{1,0:T(8,128)(2,1)S(1)}, u32[]{:S(2)}, u32[]{:S(2)}) collective-permute-start(bf16[256,256]{1,0:T(8,128)(2,1)S(1)} %get-tuple-element.79), channel_id=1, source_target_pairs={{0,12},{2,14},{4,8},{6,10},{8,20},{10,22},{12,16},{14,18},{16,28},... | collective-permute-start | bytes 393224 | tf_op jit(solution)/shard_map/ppermute | solution.py:428
  68.1 5.1 %collective-permute-done.21.refs_9_ = bf16[256,256]{1,0:T(8,128)(2,1)S(1)} collective-permute-done((bf16[256,256]{1,0:T(8,128)(2,1)S(1)}, bf16[256,256]{1,0:T(8,128)(2,1)S(1)}, u32[]{:S(2)}, u32[]{:S(2)}) %collective-permute-start.21) | collective-permute-done | bytes 131104 | tf_op jit(solution)/shard_map/ppermute | solution.py:428
  74.3 1.8 %collective-permute-start.24 = (bf16[256,256]{1,0:T(8,128)(2,1)S(1)}, bf16[256,256]{1,0:T(8,128)(2,1)S(1)}, u32[]{:S(2)}, u32[]{:S(2)}) collective-permute-start(bf16[256,256]{1,0:T(8,128)(2,1)S(1)} %get-tuple-element.91), channel_id=1, source_target_pairs={{0,4},{2,6},{4,0},{6,2},{1,5},{3,7},{5,1},{7,3},{8,12},{10,14},{12... | collective-permute-start | bytes 393224 | tf_op jit(solution)/shard_map/ppermute | solution.py:431
  76.2 10.6 %collective-permute-done.16.refs_7_ = bf16[256,256]{1,0:T(8,128)(2,1)S(1)} collective-permute-done((bf16[256,256]{1,0:T(8,128)(2,1)S(1)}, bf16[256,256]{1,0:T(8,128)(2,1)S(1)}, u32[]{:S(2)}, u32[]{:S(2)}) %collective-permute-start.16) | collective-permute-done | bytes 131104 | tf_op jit(solution)/shard_map/ppermute | solution.py:428
  88.0 2.6 %collective-permute-start.28 = (bf16[256,256]{1,0:T(8,128)(2,1)S(1)}, bf16[256,256]{1,0:T(8,128)(2,1)S(1)}, u32[]{:S(2)}, u32[]{:S(2)}) collective-permute-start(bf16[256,256]{1,0:T(8,128)(2,1)S(1)} %get-tuple-element.96), channel_id=1, source_target_pairs={{0,6},{2,4},{4,2},{6,0},{1,7},{3,5},{5,3},{7,1},{8,14},{10,12},{12... | collective-permute-start | bytes 393224 | tf_op jit(solution)/shard_map/ppermute | solution.py:431
  91.6 6.3 %collective-permute-start.19 = (bf16[256,1024]{1,0:T(8,128)(2,1)S(1)}, bf16[256,1024]{1,0:T(8,128)(2,1)S(1)}, u32[]{:S(2)}, u32[]{:S(2)}) collective-permute-start(bf16[256,1024]{1,0:T(8,128)(2,1)S(1)} %other_rows.1), channel_id=1, source_target_pairs={{0,1},{1,0},{2,3},{3,2},{4,5},{5,4},{6,7},{7,6},{8,9},{9,8},{10,11... | collective-permute-start | bytes 1572872 | tf_op jit(solution)/shard_map/ppermute | solution.py:393
  98.8 4.2 %collective-permute-done.28.refs_5_ = bf16[256,256]{1,0:T(8,128)(2,1)S(1)} collective-permute-done((bf16[256,256]{1,0:T(8,128)(2,1)S(1)}, bf16[256,256]{1,0:T(8,128)(2,1)S(1)}, u32[]{:S(2)}, u32[]{:S(2)}) %collective-permute-start.28) | collective-permute-done | bytes 131104 | tf_op jit(solution)/shard_map/ppermute | solution.py:431
  103.4 1.2 %collective-permute-start.30 = (bf16[256,1024]{1,0:T(8,128)(2,1)S(1)}, bf16[256,1024]{1,0:T(8,128)(2,1)S(1)}, u32[]{:S(2)}, u32[]{:S(2)}) collective-permute-start(bf16[256,1024]{1,0:T(8,128)(2,1)S(1)} %half_space.3), channel_id=1, source_target_pairs={{0,1},{1,0},{2,3},{3,2},{4,5},{5,4},{6,7},{7,6},{8,9},{9,8},{10,11... | collective-permute-start | bytes 1572872 | tf_op jit(solution)/shard_map/ppermute | solution.py:393
  105.1 1.1 collective-permute-done.30.refs_3_
  106.2 1.2 %finish.1 = (bf16[512,1024]{1,0:T(8,128)(2,1)}, f32[128,1024]{1,0:T(8,128)}) custom-call(bf16[512,1024]{1,0:T(8,128)(2,1)S(1)} %get-tuple-element.74.refs_1_.refs_0_, bf16[256,1024]{1,0:T(8,128)(2,1)S(1)} %collective-permute-done.19.refs_1_, bf16[256,1024]{1,0:T(8,128)(2,1)S(1)} %half_space.2.refs_2_, bf16[256,1024]{1,0:T(8,128)(2,1)S(1)} %collective-permute-done.30.refs_3_), custom_call_target="tpu_custom_call" | custom-call | flops 1048576 | bytes 4194304 | tf_op jit(solution)/shard_map/finish/pallas_call | solution.py:365
  (71 shorter events, 15.3 us)
Async XLA Ops:
  0.6 3.9 %collective-permute-start.2 = (bf16[512,1024]{1,0:T(8,128)(2,1)}, bf16[512,1024]{1,0:T(8,128)(2,1)S(1)}, u32[]{:S(2)}, u32[]{:S(2)}) collective-permute-start(bf16[512,1024]{1,0:T(8,128)(2,1)} %bitcast.5), channel_id=1, source_target_pairs={{0,1},{1,0},{2,3},{3,2},{4,5},{5,4},{6,7},{7,6},{8,9},{9,8},{10,11... | collective-permute-start | bytes 3145736 | tf_op jit(solution)/shard_map/ppermute | solution.py:393
  1.4 8.5 %collective-permute-start = (bf16[512,1024]{1,0:T(8,128)(2,1)}, bf16[512,1024]{1,0:T(8,128)(2,1)S(1)}, u32[]{:S(2)}, u32[]{:S(2)}) collective-permute-start(bf16[512,1024]{1,0:T(8,128)(2,1)} %bitcast.11), channel_id=1, source_target_pairs={{0,1},{1,0},{2,3},{3,2},{4,5},{5,4},{6,7},{7,6},{8,9},{9,8},{10,11... | collective-permute-start | bytes 3145736 | tf_op jit(solution)/shard_map/ppermute | solution.py:393
  1.5 8.4 %collective-permute-start.1 = (f32[128,1024]{1,0:T(8,128)}, f32[128,1024]{1,0:T(8,128)S(1)}, u32[]{:S(2)}, u32[]{:S(2)}) collective-permute-start(f32[128,1024]{1,0:T(8,128)} %bitcast.8), channel_id=1, source_target_pairs={{0,1},{1,0},{2,3},{3,2},{4,5},{5,4},{6,7},{7,6},{8,9},{9,8},{10,11... | collective-permute-start | bytes 1572872 | tf_op jit(solution)/shard_map/ppermute | solution.py:393
  4.9 11.5 %collective-permute-start.3 = (bf16[256,256]{1,0:T(8,128)(2,1)S(1)}, bf16[256,256]{1,0:T(8,128)(2,1)S(1)}, u32[]{:S(2)}, u32[]{:S(2)}) collective-permute-start(bf16[256,256]{1,0:T(8,128)(2,1)S(1)} %get-tuple-element.57), channel_id=1, source_target_pairs={{0,4},{2,6},{4,0},{6,2},{1,5},{3,7},{5,1},{7,3},{8,12},{10,14},{12... | collective-permute-start | bytes 393224 | tf_op jit(solution)/shard_map/ppermute | solution.py:431
  7.3 17.2 %collective-permute-start.4 = (bf16[256,256]{1,0:T(8,128)(2,1)S(1)}, bf16[256,256]{1,0:T(8,128)(2,1)S(1)}, u32[]{:S(2)}, u32[]{:S(2)}) collective-permute-start(bf16[256,256]{1,0:T(8,128)(2,1)S(1)} %get-tuple-element.58), channel_id=1, source_target_pairs={{0,6},{2,4},{4,2},{6,0},{1,7},{3,5},{5,3},{7,1},{8,14},{10,12},{12... | collective-permute-start | bytes 393224 | tf_op jit(solution)/shard_map/ppermute | solution.py:431
  7.3 17.2 %collective-permute-start.5 = (bf16[256,256]{1,0:T(8,128)(2,1)S(1)}, bf16[256,256]{1,0:T(8,128)(2,1)S(1)}, u32[]{:S(2)}, u32[]{:S(2)}) collective-permute-start(bf16[256,256]{1,0:T(8,128)(2,1)S(1)} %get-tuple-element.59), channel_id=1, source_target_pairs={{0,2},{2,0},{4,6},{6,4},{1,3},{3,1},{5,7},{7,5},{8,10},{10,8},{12,... | collective-permute-start | bytes 393224 | tf_op jit(solution)/shard_map/ppermute | solution.py:431
  9.9 14.6 %copy-start.4 = (bf16[512,512]{1,0:T(8,128)(2,1)S(1)}, bf16[512,512]{1,0:T(8,128)(2,1)}, u32[]{:S(2)}) copy-start(bf16[512,512]{1,0:T(8,128)(2,1)} %constant.8.clone.refs_4_.refs_0_.refs_2_) | copy-start | bytes 1572868
  11.2 16.7 %collective-permute-start.9 = (bf16[256,256]{1,0:T(8,128)(2,1)S(1)}, bf16[256,256]{1,0:T(8,128)(2,1)S(1)}, u32[]{:S(2)}, u32[]{:S(2)}) collective-permute-start(bf16[256,256]{1,0:T(8,128)(2,1)S(1)} %get-tuple-element.66), channel_id=1, source_target_pairs={{0,4},{2,6},{4,0},{6,2},{1,5},{3,7},{5,1},{7,3},{8,12},{10,14},{12... | collective-permute-start | bytes 393224 | tf_op jit(solution)/shard_map/ppermute | solution.py:431
  12.7 22.6 %collective-permute-start.10 = (bf16[256,256]{1,0:T(8,128)(2,1)S(1)}, bf16[256,256]{1,0:T(8,128)(2,1)S(1)}, u32[]{:S(2)}, u32[]{:S(2)}) collective-permute-start(bf16[256,256]{1,0:T(8,128)(2,1)S(1)} %get-tuple-element.67), channel_id=1, source_target_pairs={{0,6},{2,4},{4,2},{6,0},{1,7},{3,5},{5,3},{7,1},{8,14},{10,12},{12... | collective-permute-start | bytes 393224 | tf_op jit(solution)/shard_map/ppermute | solution.py:431
  16.3 18.9 %collective-permute-start.11 = (bf16[256,256]{1,0:T(8,128)(2,1)S(1)}, bf16[256,256]{1,0:T(8,128)(2,1)S(1)}, u32[]{:S(2)}, u32[]{:S(2)}) collective-permute-start(bf16[256,256]{1,0:T(8,128)(2,1)S(1)} %get-tuple-element.68), channel_id=1, source_target_pairs={{0,2},{2,0},{4,6},{6,4},{1,3},{3,1},{5,7},{7,5},{8,10},{10,8},{12,... | collective-permute-start | bytes 393224 | tf_op jit(solution)/shard_map/ppermute | solution.py:431
  25.5 13.5 %collective-permute-start.6 = (bf16[256,256]{1,0:T(8,128)(2,1)S(1)}, bf16[256,256]{1,0:T(8,128)(2,1)S(1)}, u32[]{:S(2)}, u32[]{:S(2)}) collective-permute-start(bf16[256,256]{1,0:T(8,128)(2,1)S(1)} %get-tuple-element.61), channel_id=1, source_target_pairs={{0,4},{2,6},{4,0},{6,2},{1,5},{3,7},{5,1},{7,3},{8,12},{10,14},{12... | collective-permute-start | bytes 393224 | tf_op jit(solution)/shard_map/ppermute | solution.py:431
  25.6 20.9 %collective-permute-start.7 = (bf16[256,256]{1,0:T(8,128)(2,1)S(1)}, bf16[256,256]{1,0:T(8,128)(2,1)S(1)}, u32[]{:S(2)}, u32[]{:S(2)}) collective-permute-start(bf16[256,256]{1,0:T(8,128)(2,1)S(1)} %get-tuple-element.62), channel_id=1, source_target_pairs={{0,6},{2,4},{4,2},{6,0},{1,7},{3,5},{5,3},{7,1},{8,14},{10,12},{12... | collective-permute-start | bytes 393224 | tf_op jit(solution)/shard_map/ppermute | solution.py:431
  27.9 18.6 %collective-permute-start.8 = (bf16[256,256]{1,0:T(8,128)(2,1)S(1)}, bf16[256,256]{1,0:T(8,128)(2,1)S(1)}, u32[]{:S(2)}, u32[]{:S(2)}) collective-permute-start(bf16[256,256]{1,0:T(8,128)(2,1)S(1)} %get-tuple-element.63), channel_id=1, source_target_pairs={{0,2},{2,0},{4,6},{6,4},{1,3},{3,1},{5,7},{7,5},{8,10},{10,8},{12,... | collective-permute-start | bytes 393224 | tf_op jit(solution)/shard_map/ppermute | solution.py:431
  36.2 13.6 %collective-permute-start.12 = (bf16[256,256]{1,0:T(8,128)(2,1)S(1)}, bf16[256,256]{1,0:T(8,128)(2,1)S(1)}, u32[]{:S(2)}, u32[]{:S(2)}) collective-permute-start(bf16[256,256]{1,0:T(8,128)(2,1)S(1)} %get-tuple-element.70), channel_id=1, source_target_pairs={{0,4},{2,6},{4,0},{6,2},{1,5},{3,7},{5,1},{7,3},{8,12},{10,14},{12... | collective-permute-start | bytes 393224 | tf_op jit(solution)/shard_map/ppermute | solution.py:431
  36.3 16.3 %collective-permute-start.13 = (bf16[256,256]{1,0:T(8,128)(2,1)S(1)}, bf16[256,256]{1,0:T(8,128)(2,1)S(1)}, u32[]{:S(2)}, u32[]{:S(2)}) collective-permute-start(bf16[256,256]{1,0:T(8,128)(2,1)S(1)} %get-tuple-element.71), channel_id=1, source_target_pairs={{0,6},{2,4},{4,2},{6,0},{1,7},{3,5},{5,3},{7,1},{8,14},{10,12},{12... | collective-permute-start | bytes 393224 | tf_op jit(solution)/shard_map/ppermute | solution.py:431
  39.1 13.6 %collective-permute-start.14 = (bf16[256,256]{1,0:T(8,128)(2,1)S(1)}, bf16[256,256]{1,0:T(8,128)(2,1)S(1)}, u32[]{:S(2)}, u32[]{:S(2)}) collective-permute-start(bf16[256,256]{1,0:T(8,128)(2,1)S(1)} %get-tuple-element.72), channel_id=1, source_target_pairs={{0,2},{2,0},{4,6},{6,4},{1,3},{3,1},{5,7},{7,5},{8,10},{10,8},{12,... | collective-permute-start | bytes 393224 | tf_op jit(solution)/shard_map/ppermute | solution.py:431
  54.1 12.1 %collective-permute-start.20 = (bf16[256,256]{1,0:T(8,128)(2,1)S(1)}, bf16[256,256]{1,0:T(8,128)(2,1)S(1)}, u32[]{:S(2)}, u32[]{:S(2)}) collective-permute-start(bf16[256,256]{1,0:T(8,128)(2,1)S(1)} %get-tuple-element.87), channel_id=1, source_target_pairs={{0,12},{2,14},{4,8},{6,10},{8,20},{10,22},{12,16},{14,18},{16,28},... | collective-permute-start | bytes 393224 | tf_op jit(solution)/shard_map/ppermute | solution.py:428
  55.4 17.9 %collective-permute-start.21 = (bf16[256,256]{1,0:T(8,128)(2,1)S(1)}, bf16[256,256]{1,0:T(8,128)(2,1)S(1)}, u32[]{:S(2)}, u32[]{:S(2)}) collective-permute-start(bf16[256,256]{1,0:T(8,128)(2,1)S(1)} %get-tuple-element.88), channel_id=1, source_target_pairs={{0,14},{2,12},{4,10},{6,8},{8,22},{10,20},{12,18},{14,16},{16,30},... | collective-permute-start | bytes 393224 | tf_op jit(solution)/shard_map/ppermute | solution.py:428
  57.3 15.9 %collective-permute-start.22 = (bf16[256,256]{1,0:T(8,128)(2,1)S(1)}, bf16[256,256]{1,0:T(8,128)(2,1)S(1)}, u32[]{:S(2)}, u32[]{:S(2)}) collective-permute-start(bf16[256,256]{1,0:T(8,128)(2,1)S(1)} %get-tuple-element.89), channel_id=1, source_target_pairs={{0,10},{2,8},{4,14},{6,12},{8,18},{10,16},{12,22},{14,20},{16,26},... | collective-permute-start | bytes 393224 | tf_op jit(solution)/shard_map/ppermute | solution.py:428
  60.5 12.7 %collective-permute-start.23 = (bf16[256,256]{1,0:T(8,128)(2,1)S(1)}, bf16[256,256]{1,0:T(8,128)(2,1)S(1)}, u32[]{:S(2)}, u32[]{:S(2)}) collective-permute-start(bf16[256,256]{1,0:T(8,128)(2,1)S(1)} %get-tuple-element.90), channel_id=1, source_target_pairs={{0,8},{2,10},{4,12},{6,14},{8,16},{10,18},{12,20},{14,22},{16,24},... | collective-permute-start | bytes 393224 | tf_op jit(solution)/shard_map/ppermute | solution.py:428
  61.2 25.7 %collective-permute-start.18 = (bf16[256,256]{1,0:T(8,128)(2,1)S(1)}, bf16[256,256]{1,0:T(8,128)(2,1)S(1)}, u32[]{:S(2)}, u32[]{:S(2)}) collective-permute-start(bf16[256,256]{1,0:T(8,128)(2,1)S(1)} %get-tuple-element.76.refs_0_), channel_id=1, source_target_pairs={{0,8},{2,10},{4,12},{6,14},{8,16},{10,18},{12,20},{14,22},{16,24},... | collective-permute-start | bytes 393224 | tf_op jit(solution)/shard_map/ppermute | solution.py:428
  66.1 9.9 %collective-permute-start.15 = (bf16[256,256]{1,0:T(8,128)(2,1)S(1)}, bf16[256,256]{1,0:T(8,128)(2,1)S(1)}, u32[]{:S(2)}, u32[]{:S(2)}) collective-permute-start(bf16[256,256]{1,0:T(8,128)(2,1)S(1)} %get-tuple-element.79), channel_id=1, source_target_pairs={{0,12},{2,14},{4,8},{6,10},{8,20},{10,22},{12,16},{14,18},{16,28},... | collective-permute-start | bytes 393224 | tf_op jit(solution)/shard_map/ppermute | solution.py:428
  73.2 13.7 %collective-permute-start.16 = (bf16[256,256]{1,0:T(8,128)(2,1)S(1)}, bf16[256,256]{1,0:T(8,128)(2,1)S(1)}, u32[]{:S(2)}, u32[]{:S(2)}) collective-permute-start(bf16[256,256]{1,0:T(8,128)(2,1)S(1)} %get-tuple-element.80), channel_id=1, source_target_pairs={{0,14},{2,12},{4,10},{6,8},{8,22},{10,20},{12,18},{14,16},{16,30},... | collective-permute-start | bytes 393224 | tf_op jit(solution)/shard_map/ppermute | solution.py:428
  73.2 13.7 %collective-permute-start.17 = (bf16[256,256]{1,0:T(8,128)(2,1)S(1)}, bf16[256,256]{1,0:T(8,128)(2,1)S(1)}, u32[]{:S(2)}, u32[]{:S(2)}) collective-permute-start(bf16[256,256]{1,0:T(8,128)(2,1)S(1)} %get-tuple-element.81), channel_id=1, source_target_pairs={{0,10},{2,8},{4,14},{6,12},{8,18},{10,16},{12,22},{14,20},{16,26},... | collective-permute-start | bytes 393224 | tf_op jit(solution)/shard_map/ppermute | solution.py:428
  74.3 16.4 %collective-permute-start.24 = (bf16[256,256]{1,0:T(8,128)(2,1)S(1)}, bf16[256,256]{1,0:T(8,128)(2,1)S(1)}, u32[]{:S(2)}, u32[]{:S(2)}) collective-permute-start(bf16[256,256]{1,0:T(8,128)(2,1)S(1)} %get-tuple-element.91), channel_id=1, source_target_pairs={{0,4},{2,6},{4,0},{6,2},{1,5},{3,7},{5,1},{7,3},{8,12},{10,14},{12... | collective-permute-start | bytes 393224 | tf_op jit(solution)/shard_map/ppermute | solution.py:431
  76.0 15.5 %collective-permute-start.25 = (bf16[256,256]{1,0:T(8,128)(2,1)S(1)}, bf16[256,256]{1,0:T(8,128)(2,1)S(1)}, u32[]{:S(2)}, u32[]{:S(2)}) collective-permute-start(bf16[256,256]{1,0:T(8,128)(2,1)S(1)} %get-tuple-element.92), channel_id=1, source_target_pairs={{0,6},{2,4},{4,2},{6,0},{1,7},{3,5},{5,3},{7,1},{8,14},{10,12},{12... | collective-permute-start | bytes 393224 | tf_op jit(solution)/shard_map/ppermute | solution.py:431
  86.9 11.0 %collective-permute-start.26 = (bf16[256,256]{1,0:T(8,128)(2,1)S(1)}, bf16[256,256]{1,0:T(8,128)(2,1)S(1)}, u32[]{:S(2)}, u32[]{:S(2)}) collective-permute-start(bf16[256,256]{1,0:T(8,128)(2,1)S(1)} %get-tuple-element.93), channel_id=1, source_target_pairs={{0,2},{2,0},{4,6},{6,4},{1,3},{3,1},{5,7},{7,5},{8,10},{10,8},{12,... | collective-permute-start | bytes 393224 | tf_op jit(solution)/shard_map/ppermute | solution.py:431
  87.9 10.9 %collective-permute-start.27 = (bf16[256,256]{1,0:T(8,128)(2,1)S(1)}, bf16[256,256]{1,0:T(8,128)(2,1)S(1)}, u32[]{:S(2)}, u32[]{:S(2)}) collective-permute-start(bf16[256,256]{1,0:T(8,128)(2,1)S(1)} %get-tuple-element.95), channel_id=1, source_target_pairs={{0,4},{2,6},{4,0},{6,2},{1,5},{3,7},{5,1},{7,3},{8,12},{10,14},{12... | collective-permute-start | bytes 393224 | tf_op jit(solution)/shard_map/ppermute | solution.py:431
  88.0 15.0 %collective-permute-start.28 = (bf16[256,256]{1,0:T(8,128)(2,1)S(1)}, bf16[256,256]{1,0:T(8,128)(2,1)S(1)}, u32[]{:S(2)}, u32[]{:S(2)}) collective-permute-start(bf16[256,256]{1,0:T(8,128)(2,1)S(1)} %get-tuple-element.96), channel_id=1, source_target_pairs={{0,6},{2,4},{4,2},{6,0},{1,7},{3,5},{5,3},{7,1},{8,14},{10,12},{12... | collective-permute-start | bytes 393224 | tf_op jit(solution)/shard_map/ppermute | solution.py:431
  90.6 12.4 %collective-permute-start.29 = (bf16[256,256]{1,0:T(8,128)(2,1)S(1)}, bf16[256,256]{1,0:T(8,128)(2,1)S(1)}, u32[]{:S(2)}, u32[]{:S(2)}) collective-permute-start(bf16[256,256]{1,0:T(8,128)(2,1)S(1)} %get-tuple-element.97), channel_id=1, source_target_pairs={{0,2},{2,0},{4,6},{6,4},{1,3},{3,1},{5,7},{7,5},{8,10},{10,8},{12,... | collective-permute-start | bytes 393224 | tf_op jit(solution)/shard_map/ppermute | solution.py:431
  91.6 13.5 %collective-permute-start.19 = (bf16[256,1024]{1,0:T(8,128)(2,1)S(1)}, bf16[256,1024]{1,0:T(8,128)(2,1)S(1)}, u32[]{:S(2)}, u32[]{:S(2)}) collective-permute-start(bf16[256,1024]{1,0:T(8,128)(2,1)S(1)} %other_rows.1), channel_id=1, source_target_pairs={{0,1},{1,0},{2,3},{3,2},{4,5},{5,4},{6,7},{7,6},{8,9},{9,8},{10,11... | collective-permute-start | bytes 1572872 | tf_op jit(solution)/shard_map/ppermute | solution.py:393
  103.4 2.7 %collective-permute-start.30 = (bf16[256,1024]{1,0:T(8,128)(2,1)S(1)}, bf16[256,1024]{1,0:T(8,128)(2,1)S(1)}, u32[]{:S(2)}, u32[]{:S(2)}) collective-permute-start(bf16[256,1024]{1,0:T(8,128)(2,1)S(1)} %half_space.3), channel_id=1, source_target_pairs={{0,1},{1,0},{2,3},{3,2},{4,5},{5,4},{6,7},{7,6},{8,9},{9,8},{10,11... | collective-permute-start | bytes 1572872 | tf_op jit(solution)/shard_map/ppermute | solution.py:393
  (9 other events, 44.5 us)

commit v5 on v4

--- a/solution.py
+++ b/solution.py
@@ -150,30 +150,7 @@
             ]
 
 
-def own_modes_kernel(fields_ref, table_ref, out_ref):
-    rows, half = out_ref.shape
-    mine = rows_of(lax.axis_index("core") * rows, rows)
-    out_ref[...] = dot(fields_ref[mine, :half] + fields_ref[mine, half:], table_ref[...]).astype(BF16)
-
-
-def even_to_modes_kernel(other_ref, own_ref, table_ref, *refs):
-    outs, modes = refs[:-1], refs[-1]
-    rows, half = own_ref.shape
-    own = rows // 2
-    core = lax.axis_index("core")
-    theirs = rows_of(core * rows, rows)
-    modes[...] = dot(other_ref[theirs, :half] + other_ref[theirs, half:], table_ref[...]).astype(BF16)
-    block = half // len(outs)
-    for k, out in zip(partners(len(outs)), outs):
-        columns = rows_of((lax.axis_index("z") ^ k) * block, block)
-        for part in range(2):
-            lanes = slice(part * block, (part + 1) * block)
-            lines = slice(part * own, (part + 1) * own)
-            out[rows_of(core * own, own), lanes] = own_ref[lines, columns]
-            out[rows_of((core ^ 1) * own, own), lanes] = modes[lines, columns]
-
-
-def odd_pieces(fields_ref, other_ref, table_ref, *refs):
+def all_pieces(sign, fields_ref, other_ref, table_ref, *refs):
     outs, (folded, modes) = refs[:-2], refs[-2:]
     half = table_ref.shape[0]
     own = folded.shape[0] // 4
@@ -182,7 +159,7 @@
         mine = rows_of((2 * core + part) * own, own)
         for index, source in enumerate((fields_ref, other_ref)):
             there = rows_of(2 * part * own + (core ^ index) * own, own)
-            folded[there, :] = source[mine, :half] - source[mine, half:]
+            folded[there, :] = source[mine, :half] + sign * source[mine, half:]
     modes[...] = dot(folded[...], table_ref[...]).astype(BF16)
     split_modes(lax.axis_index("z"), modes, outs)
 
@@ -195,7 +172,7 @@
     for index, block in enumerate((blocks_ref[depth], second)):
         settings_ref[2 * index] = omega_top * (block.astype(F32) + 1.0) / NFREQ
         settings_ref[2 * index + 1] = reference_ref[0]
-    odd_pieces(*refs[:-3], *refs[-2:])
+    all_pieces(-1, *refs[:-3], *refs[-2:])
 
 
 def along_x_kernel(
@@ -443,12 +420,9 @@
         )[0]
 
     share = (rows, half)
-    own_evens = call(
-        own_modes_kernel, (fields, even_y_t), [of(share)], flops=flops // 2, name="own_modes"
-    )[0]
     evens = call(
-        even_to_modes_kernel, (fields_other, own_evens, even_y_t),
-        pieces_of, [pltpu.VMEM(share, BF16)], flops // 2, "even_to_modes",
+        functools.partial(all_pieces, 1), (fields, fields_other, even_y_t),
+        pieces_of, [part, part], flops, "even_to_modes",
     )
     *odds, settings = call(
         odd_to_modes_kernel,

time: 108 us -> 110 us (1.019)
  waiting for transfers between devices: 45.5 us -> 47.3 us
    ppermute x5, waiting for transfers between devices: 1.08 us -> 3.06 us  [other_core(): return lax.ppermute(value, 'core', [(0, 1), (1, 0)])]
    pallas_call x21 -> x20, Pallas kernels: 18.3 us -> 18.3 us  [call(): pl.pallas_call(functools.partial(after, len(behind), kernel), out_shape=t...]
  transfers between devices with their start and end apart: 31 -> 31, of which waited for: 10 -> 11; matrix products, arithmetic and copies ran while one was open for 0% -> 0% of each run, Pallas kernels for 15% -> 14%
where the time goes in v5:
time: 110 us; the launch traced here: 109 us
  waiting for transfers between devices  47.3 us (43%)
  starting transfers between devices  39.2 us (36%)
  Pallas kernels  18.3 us (17%)
  local copies, waits for them, and re-layouts  2.31 us (2%)
  between operations  2.24 us (2%)
    ppermute x18, waiting for transfers between devices, exchange(): got.append(lax.ppermute(piece, 'z', pairs) if k else piece)  28.5 us
    ppermute x18, starting transfers between devices, exchange(): got.append(lax.ppermute(piece, 'z', pairs) if k else piece)  20.4 us
    pallas_call x20, Pallas kernels, call(): pl.pallas_call(functools.partial(after, len(behind), kernel), out_shape=t...  18.3 us
    ppermute x8, waiting for transfers between devices, exchange(): got.append(lax.ppermute(piece, ('depth', 'z'), pairs))  15.7 us
    ppermute x8, starting transfers between devices, exchange(): got.append(lax.ppermute(piece, ('depth', 'z'), pairs))  9.84 us
    ppermute x5, starting transfers between devices, other_core(): return lax.ppermute(value, 'core', [(0, 1), (1, 0)])  8.88 us
    ppermute x5, waiting for transfers between devices, other_core(): return lax.ppermute(value, 'core', [(0, 1), (1, 0)])  3.06 us
    unnamed x20, local copies, waits for them, and re-layouts  2.31 us
  transfers between devices with their start and end apart: 31, of which 11 were waited for; matrix products, arithmetic and copies ran while one was open for 0% of the time, Pallas kernels for 14%

profile of v5, /device:TPU:9, one launch (start us, length us, event | category | flops | bytes accessed | tf_op | source)
XLA Modules:
  0.0 109.2 jit_solution(1569401019549923124)
XLA Ops:
  1.9 2.0 %collective-permute-done.2.refs_6_.refs_1_ = bf16[512,1024]{1,0:T(8,128)(2,1)S(1)} collective-permute-done((bf16[512,1024]{1,0:T(8,128)(2,1)}, bf16[512,1024]{1,0:T(8,128)(2,1)S(1)}, u32[]{:S(2)}, u32[]{:S(2)}) %collective-permute-start.2) | collective-permute-done | bytes 1048608 | tf_op jit(solution)/shard_map/ppermute | solution.py:370
  4.9 1.2 %copy-done.5 = bf16[1,2,2,128,1024]{4,3,2,1,0:T(8,128)(2,1)S(1)} copy-done((bf16[1,2,2,128,1024]{4,3,2,1,0:T(8,128)(2,1)S(1)}, bf16[1,2,2,128,1024]{4,3,2,1,0:T(8,128)(2,1)}, u32[]{:S(2)}) %copy-start.5) | copy-done | bytes 1048600
  6.8 2.4 %collective-permute-start.3 = (bf16[256,256]{1,0:T(8,128)(2,1)S(1)}, bf16[256,256]{1,0:T(8,128)(2,1)S(1)}, u32[]{:S(2)}, u32[]{:S(2)}) collective-permute-start(bf16[256,256]{1,0:T(8,128)(2,1)S(1)} %get-tuple-element.57), channel_id=1, source_target_pairs={{0,4},{2,6},{4,0},{6,2},{1,5},{3,7},{5,1},{7,3},{8,12},{10,14},{12... | collective-permute-start | bytes 393224 | tf_op jit(solution)/shard_map/ppermute | solution.py:408
  9.1 1.3 %collective-permute-start.5 = (bf16[256,256]{1,0:T(8,128)(2,1)S(1)}, bf16[256,256]{1,0:T(8,128)(2,1)S(1)}, u32[]{:S(2)}, u32[]{:S(2)}) collective-permute-start(bf16[256,256]{1,0:T(8,128)(2,1)S(1)} %get-tuple-element.59), channel_id=1, source_target_pairs={{0,2},{2,0},{4,6},{6,4},{1,3},{3,1},{5,7},{7,5},{8,10},{10,8},{12,... | collective-permute-start | bytes 393224 | tf_op jit(solution)/shard_map/ppermute | solution.py:408
  11.8 1.3 %odd_to_modes.1 = (bf16[256,256]{1,0:T(8,128)(2,1)S(1)}, bf16[256,256]{1,0:T(8,128)(2,1)S(1)}, bf16[256,256]{1,0:T(8,128)(2,1)S(1)}, bf16[256,256]{1,0:T(8,128)(2,1)S(1)}, f32[4]{0:T(128)S(1)}) custom-call(bf16[512,1024]{1,0:T(8,128)(2,1)S(1)} %collective-permute-done.refs_0_.refs_3_, f32[128,1024]{1,0:T(8,128)S(1)} %collective-permute-done.1.refs_1_.refs_2_.refs_3_, ...), custom_call_target="tpu_custom_call" | custom-call | flops 268435456 | bytes 3145768 | tf_op jit(solution)/shard_map/odd_to_modes/pallas_call | solution.py:342
  13.1 1.5 %collective-permute-start.9 = (bf16[256,256]{1,0:T(8,128)(2,1)S(1)}, bf16[256,256]{1,0:T(8,128)(2,1)S(1)}, u32[]{:S(2)}, u32[]{:S(2)}) collective-permute-start(bf16[256,256]{1,0:T(8,128)(2,1)S(1)} %get-tuple-element.66), channel_id=1, source_target_pairs={{0,4},{2,6},{4,0},{6,2},{1,5},{3,7},{5,1},{7,3},{8,12},{10,14},{12... | collective-permute-start | bytes 393224 | tf_op jit(solution)/shard_map/ppermute | solution.py:408
  16.5 1.7 %phases.2 = (f32[256,1024]{1,0:T(8,128)S(1)}, f32[256,1024]{1,0:T(8,128)S(1)}) custom-call(f32[4]{0:T(128)S(1)} %get-tuple-element.51.refs_0_.refs_1_, f32[128,1024]{1,0:T(8,128)S(1)} %bitcast.9, f32[128,1024]{1,0:T(8,128)S(1)} %collective-permute-done.1.refs_1_.refs_2_.refs_3_), custom_call_target="tpu_custom_call" | custom-call | flops 104857600 | bytes 3145744 | tf_op jit(solution)/shard_map/phases/pallas_call | solution.py:342
  18.2 2.2 %collective-permute-start.11 = (bf16[256,256]{1,0:T(8,128)(2,1)S(1)}, bf16[256,256]{1,0:T(8,128)(2,1)S(1)}, u32[]{:S(2)}, u32[]{:S(2)}) collective-permute-start(bf16[256,256]{1,0:T(8,128)(2,1)S(1)} %get-tuple-element.68), channel_id=1, source_target_pairs={{0,2},{2,0},{4,6},{6,4},{1,3},{3,1},{5,7},{7,5},{8,10},{10,8},{12,... | collective-permute-start | bytes 393224 | tf_op jit(solution)/shard_map/ppermute | solution.py:408
  20.4 5.9 %collective-permute-done.4.refs_9_ = bf16[256,256]{1,0:T(8,128)(2,1)S(1)} collective-permute-done((bf16[256,256]{1,0:T(8,128)(2,1)S(1)}, bf16[256,256]{1,0:T(8,128)(2,1)S(1)}, u32[]{:S(2)}, u32[]{:S(2)}) %collective-permute-start.4) | collective-permute-done | bytes 131104 | tf_op jit(solution)/shard_map/ppermute | solution.py:408
  27.4 2.3 %collective-permute-start.7 = (bf16[256,256]{1,0:T(8,128)(2,1)S(1)}, bf16[256,256]{1,0:T(8,128)(2,1)S(1)}, u32[]{:S(2)}, u32[]{:S(2)}) collective-permute-start(bf16[256,256]{1,0:T(8,128)(2,1)S(1)} %get-tuple-element.62), channel_id=1, source_target_pairs={{0,6},{2,4},{4,2},{6,0},{1,7},{3,5},{5,3},{7,1},{8,14},{10,12},{12... | collective-permute-start | bytes 393224 | tf_op jit(solution)/shard_map/ppermute | solution.py:408
  29.7 1.3 %collective-permute-start.8 = (bf16[256,256]{1,0:T(8,128)(2,1)S(1)}, bf16[256,256]{1,0:T(8,128)(2,1)S(1)}, u32[]{:S(2)}, u32[]{:S(2)}) collective-permute-start(bf16[256,256]{1,0:T(8,128)(2,1)S(1)} %get-tuple-element.63), channel_id=1, source_target_pairs={{0,2},{2,0},{4,6},{6,4},{1,3},{3,1},{5,7},{7,5},{8,10},{10,8},{12,... | collective-permute-start | bytes 393224 | tf_op jit(solution)/shard_map/ppermute | solution.py:408
  31.0 6.1 %collective-permute-done.10.refs_7_ = bf16[256,256]{1,0:T(8,128)(2,1)S(1)} collective-permute-done((bf16[256,256]{1,0:T(8,128)(2,1)S(1)}, bf16[256,256]{1,0:T(8,128)(2,1)S(1)}, u32[]{:S(2)}, u32[]{:S(2)}) %collective-permute-start.10) | collective-permute-done | bytes 131104 | tf_op jit(solution)/shard_map/ppermute | solution.py:408
  38.1 2.7 %collective-permute-start.13 = (bf16[256,256]{1,0:T(8,128)(2,1)S(1)}, bf16[256,256]{1,0:T(8,128)(2,1)S(1)}, u32[]{:S(2)}, u32[]{:S(2)}) collective-permute-start(bf16[256,256]{1,0:T(8,128)(2,1)S(1)} %get-tuple-element.71), channel_id=1, source_target_pairs={{0,6},{2,4},{4,2},{6,0},{1,7},{3,5},{5,3},{7,1},{8,14},{10,12},{12... | collective-permute-start | bytes 393224 | tf_op jit(solution)/shard_map/ppermute | solution.py:408
  40.8 1.1 %collective-permute-start.14 = (bf16[256,256]{1,0:T(8,128)(2,1)S(1)}, bf16[256,256]{1,0:T(8,128)(2,1)S(1)}, u32[]{:S(2)}, u32[]{:S(2)}) collective-permute-start(bf16[256,256]{1,0:T(8,128)(2,1)S(1)} %get-tuple-element.72), channel_id=1, source_target_pairs={{0,2},{2,0},{4,6},{6,4},{1,3},{3,1},{5,7},{7,5},{8,10},{10,8},{12,... | collective-permute-start | bytes 393224 | tf_op jit(solution)/shard_map/ppermute | solution.py:408
  41.9 6.3 %collective-permute-done.7.refs_2_ = bf16[256,256]{1,0:T(8,128)(2,1)S(1)} collective-permute-done((bf16[256,256]{1,0:T(8,128)(2,1)S(1)}, bf16[256,256]{1,0:T(8,128)(2,1)S(1)}, u32[]{:S(2)}, u32[]{:S(2)}) %collective-permute-start.7) | collective-permute-done | bytes 131104 | tf_op jit(solution)/shard_map/ppermute | solution.py:408
  48.8 2.8 %collective-permute-done.12.refs_7_ = bf16[256,256]{1,0:T(8,128)(2,1)S(1)} collective-permute-done((bf16[256,256]{1,0:T(8,128)(2,1)S(1)}, bf16[256,256]{1,0:T(8,128)(2,1)S(1)}, u32[]{:S(2)}, u32[]{:S(2)}) %collective-permute-start.12) | collective-permute-done | bytes 131104 | tf_op jit(solution)/shard_map/ppermute | solution.py:408
  51.6 2.8 %collective-permute-done.13.refs_8_ = bf16[256,256]{1,0:T(8,128)(2,1)S(1)} collective-permute-done((bf16[256,256]{1,0:T(8,128)(2,1)S(1)}, bf16[256,256]{1,0:T(8,128)(2,1)S(1)}, u32[]{:S(2)}, u32[]{:S(2)}) %collective-permute-start.13) | collective-permute-done | bytes 131104 | tf_op jit(solution)/shard_map/ppermute | solution.py:408
  54.4 1.4 %turn_around.1 = (bf16[256,256]{1,0:T(8,128)(2,1)S(1)}, bf16[256,256]{1,0:T(8,128)(2,1)S(1)}, bf16[256,256]{1,0:T(8,128)(2,1)S(1)}, bf16[256,256]{1,0:T(8,128)(2...) custom-call(f32[256,1024]{1,0:T(8,128)S(1)} %get-tuple-element.52.refs_1_.refs_0_, ...), custom_call_target="tpu_custom_call" | custom-call | flops 536870912 | bytes 8912896 | tf_op jit(solution)/shard_map/turn_around/pallas_call | solution.py:342
  55.9 1.3 %collective-permute-start.20 = (bf16[256,256]{1,0:T(8,128)(2,1)S(1)}, bf16[256,256]{1,0:T(8,128)(2,1)S(1)}, u32[]{:S(2)}, u32[]{:S(2)}) collective-permute-start(bf16[256,256]{1,0:T(8,128)(2,1)S(1)} %get-tuple-element.87), channel_id=1, source_target_pairs={{0,12},{2,14},{4,8},{6,10},{8,20},{10,22},{12,16},{14,18},{16,28},... | collective-permute-start | bytes 393224 | tf_op jit(solution)/shard_map/ppermute | solution.py:405
  57.2 2.0 %collective-permute-start.21 = (bf16[256,256]{1,0:T(8,128)(2,1)S(1)}, bf16[256,256]{1,0:T(8,128)(2,1)S(1)}, u32[]{:S(2)}, u32[]{:S(2)}) collective-permute-start(bf16[256,256]{1,0:T(8,128)(2,1)S(1)} %get-tuple-element.88), channel_id=1, source_target_pairs={{0,14},{2,12},{4,10},{6,8},{8,22},{10,20},{12,18},{14,16},{16,30},... | collective-permute-start | bytes 393224 | tf_op jit(solution)/shard_map/ppermute | solution.py:405
  59.1 3.2 %collective-permute-start.22 = (bf16[256,256]{1,0:T(8,128)(2,1)S(1)}, bf16[256,256]{1,0:T(8,128)(2,1)S(1)}, u32[]{:S(2)}, u32[]{:S(2)}) collective-permute-start(bf16[256,256]{1,0:T(8,128)(2,1)S(1)} %get-tuple-element.89), channel_id=1, source_target_pairs={{0,10},{2,8},{4,14},{6,12},{8,18},{10,16},{12,22},{14,20},{16,26},... | collective-permute-start | bytes 393224 | tf_op jit(solution)/shard_map/ppermute | solution.py:405
  63.0 1.3 %collective-permute-start.18 = (bf16[256,256]{1,0:T(8,128)(2,1)S(1)}, bf16[256,256]{1,0:T(8,128)(2,1)S(1)}, u32[]{:S(2)}, u32[]{:S(2)}) collective-permute-start(bf16[256,256]{1,0:T(8,128)(2,1)S(1)} %get-tuple-element.76.refs_0_), channel_id=1, source_target_pairs={{0,8},{2,10},{4,12},{6,14},{8,16},{10,18},{12,20},{14,22},{16,24},... | collective-permute-start | bytes 393224 | tf_op jit(solution)/shard_map/ppermute | solution.py:405
  66.2 1.7 %phases.3 = (f32[256,1024]{1,0:T(8,128)S(1)}, f32[256,1024]{1,0:T(8,128)S(1)}) custom-call(bf16[256,256]{1,0:T(8,128)(2,1)S(1)} %get-tuple-element.76.refs_0_, f32[4]{0:T(128)S(1)} %get-tuple-element.51.refs_0_.refs_1_, f32[128,1024]{1,0:T(8,128)S(1)} %bitcast.10, f32[128,1024]{1,0:T(8,128)S(1)} %collective-permute-done.1.refs_1_.refs_2_.refs_3_), custom_call_target="tpu_custom_call" | custom-call | flops 104857600 | bytes 3145744 | tf_op jit(solution)/shard_map/phases/pallas_call | solution.py:342
  68.0 2.0 %collective-permute-start.15 = (bf16[256,256]{1,0:T(8,128)(2,1)S(1)}, bf16[256,256]{1,0:T(8,128)(2,1)S(1)}, u32[]{:S(2)}, u32[]{:S(2)}) collective-permute-start(bf16[256,256]{1,0:T(8,128)(2,1)S(1)} %get-tuple-element.79), channel_id=1, source_target_pairs={{0,12},{2,14},{4,8},{6,10},{8,20},{10,22},{12,16},{14,18},{16,28},... | collective-permute-start | bytes 393224 | tf_op jit(solution)/shard_map/ppermute | solution.py:405
  70.0 5.1 %collective-permute-done.21.refs_9_ = bf16[256,256]{1,0:T(8,128)(2,1)S(1)} collective-permute-done((bf16[256,256]{1,0:T(8,128)(2,1)S(1)}, bf16[256,256]{1,0:T(8,128)(2,1)S(1)}, u32[]{:S(2)}, u32[]{:S(2)}) %collective-permute-start.21) | collective-permute-done | bytes 131104 | tf_op jit(solution)/shard_map/ppermute | solution.py:405
  76.1 1.7 %collective-permute-start.24 = (bf16[256,256]{1,0:T(8,128)(2,1)S(1)}, bf16[256,256]{1,0:T(8,128)(2,1)S(1)}, u32[]{:S(2)}, u32[]{:S(2)}) collective-permute-start(bf16[256,256]{1,0:T(8,128)(2,1)S(1)} %get-tuple-element.91), channel_id=1, source_target_pairs={{0,4},{2,6},{4,0},{6,2},{1,5},{3,7},{5,1},{7,3},{8,12},{10,14},{12... | collective-permute-start | bytes 393224 | tf_op jit(solution)/shard_map/ppermute | solution.py:408
  78.1 10.6 %collective-permute-done.16.refs_7_ = bf16[256,256]{1,0:T(8,128)(2,1)S(1)} collective-permute-done((bf16[256,256]{1,0:T(8,128)(2,1)S(1)}, bf16[256,256]{1,0:T(8,128)(2,1)S(1)}, u32[]{:S(2)}, u32[]{:S(2)}) %collective-permute-start.16) | collective-permute-done | bytes 131104 | tf_op jit(solution)/shard_map/ppermute | solution.py:405
  89.8 2.6 %collective-permute-start.28 = (bf16[256,256]{1,0:T(8,128)(2,1)S(1)}, bf16[256,256]{1,0:T(8,128)(2,1)S(1)}, u32[]{:S(2)}, u32[]{:S(2)}) collective-permute-start(bf16[256,256]{1,0:T(8,128)(2,1)S(1)} %get-tuple-element.96), channel_id=1, source_target_pairs={{0,6},{2,4},{4,2},{6,0},{1,7},{3,5},{5,3},{7,1},{8,14},{10,12},{12... | collective-permute-start | bytes 393224 | tf_op jit(solution)/shard_map/ppermute | solution.py:408
  93.4 6.4 %collective-permute-start.19 = (bf16[256,1024]{1,0:T(8,128)(2,1)S(1)}, bf16[256,1024]{1,0:T(8,128)(2,1)S(1)}, u32[]{:S(2)}, u32[]{:S(2)}) collective-permute-start(bf16[256,1024]{1,0:T(8,128)(2,1)S(1)} %other_rows.1), channel_id=1, source_target_pairs={{0,1},{1,0},{2,3},{3,2},{4,5},{5,4},{6,7},{7,6},{8,9},{9,8},{10,11... | collective-permute-start | bytes 1572872 | tf_op jit(solution)/shard_map/ppermute | solution.py:370
  100.6 4.1 %collective-permute-done.28.refs_5_ = bf16[256,256]{1,0:T(8,128)(2,1)S(1)} collective-permute-done((bf16[256,256]{1,0:T(8,128)(2,1)S(1)}, bf16[256,256]{1,0:T(8,128)(2,1)S(1)}, u32[]{:S(2)}, u32[]{:S(2)}) %collective-permute-start.28) | collective-permute-done | bytes 131104 | tf_op jit(solution)/shard_map/ppermute | solution.py:408
  105.2 1.2 %collective-permute-start.30 = (bf16[256,1024]{1,0:T(8,128)(2,1)S(1)}, bf16[256,1024]{1,0:T(8,128)(2,1)S(1)}, u32[]{:S(2)}, u32[]{:S(2)}) collective-permute-start(bf16[256,1024]{1,0:T(8,128)(2,1)S(1)} %half_space.3), channel_id=1, source_target_pairs={{0,1},{1,0},{2,3},{3,2},{4,5},{5,4},{6,7},{7,6},{8,9},{9,8},{10,11... | collective-permute-start | bytes 1572872 | tf_op jit(solution)/shard_map/ppermute | solution.py:370
  108.0 1.2 %finish.1 = (bf16[512,1024]{1,0:T(8,128)(2,1)}, f32[128,1024]{1,0:T(8,128)}) custom-call(bf16[512,1024]{1,0:T(8,128)(2,1)S(1)} %get-tuple-element.74.refs_1_.refs_0_, bf16[256,1024]{1,0:T(8,128)(2,1)S(1)} %collective-permute-done.19.refs_1_, bf16[256,1024]{1,0:T(8,128)(2,1)S(1)} %half_space.2.refs_2_, bf16[256,1024]{1,0:T(8,128)(2,1)S(1)} %collective-permute-done.30.refs_3_), custom_call_target="tpu_custom_call" | custom-call | flops 1048576 | bytes 4194304 | tf_op jit(solution)/shard_map/finish/pallas_call | solution.py:342
  (70 shorter events, 16.3 us)
Async XLA Ops:
  0.6 3.2 %collective-permute-start.2 = (bf16[512,1024]{1,0:T(8,128)(2,1)}, bf16[512,1024]{1,0:T(8,128)(2,1)S(1)}, u32[]{:S(2)}, u32[]{:S(2)}) collective-permute-start(bf16[512,1024]{1,0:T(8,128)(2,1)} %bitcast.5), channel_id=1, source_target_pairs={{0,1},{1,0},{2,3},{3,2},{4,5},{5,4},{6,7},{7,6},{8,9},{9,8},{10,11... | collective-permute-start | bytes 3145736 | tf_op jit(solution)/shard_map/ppermute | solution.py:370
  1.4 10.4 %collective-permute-start = (bf16[512,1024]{1,0:T(8,128)(2,1)}, bf16[512,1024]{1,0:T(8,128)(2,1)S(1)}, u32[]{:S(2)}, u32[]{:S(2)}) collective-permute-start(bf16[512,1024]{1,0:T(8,128)(2,1)} %bitcast.11), channel_id=1, source_target_pairs={{0,1},{1,0},{2,3},{3,2},{4,5},{5,4},{6,7},{7,6},{8,9},{9,8},{10,11... | collective-permute-start | bytes 3145736 | tf_op jit(solution)/shard_map/ppermute | solution.py:370
  1.4 10.3 %collective-permute-start.1 = (f32[128,1024]{1,0:T(8,128)}, f32[128,1024]{1,0:T(8,128)S(1)}, u32[]{:S(2)}, u32[]{:S(2)}) collective-permute-start(f32[128,1024]{1,0:T(8,128)} %bitcast.8), channel_id=1, source_target_pairs={{0,1},{1,0},{2,3},{3,2},{4,5},{5,4},{6,7},{7,6},{8,9},{9,8},{10,11... | collective-permute-start | bytes 1572872 | tf_op jit(solution)/shard_map/ppermute | solution.py:370
  6.8 11.4 %collective-permute-start.3 = (bf16[256,256]{1,0:T(8,128)(2,1)S(1)}, bf16[256,256]{1,0:T(8,128)(2,1)S(1)}, u32[]{:S(2)}, u32[]{:S(2)}) collective-permute-start(bf16[256,256]{1,0:T(8,128)(2,1)S(1)} %get-tuple-element.57), channel_id=1, source_target_pairs={{0,4},{2,6},{4,0},{6,2},{1,5},{3,7},{5,1},{7,3},{8,12},{10,14},{12... | collective-permute-start | bytes 393224 | tf_op jit(solution)/shard_map/ppermute | solution.py:408
  9.1 17.2 %collective-permute-start.4 = (bf16[256,256]{1,0:T(8,128)(2,1)S(1)}, bf16[256,256]{1,0:T(8,128)(2,1)S(1)}, u32[]{:S(2)}, u32[]{:S(2)}) collective-permute-start(bf16[256,256]{1,0:T(8,128)(2,1)S(1)} %get-tuple-element.58), channel_id=1, source_target_pairs={{0,6},{2,4},{4,2},{6,0},{1,7},{3,5},{5,3},{7,1},{8,14},{10,12},{12... | collective-permute-start | bytes 393224 | tf_op jit(solution)/shard_map/ppermute | solution.py:408
  9.1 17.2 %collective-permute-start.5 = (bf16[256,256]{1,0:T(8,128)(2,1)S(1)}, bf16[256,256]{1,0:T(8,128)(2,1)S(1)}, u32[]{:S(2)}, u32[]{:S(2)}) collective-permute-start(bf16[256,256]{1,0:T(8,128)(2,1)S(1)} %get-tuple-element.59), channel_id=1, source_target_pairs={{0,2},{2,0},{4,6},{6,4},{1,3},{3,1},{5,7},{7,5},{8,10},{10,8},{12,... | collective-permute-start | bytes 393224 | tf_op jit(solution)/shard_map/ppermute | solution.py:408
  11.8 14.6 %copy-start.4 = (bf16[512,512]{1,0:T(8,128)(2,1)S(1)}, bf16[512,512]{1,0:T(8,128)(2,1)}, u32[]{:S(2)}) copy-start(bf16[512,512]{1,0:T(8,128)(2,1)} %constant.9.clone.refs_2_.refs_5_.refs_3_.refs_4_) | copy-start | bytes 1572868
  13.1 16.6 %collective-permute-start.9 = (bf16[256,256]{1,0:T(8,128)(2,1)S(1)}, bf16[256,256]{1,0:T(8,128)(2,1)S(1)}, u32[]{:S(2)}, u32[]{:S(2)}) collective-permute-start(bf16[256,256]{1,0:T(8,128)(2,1)S(1)} %get-tuple-element.66), channel_id=1, source_target_pairs={{0,4},{2,6},{4,0},{6,2},{1,5},{3,7},{5,1},{7,3},{8,12},{10,14},{12... | collective-permute-start | bytes 393224 | tf_op jit(solution)/shard_map/ppermute | solution.py:408
  14.5 22.5 %collective-permute-start.10 = (bf16[256,256]{1,0:T(8,128)(2,1)S(1)}, bf16[256,256]{1,0:T(8,128)(2,1)S(1)}, u32[]{:S(2)}, u32[]{:S(2)}) collective-permute-start(bf16[256,256]{1,0:T(8,128)(2,1)S(1)} %get-tuple-element.67), channel_id=1, source_target_pairs={{0,6},{2,4},{4,2},{6,0},{1,7},{3,5},{5,3},{7,1},{8,14},{10,12},{12... | collective-permute-start | bytes 393224 | tf_op jit(solution)/shard_map/ppermute | solution.py:408
  18.2 18.8 %collective-permute-start.11 = (bf16[256,256]{1,0:T(8,128)(2,1)S(1)}, bf16[256,256]{1,0:T(8,128)(2,1)S(1)}, u32[]{:S(2)}, u32[]{:S(2)}) collective-permute-start(bf16[256,256]{1,0:T(8,128)(2,1)S(1)} %get-tuple-element.68), channel_id=1, source_target_pairs={{0,2},{2,0},{4,6},{6,4},{1,3},{3,1},{5,7},{7,5},{8,10},{10,8},{12,... | collective-permute-start | bytes 393224 | tf_op jit(solution)/shard_map/ppermute | solution.py:408
  27.4 13.5 %collective-permute-start.6 = (bf16[256,256]{1,0:T(8,128)(2,1)S(1)}, bf16[256,256]{1,0:T(8,128)(2,1)S(1)}, u32[]{:S(2)}, u32[]{:S(2)}) collective-permute-start(bf16[256,256]{1,0:T(8,128)(2,1)S(1)} %get-tuple-element.61), channel_id=1, source_target_pairs={{0,4},{2,6},{4,0},{6,2},{1,5},{3,7},{5,1},{7,3},{8,12},{10,14},{12... | collective-permute-start | bytes 393224 | tf_op jit(solution)/shard_map/ppermute | solution.py:408
  27.4 20.8 %collective-permute-start.7 = (bf16[256,256]{1,0:T(8,128)(2,1)S(1)}, bf16[256,256]{1,0:T(8,128)(2,1)S(1)}, u32[]{:S(2)}, u32[]{:S(2)}) collective-permute-start(bf16[256,256]{1,0:T(8,128)(2,1)S(1)} %get-tuple-element.62), channel_id=1, source_target_pairs={{0,6},{2,4},{4,2},{6,0},{1,7},{3,5},{5,3},{7,1},{8,14},{10,12},{12... | collective-permute-start | bytes 393224 | tf_op jit(solution)/shard_map/ppermute | solution.py:408
  29.7 18.6 %collective-permute-start.8 = (bf16[256,256]{1,0:T(8,128)(2,1)S(1)}, bf16[256,256]{1,0:T(8,128)(2,1)S(1)}, u32[]{:S(2)}, u32[]{:S(2)}) collective-permute-start(bf16[256,256]{1,0:T(8,128)(2,1)S(1)} %get-tuple-element.63), channel_id=1, source_target_pairs={{0,2},{2,0},{4,6},{6,4},{1,3},{3,1},{5,7},{7,5},{8,10},{10,8},{12,... | collective-permute-start | bytes 393224 | tf_op jit(solution)/shard_map/ppermute | solution.py:408
  38.0 13.6 %collective-permute-start.12 = (bf16[256,256]{1,0:T(8,128)(2,1)S(1)}, bf16[256,256]{1,0:T(8,128)(2,1)S(1)}, u32[]{:S(2)}, u32[]{:S(2)}) collective-permute-start(bf16[256,256]{1,0:T(8,128)(2,1)S(1)} %get-tuple-element.70), channel_id=1, source_target_pairs={{0,4},{2,6},{4,0},{6,2},{1,5},{3,7},{5,1},{7,3},{8,12},{10,14},{12... | collective-permute-start | bytes 393224 | tf_op jit(solution)/shard_map/ppermute | solution.py:408
  38.1 16.3 %collective-permute-start.13 = (bf16[256,256]{1,0:T(8,128)(2,1)S(1)}, bf16[256,256]{1,0:T(8,128)(2,1)S(1)}, u32[]{:S(2)}, u32[]{:S(2)}) collective-permute-start(bf16[256,256]{1,0:T(8,128)(2,1)S(1)} %get-tuple-element.71), channel_id=1, source_target_pairs={{0,6},{2,4},{4,2},{6,0},{1,7},{3,5},{5,3},{7,1},{8,14},{10,12},{12... | collective-permute-start | bytes 393224 | tf_op jit(solution)/shard_map/ppermute | solution.py:408
  40.8 13.6 %collective-permute-start.14 = (bf16[256,256]{1,0:T(8,128)(2,1)S(1)}, bf16[256,256]{1,0:T(8,128)(2,1)S(1)}, u32[]{:S(2)}, u32[]{:S(2)}) collective-permute-start(bf16[256,256]{1,0:T(8,128)(2,1)S(1)} %get-tuple-element.72), channel_id=1, source_target_pairs={{0,2},{2,0},{4,6},{6,4},{1,3},{3,1},{5,7},{7,5},{8,10},{10,8},{12,... | collective-permute-start | bytes 393224 | tf_op jit(solution)/shard_map/ppermute | solution.py:408
  55.9 12.1 %collective-permute-start.20 = (bf16[256,256]{1,0:T(8,128)(2,1)S(1)}, bf16[256,256]{1,0:T(8,128)(2,1)S(1)}, u32[]{:S(2)}, u32[]{:S(2)}) collective-permute-start(bf16[256,256]{1,0:T(8,128)(2,1)S(1)} %get-tuple-element.87), channel_id=1, source_target_pairs={{0,12},{2,14},{4,8},{6,10},{8,20},{10,22},{12,16},{14,18},{16,28},... | collective-permute-start | bytes 393224 | tf_op jit(solution)/shard_map/ppermute | solution.py:405
  57.2 17.9 %collective-permute-start.21 = (bf16[256,256]{1,0:T(8,128)(2,1)S(1)}, bf16[256,256]{1,0:T(8,128)(2,1)S(1)}, u32[]{:S(2)}, u32[]{:S(2)}) collective-permute-start(bf16[256,256]{1,0:T(8,128)(2,1)S(1)} %get-tuple-element.88), channel_id=1, source_target_pairs={{0,14},{2,12},{4,10},{6,8},{8,22},{10,20},{12,18},{14,16},{16,30},... | collective-permute-start | bytes 393224 | tf_op jit(solution)/shard_map/ppermute | solution.py:405
  59.1 15.9 %collective-permute-start.22 = (bf16[256,256]{1,0:T(8,128)(2,1)S(1)}, bf16[256,256]{1,0:T(8,128)(2,1)S(1)}, u32[]{:S(2)}, u32[]{:S(2)}) collective-permute-start(bf16[256,256]{1,0:T(8,128)(2,1)S(1)} %get-tuple-element.89), channel_id=1, source_target_pairs={{0,10},{2,8},{4,14},{6,12},{8,18},{10,16},{12,22},{14,20},{16,26},... | collective-permute-start | bytes 393224 | tf_op jit(solution)/shard_map/ppermute | solution.py:405
  62.3 12.7 %collective-permute-start.23 = (bf16[256,256]{1,0:T(8,128)(2,1)S(1)}, bf16[256,256]{1,0:T(8,128)(2,1)S(1)}, u32[]{:S(2)}, u32[]{:S(2)}) collective-permute-start(bf16[256,256]{1,0:T(8,128)(2,1)S(1)} %get-tuple-element.90), channel_id=1, source_target_pairs={{0,8},{2,10},{4,12},{6,14},{8,16},{10,18},{12,20},{14,22},{16,24},... | collective-permute-start | bytes 393224 | tf_op jit(solution)/shard_map/ppermute | solution.py:405
  63.0 25.6 %collective-permute-start.18 = (bf16[256,256]{1,0:T(8,128)(2,1)S(1)}, bf16[256,256]{1,0:T(8,128)(2,1)S(1)}, u32[]{:S(2)}, u32[]{:S(2)}) collective-permute-start(bf16[256,256]{1,0:T(8,128)(2,1)S(1)} %get-tuple-element.76.refs_0_), channel_id=1, source_target_pairs={{0,8},{2,10},{4,12},{6,14},{8,16},{10,18},{12,20},{14,22},{16,24},... | collective-permute-start | bytes 393224 | tf_op jit(solution)/shard_map/ppermute | solution.py:405
  68.0 9.8 %collective-permute-start.15 = (bf16[256,256]{1,0:T(8,128)(2,1)S(1)}, bf16[256,256]{1,0:T(8,128)(2,1)S(1)}, u32[]{:S(2)}, u32[]{:S(2)}) collective-permute-start(bf16[256,256]{1,0:T(8,128)(2,1)S(1)} %get-tuple-element.79), channel_id=1, source_target_pairs={{0,12},{2,14},{4,8},{6,10},{8,20},{10,22},{12,16},{14,18},{16,28},... | collective-permute-start | bytes 393224 | tf_op jit(solution)/shard_map/ppermute | solution.py:405
  75.0 13.6 %collective-permute-start.16 = (bf16[256,256]{1,0:T(8,128)(2,1)S(1)}, bf16[256,256]{1,0:T(8,128)(2,1)S(1)}, u32[]{:S(2)}, u32[]{:S(2)}) collective-permute-start(bf16[256,256]{1,0:T(8,128)(2,1)S(1)} %get-tuple-element.80), channel_id=1, source_target_pairs={{0,14},{2,12},{4,10},{6,8},{8,22},{10,20},{12,18},{14,16},{16,30},... | collective-permute-start | bytes 393224 | tf_op jit(solution)/shard_map/ppermute | solution.py:405
  75.1 13.6 %collective-permute-start.17 = (bf16[256,256]{1,0:T(8,128)(2,1)S(1)}, bf16[256,256]{1,0:T(8,128)(2,1)S(1)}, u32[]{:S(2)}, u32[]{:S(2)}) collective-permute-start(bf16[256,256]{1,0:T(8,128)(2,1)S(1)} %get-tuple-element.81), channel_id=1, source_target_pairs={{0,10},{2,8},{4,14},{6,12},{8,18},{10,16},{12,22},{14,20},{16,26},... | collective-permute-start | bytes 393224 | tf_op jit(solution)/shard_map/ppermute | solution.py:405
  76.1 16.3 %collective-permute-start.24 = (bf16[256,256]{1,0:T(8,128)(2,1)S(1)}, bf16[256,256]{1,0:T(8,128)(2,1)S(1)}, u32[]{:S(2)}, u32[]{:S(2)}) collective-permute-start(bf16[256,256]{1,0:T(8,128)(2,1)S(1)} %get-tuple-element.91), channel_id=1, source_target_pairs={{0,4},{2,6},{4,0},{6,2},{1,5},{3,7},{5,1},{7,3},{8,12},{10,14},{12... | collective-permute-start | bytes 393224 | tf_op jit(solution)/shard_map/ppermute | solution.py:408
  77.8 15.6 %collective-permute-start.25 = (bf16[256,256]{1,0:T(8,128)(2,1)S(1)}, bf16[256,256]{1,0:T(8,128)(2,1)S(1)}, u32[]{:S(2)}, u32[]{:S(2)}) collective-permute-start(bf16[256,256]{1,0:T(8,128)(2,1)S(1)} %get-tuple-element.92), channel_id=1, source_target_pairs={{0,6},{2,4},{4,2},{6,0},{1,7},{3,5},{5,3},{7,1},{8,14},{10,12},{12... | collective-permute-start | bytes 393224 | tf_op jit(solution)/shard_map/ppermute | solution.py:408
  88.7 11.1 %collective-permute-start.26 = (bf16[256,256]{1,0:T(8,128)(2,1)S(1)}, bf16[256,256]{1,0:T(8,128)(2,1)S(1)}, u32[]{:S(2)}, u32[]{:S(2)}) collective-permute-start(bf16[256,256]{1,0:T(8,128)(2,1)S(1)} %get-tuple-element.93), channel_id=1, source_target_pairs={{0,2},{2,0},{4,6},{6,4},{1,3},{3,1},{5,7},{7,5},{8,10},{10,8},{12,... | collective-permute-start | bytes 393224 | tf_op jit(solution)/shard_map/ppermute | solution.py:408
  89.7 10.9 %collective-permute-start.27 = (bf16[256,256]{1,0:T(8,128)(2,1)S(1)}, bf16[256,256]{1,0:T(8,128)(2,1)S(1)}, u32[]{:S(2)}, u32[]{:S(2)}) collective-permute-start(bf16[256,256]{1,0:T(8,128)(2,1)S(1)} %get-tuple-element.95), channel_id=1, source_target_pairs={{0,4},{2,6},{4,0},{6,2},{1,5},{3,7},{5,1},{7,3},{8,12},{10,14},{12... | collective-permute-start | bytes 393224 | tf_op jit(solution)/shard_map/ppermute | solution.py:408
  89.8 15.0 %collective-permute-start.28 = (bf16[256,256]{1,0:T(8,128)(2,1)S(1)}, bf16[256,256]{1,0:T(8,128)(2,1)S(1)}, u32[]{:S(2)}, u32[]{:S(2)}) collective-permute-start(bf16[256,256]{1,0:T(8,128)(2,1)S(1)} %get-tuple-element.96), channel_id=1, source_target_pairs={{0,6},{2,4},{4,2},{6,0},{1,7},{3,5},{5,3},{7,1},{8,14},{10,12},{12... | collective-permute-start | bytes 393224 | tf_op jit(solution)/shard_map/ppermute | solution.py:408
  92.4 12.4 %collective-permute-start.29 = (bf16[256,256]{1,0:T(8,128)(2,1)S(1)}, bf16[256,256]{1,0:T(8,128)(2,1)S(1)}, u32[]{:S(2)}, u32[]{:S(2)}) collective-permute-start(bf16[256,256]{1,0:T(8,128)(2,1)S(1)} %get-tuple-element.97), channel_id=1, source_target_pairs={{0,2},{2,0},{4,6},{6,4},{1,3},{3,1},{5,7},{7,5},{8,10},{10,8},{12,... | collective-permute-start | bytes 393224 | tf_op jit(solution)/shard_map/ppermute | solution.py:408
  93.4 13.6 %collective-permute-start.19 = (bf16[256,1024]{1,0:T(8,128)(2,1)S(1)}, bf16[256,1024]{1,0:T(8,128)(2,1)S(1)}, u32[]{:S(2)}, u32[]{:S(2)}) collective-permute-start(bf16[256,1024]{1,0:T(8,128)(2,1)S(1)} %other_rows.1), channel_id=1, source_target_pairs={{0,1},{1,0},{2,3},{3,2},{4,5},{5,4},{6,7},{7,6},{8,9},{9,8},{10,11... | collective-permute-start | bytes 1572872 | tf_op jit(solution)/shard_map/ppermute | solution.py:370
  105.2 2.8 %collective-permute-start.30 = (bf16[256,1024]{1,0:T(8,128)(2,1)S(1)}, bf16[256,1024]{1,0:T(8,128)(2,1)S(1)}, u32[]{:S(2)}, u32[]{:S(2)}) collective-permute-start(bf16[256,1024]{1,0:T(8,128)(2,1)S(1)} %half_space.3), channel_id=1, source_target_pairs={{0,1},{1,0},{2,3},{3,2},{4,5},{5,4},{6,7},{7,6},{8,9},{9,8},{10,11... | collective-permute-start | bytes 1572872 | tf_op jit(solution)/shard_map/ppermute | solution.py:370
  (9 other events, 49.5 us)
